TPU v7x, 32 devices: a whole 2x2x4 slice. The times are simulated.
32 devices in a mesh: groups: 2 (over y), pos: 4 (over z), strand: 2 (over core), heads: 2 (over x).
Axes of the slice: x: 2, y: 2, z: 4, core: 2. Of those that a mesh axis runs over, the one named last changes fastest.
Arguments:
- base_codes: int32 [131072], P(('groups', 'pos')), parts along dimension 0, may hold values from 0 to 3
- embed_table: bfloat16 [512, 1536], P(None, 'heads'), may hold values from -0.5 to 0.5
- attn_gain: float32 [1536], replicated, may hold values from 0.1 to 1.9
- w_query: bfloat16 [1536, 1024], P(None, 'heads')
- w_key: bfloat16 [1536, 128], P(None, 'heads')
- w_value: bfloat16 [1536, 192], P(None, 'heads'), may hold values from -0.15625 to 0.15625
- w_out: bfloat16 [1536, 1536], P('heads'), may hold values from -0.15625 to 0.15625
- head_gain: float32 [1536], replicated, may hold values from 0.1 to 1.9
- w_tracks: bfloat16 [1536, 2, 1536], P(None, None, 'heads'), may hold values from -0.15625 to 0.15625
- track_pairs: int32 [3072], P(('strand', 'heads')), may hold values from 0 to 3071, as said below
Outputs:
- tracks_out: float32 [1024, 3072], P(('groups', 'pos'), ('strand', 'heads')), parts along dimension 0
There are 2 independent parts, one for each index of `groups`. A program takes and returns all parts, laid end to end along the dimension named above; an argument that names none is the same for every part. Nothing has to cross between parts.
Inputs may be any that keep to these rules, and one draw needn't show every extreme that they name: track_pairs is an involution: each aligned pair of tracks 2 j and 2 j + 1 is either swapped or left in place.
All inputs are finite; a program needn't handle non-finite values.
Results may differ from a plain program's by a relative error of at most 0.008.
Values may be sent and summed in bfloat16 or wider, within the bound.
No kernel may reach another device: no remote copies, remote signals or barrier semaphores. Data moves between devices by JAX's collectives and lax.ppermute only.
A program may use at most 64 MiB of HBM per device.

v0:
```python
import math

import jax
import jax.numpy as jnp
from jax import lax
from jax.sharding import PartitionSpec as P

KDIM = 128
VDIM = 192
BIN = 128


def from_partner(value, axis, distance):
    mask = 2**distance
    pairs = [(source, source ^ mask) for source in range(lax.axis_size(axis))]
    return lax.ppermute(value, axis, pairs)


def rotate(values, positions):
    row_total = values.shape[0]
    head_total = values.shape[1] // KDIM
    half_dim = KDIM // 2
    inverse = jnp.exp(jnp.arange(half_dim, dtype=jnp.float32) * (-math.log(10000.0) / half_dim))
    angles = positions.astype(jnp.float32)[:, None] * inverse[None, :]
    cosine = jnp.cos(angles)[:, None, :]
    sine_val = jnp.sin(angles)[:, None, :]
    shaped = values.astype(jnp.float32).reshape(row_total, head_total, KDIM)
    low_part = shaped[:, :, :half_dim]
    high_part = shaped[:, :, half_dim:]
    turned = jnp.concatenate(
        [low_part * cosine - high_part * sine_val, high_part * cosine + low_part * sine_val], axis=2
    )
    return turned.reshape(row_total, head_total * KDIM).astype(jnp.bfloat16)


def embed_bases(base_block, lookup):
    onehot = (base_block[:, :, None] == jnp.arange(4, dtype=jnp.int32)[None, None, :]).astype(
        jnp.bfloat16
    )
    onehot = onehot.reshape(base_block.shape[0], base_block.shape[1] * 4)
    return jnp.dot(onehot, lookup, preferred_element_type=jnp.float32).astype(jnp.bfloat16)


def normalize(values, gain_vec):
    floats = values.astype(jnp.float32)
    square = jnp.mean(floats * floats, axis=-1, keepdims=True)
    return (floats * lax.rsqrt(square + 1e-06) * gain_vec).astype(jnp.bfloat16)


def init_state(head_count, row_count):
    return (
        jnp.full((head_count, row_count), -1e30, jnp.float32),
        jnp.zeros((head_count, row_count), jnp.float32),
        jnp.zeros((head_count, row_count, VDIM), jnp.float32),
    )


def absorb(per_head, score_scale, carried, arrived):
    top_score, weight_sum, weighted = carried
    keys_rot, value_cols = arrived
    scores = (
        jnp.einsum("hrk,nk->hrn", per_head, keys_rot, preferred_element_type=jnp.float32)
        * score_scale
    )
    newest = jnp.maximum(top_score, jnp.max(scores, axis=2))
    weights = jnp.exp(scores - newest[:, :, None])
    weight_sum = jnp.sum(weights, axis=2)
    weighted = jnp.einsum(
        "hrn,nv->hrv", weights.astype(jnp.bfloat16), value_cols, preferred_element_type=jnp.float32
    )
    return (newest, weight_sum, weighted)


def body(
    base_codes,
    embed_table,
    attn_gain,
    w_query,
    w_key,
    w_value,
    w_out,
    head_gain,
    w_tracks,
    track_pairs,
):
    row_count = base_codes.shape[0] // BIN
    pos_total = lax.axis_size("pos")
    strand_idx = lax.axis_index("strand")
    pos_idx = lax.axis_index("pos")
    base_block = base_codes.reshape(row_count, BIN)
    flipped = 3 - base_block[::-1, ::-1]
    offsets = jnp.arange(row_count, dtype=jnp.int32)
    chosen = jnp.where(strand_idx == 0, base_block, flipped)
    own_part = embed_bases(chosen, embed_table)
    first_row = jnp.where(strand_idx == 0, pos_idx, pos_total - 1 - pos_idx) * row_count
    positions = first_row + offsets
    inputs = lax.all_gather(own_part, "heads", axis=1, tiled=True)
    normed = normalize(inputs, attn_gain)
    queries = rotate(
        jnp.dot(normed, w_query, preferred_element_type=jnp.float32).astype(jnp.bfloat16), positions
    )
    key_part = jnp.dot(normed, w_key, preferred_element_type=jnp.float32).astype(jnp.bfloat16)
    value_part = jnp.dot(normed, w_value, preferred_element_type=jnp.float32).astype(jnp.bfloat16)
    score_scale = KDIM ** (-0.5)
    local_heads = w_query.shape[1] // KDIM
    key_cols, value_cols = (
        lax.all_gather(key_part, "heads", axis=1, tiled=True),
        lax.all_gather(value_part, "heads", axis=1, tiled=True),
    )
    keys_rot = rotate(key_cols, positions)
    per_head = queries.reshape(row_count, local_heads, KDIM).transpose(1, 0, 2)
    top_score, weight_sum, weighted = absorb(
        per_head,
        score_scale,
        init_state(local_heads, row_count),
        (
            lax.all_gather(keys_rot, "pos", axis=0, tiled=True),
            lax.all_gather(value_cols, "pos", axis=0, tiled=True),
        ),
    )
    own_heads = (weighted / weight_sum[:, :, None]).astype(jnp.bfloat16)
    merged = own_heads.transpose(1, 0, 2).reshape(row_count, local_heads * VDIM)
    share_rows = row_count // lax.axis_size("heads")
    mixed_share = lax.psum_scatter(
        jnp.dot(merged, w_out, preferred_element_type=jnp.float32).astype(jnp.bfloat16),
        "heads",
        scatter_dimension=0,
        tiled=True,
    ).astype(jnp.float32)
    input_share = lax.dynamic_slice_in_dim(
        inputs, lax.axis_index("heads") * share_rows, share_rows, 0
    )
    hidden_share = (input_share.astype(jnp.float32) + mixed_share).astype(jnp.bfloat16)
    normed_out = lax.all_gather(normalize(hidden_share, head_gain), "heads", axis=0, tiled=True)
    logits = jnp.einsum("rd,dsc->rsc", normed_out, w_tracks, preferred_element_type=jnp.float32)
    predicted = jax.nn.softplus(logits).astype(jnp.bfloat16)
    aligned = jnp.where(strand_idx == 0, predicted, predicted[::-1])
    kept_half = lax.dynamic_index_in_dim(aligned, strand_idx, 1, keepdims=False)
    sent_half = lax.dynamic_index_in_dim(aligned, 1 - strand_idx, 1, keepdims=False)
    received = from_partner(sent_half, "strand", 0)
    forward_vals = jnp.where(strand_idx == 0, kept_half, received)
    reverse_vals = jnp.where(strand_idx == 0, received, kept_half)
    local_pairs = track_pairs % forward_vals.shape[1]
    paired = jnp.take(reverse_vals, local_pairs, axis=1)
    return 0.5 * (forward_vals.astype(jnp.float32) + paired.astype(jnp.float32))


def solution(mesh):
    placed = (
        P(("groups", "pos")),
        P(None, "heads"),
        P(),
        P(None, "heads"),
        P(None, "heads"),
        P(None, "heads"),
        P("heads", None),
        P(),
        P(None, None, "heads"),
        P(("strand", "heads")),
    )
    return jax.shard_map(
        body,
        mesh=mesh,
        in_specs=placed,
        out_specs=P(("groups", "pos"), ("strand", "heads")),
        check_vma=False,
    )
```

profile of v0, /device:TPU:0, one launch (start us, length us, event | category | flops | bytes accessed | tf_op | source)
XLA Modules:
  0.0 96.0 jit_solution(1616610870687609975)
XLA Ops:
  6.6 1.1 %rev.6 = s32[128,128]{1,0:T(8,128)S(1)} reverse(s32[128,128]{1,0:T(8,128)} %bitcast.47), dimensions={0,1} | reverse | bytes 131072 | tf_op jit(solution)/shard_map/rev | solution.py:91
  7.6 0.9 subtract_select_fusion
  8.6 0.1 eq.33
  8.8 1.6 %convolution_convert_fusion.1 = bf16[128,768]{1,0:T(8,128)(2,1)S(1)} fusion(bf16[512,768]{1,0:T(8,128)(2,1)} %param.11, s32[128,512]{0,1:T(8,128)S(1)} %bitcast.46, s32[512]{0:T(512)S(1)} %eq.33), kind=kOutput, calls=%fused_computation.8 | convolution fusion | flops 100827136 | bytes 1247232 | tf_op jit(solution)/shard_map/dot_general | solution.py:41
  10.4 8.5 %all_gather.18 = bf16[128,1536]{1,0:T(8,128)(2,1)S(1)} all-gather(bf16[128,768]{1,0:T(8,128)(2,1)S(1)} %convolution_convert_fusion.1), channel_id=1, replica_groups=mesh['groups'=2,'pos'=4,'strand'=2,'heads'=2] {'heads'}, dimensions={1}, use_global_device_ids=true | all-gather | bytes 589824 | tf_op jit(solution)/shard_map/all_gather | solution.py:97
  18.9 0.2 fusion.7
  19.1 0.4 fusion.4
  19.6 0.2 fusion.38
  19.9 1.3 %convolution_convert_fusion.4 = bf16[128,64]{0,1:T(8,128)(2,1)S(1)} fusion(bf16[1536,64]{0,1:T(8,128)(2,1)} %param.14, bf16[128,1536]{1,0:T(8,128)(2,1)S(1)} %all_gather.18, f32[1536]{0:T(1024)S(1)} %copy-done.3, f32[128]{0:T(128)S(1)} %add_rsqrt_fusion.1), kind=kOutput, calls=%fused_computation.13 | convolution fusion | flops 25960448 | bytes 612864 | tf_op jit(solution)/shard_map/dot_general | solution.py:102
  21.2 4.4 %all_gather.19 = bf16[128,128]{0,1:T(8,128)(2,1)S(1)} all-gather(bf16[128,64]{0,1:T(8,128)(2,1)S(1)} %convolution_convert_fusion.4), channel_id=1, replica_groups=mesh['groups'=2,'pos'=4,'strand'=2,'heads'=2] {'heads'}, dimensions={1}, use_global_device_ids=true | all-gather | bytes 49152 | tf_op jit(solution)/shard_map/all_gather | solution.py:107
  25.6 0.3 multiply_cosine_fusion
  25.9 0.2 fusion.31
  26.1 13.0 %all-gather = bf16[512,1,128]{0,2,1:T(8,128)(2,1)S(1)} all-gather(bf16[128,1,128]{0,2,1:T(8,128)(2,1)S(1)} %pad_maximum_fusion), channel_id=2, replica_groups=mesh['groups'=2,'pos'=4,'strand'=2,'heads'=2] {'pos'}, dimensions={0}, use_global_device_ids=true | all-gather | bytes 163840 | tf_op jit(solution)/shard_map/all_gather | solution.py:117
  39.2 0.4 fusion.39
  39.6 0.3 convolution_convert_fusion.3
  40.0 4.5 %all_gather.21 = bf16[128,192]{0,1:T(8,128)(2,1)S(1)} all-gather(bf16[128,96]{0,1:T(8,128)(2,1)S(1)} %convolution_convert_fusion.3), channel_id=1, replica_groups=mesh['groups'=2,'pos'=4,'strand'=2,'heads'=2] {'heads'}, dimensions={1}, use_global_device_ids=true | all-gather | bytes 73728 | tf_op jit(solution)/shard_map/all_gather | solution.py:108
  44.5 12.5 %all_gather.22 = bf16[512,192]{0,1:T(8,128)(2,1)S(1)} all-gather(bf16[128,192]{0,1:T(8,128)(2,1)S(1)} %all_gather.21), channel_id=1, replica_groups=mesh['groups'=2,'pos'=4,'strand'=2,'heads'=2] {'pos'}, dimensions={0}, use_global_device_ids=true | all-gather | bytes 245760 | tf_op jit(solution)/shard_map/all_gather | solution.py:118
  57.0 0.3 fusion.5
  57.3 0.5 fusion.3
  57.8 1.2 %convolution_convert_fusion = bf16[128,1536]{1,0:T(8,128)(2,1)} fusion(bf16[128,768]{0,1:T(8,128)(2,1)S(1)} %bitcast.48, bf16[768,1536]{1,0:T(8,128)(2,1)S(1)} %copy-done), kind=kOutput, calls=%fused_computation.3 | convolution fusion | flops 302186496 | bytes 2949120 | tf_op jit(solution)/shard_map/dot_general | solution.py:125
  59.2 11.7 %reduce-scatter.2.cloned.1.call-done = bf16[64,1536]{1,0:T(8,128)(2,1)} async-done(((bf16[128,1536]{1,0:T(8,128)(2,1)}), bf16[64,1536]{1,0:T(8,128)(2,1)}) %reduce-scatter.2.cloned.1.call-update) | async-done | bytes 196624 | tf_op jit(solution)/shard_map/reduce_scatter | solution.py:124
  70.9 1.1 %fusion.15 = f32[64]{0:T(128)S(1)} fusion(bf16[64,1536]{1,0:T(8,128)(2,1)} %reduce-scatter.2.cloned.1.call-done, bf16[128,1536]{1,0:T(8,128)(2,1)S(1)} %all_gather.18, s32[]{:T(128)S(6)} %select_n.65), kind=kLoop, calls=%fused_computation.26 | loop fusion | flops 688064 | bytes 393476 | tf_op jit(solution)/shard_map/reduce_sum | solution.py:46
  72.0 1.0 %fusion.17 = bf16[64,1536]{1,0:T(8,128)(2,1)S(1)} fusion(f32[1536]{0:T(1024)S(1)} %copy-done.4, f32[64]{0:T(128)S(1)} %add_rsqrt_fusion, bf16[64,1536]{1,0:T(8,128)(2,1)} %reduce-scatter.2.cloned.1.call-done, bf16[128,1536]{1,0:T(8,128)(2,1)S(1)} %all_gather.18, s32[]{:T(128)S(6)} %select_n.65), kind=kLoop, calls=%fused_computation.28 | loop fusion | flops 786432 | bytes 596228 | tf_op jit(solution)/shard_map/convert_element_type | solution.py:47
  73.0 7.3 %all_gather.23 = bf16[128,1536]{1,0:T(8,128)(2,1)S(1)} all-gather(bf16[64,1536]{1,0:T(8,128)(2,1)S(1)} %fusion.17), channel_id=1, replica_groups=mesh['groups'=2,'pos'=4,'strand'=2,'heads'=2] {'heads'}, dimensions={0}, use_global_device_ids=true | all-gather | bytes 589824 | tf_op jit(solution)/shard_map/all_gather | solution.py:134
  80.4 3.6 %fusion.10 = bf16[128,2,768]{2,0,1:T(8,128)(2,1)S(1)} fusion(bf16[1536,2,768]{2,1,0:T(2,128)(2,1)} %param.18, bf16[128,1536]{1,0:T(8,128)(2,1)S(1)} %all_gather.23), kind=kOutput, calls=%fused_computation.22 | convolution fusion | flops 605356032 | bytes 5505024 | tf_op jit(solution)/shard_map/rd,dsc->rsc/dot_general | solution.py:135
  83.9 0.5 rev.7
  84.5 0.2 copy.29
  84.8 0.2 copy.30
  84.9 1.2 %collective-permute-done = bf16[128,768]{0,1:T(8,128)(2,1)S(1)} collective-permute-done((bf16[128,768]{0,1:T(8,128)(2,1)S(1)}, bf16[128,768]{0,1:T(8,128)(2,1)S(1)}, u32[]{:S(2)}, u32[]{:S(2)}) %collective-permute-start) | collective-permute-done | bytes 196640 | tf_op jit(solution)/shard_map/ppermute | solution.py:16
  86.2 1.9 %gather_fusion = bf16[768,128]{1,0:T(8,128)(2,1)S(1)} fusion(bf16[128,768]{0,1:T(8,128)(2,1)S(1)} %broadcast_select_fusion.1, s32[1024]{0:T(1024)S(1)} %pad_clamp_fusion), kind=kCustom, calls=%fused_computation | custom fusion | bytes 396288 | tf_op jit(solution)/shard_map/jit(_take)/gather | solution.py:144
  88.1 0.2 fusion.18
  88.3 0.9 copy.32
  (33 shorter events, 0.6 us)
Async XLA Ops:
  6.5 51.3 %copy-start = (bf16[768,1536]{1,0:T(8,128)(2,1)S(1)}, bf16[768,1536]{1,0:T(8,128)(2,1)}, u32[]{:S(2)}) copy-start(bf16[768,1536]{1,0:T(8,128)(2,1)} %param.16) | copy-start | bytes 7077892
  6.5 12.5 %copy-start.3 = (f32[1536]{0:T(1024)S(1)}, f32[1536]{0:T(1024)}, u32[]{:S(2)}) copy-start(f32[1536]{0:T(1024)} %param.12) | copy-start | bytes 18436
  6.5 64.3 %reduce-scatter.2.cloned.1.call-start = ((), (), s32[]{:S(2)}) async-start(), calls=%async_computation.1 | async-start | bytes 589824 | tf_op jit(solution)/shard_map/reduce_scatter | solution.py:124
  8.7 10.4 %copy-start.1 = (bf16[1536,512]{1,0:T(8,128)(2,1)S(1)}, bf16[1536,512]{1,0:T(8,128)(2,1)}, u32[]{:S(2)}) copy-start(bf16[1536,512]{1,0:T(8,128)(2,1)} %param.13) | copy-start | bytes 4718596
  19.8 19.8 %copy-start.5 = (bf16[1536,96]{0,1:T(8,128)(2,1)S(1)}, bf16[1536,96]{0,1:T(8,128)(2,1)}, u32[]{:S(2)}) copy-start(bf16[1536,96]{0,1:T(8,128)(2,1)} %param.15) | copy-start | bytes 884740
  57.3 1.8 %copy-start.2 = (s32[768]{0:T(1024)S(1)}, s32[768]{0:T(1024)}, u32[]{:S(2)}) copy-start(s32[768]{0:T(1024)} %param.19) | copy-start | bytes 9220
  57.8 14.2 %copy-start.4 = (f32[1536]{0:T(1024)S(1)}, f32[1536]{0:T(1024)}, u32[]{:S(2)}) copy-start(f32[1536]{0:T(1024)} %param.17) | copy-start | bytes 18436
  84.7 1.5 %collective-permute-start = (bf16[128,768]{0,1:T(8,128)(2,1)S(1)}, bf16[128,768]{0,1:T(8,128)(2,1)S(1)}, u32[]{:S(2)}, u32[]{:S(2)}) collective-permute-start(bf16[128,768]{0,1:T(8,128)(2,1)S(1)} %copy.29), channel_id=1, source_target_pairs={{0,2},{2,0},{1,3},{3,1},{4,6},{6,4},{5,7},{7,5},{8,10},{10,8},{9,1... | collective-permute-start | bytes 589832 | tf_op jit(solution)/shard_map/ppermute | solution.py:16
Sparse Core Ops, SparseCore 0:
  59.2 11.5 reduce-scatter.1
where the time goes:
time: 96.4 us; the launch traced here: 96 us
  blocking collectives  50.2 us (52%)
  between operations  13.7 us (14%)
  waiting for transfers between devices  13 us (13%)
  matrix products  9.4 us (10%)
  local copies, waits for them, and re-layouts  5.26 us (5%)
  other arithmetic  4.38 us (5%)
    all_gather x1, blocking collectives, body(): lax.all_gather(keys_rot, 'pos', axis=0, tiled=True)  13 us
    all_gather x1, blocking collectives, body(): lax.all_gather(value_cols, 'pos', axis=0, tiled=True)  12.5 us
    reduce_scatter x1, waiting for transfers between devices, body(): lax.psum_scatter(jnp.dot(merged, w_out, preferred_element_type=jnp.float3...  11.7 us
    all_gather x1, blocking collectives, body(): inputs = lax.all_gather(own_part, 'heads', axis=1, tiled=True)  8.5 us
    all_gather x1, blocking collectives, body(): lax.all_gather(normalize(hidden_share, head_gain), 'heads', axis=0, tiled...  7.31 us
    all_gather x1, blocking collectives, body(): lax.all_gather(value_part, 'heads', axis=1, tiled=True)  4.5 us
    all_gather x1, blocking collectives, body(): lax.all_gather(key_part, 'heads', axis=1, tiled=True)  4.42 us
    dot_general x1, matrix products, body(): jnp.einsum('rd,dsc->rsc', normed_out, w_tracks, preferred_element_type=jn...  3.56 us
  transfers between devices with their start and end apart: 2, of which 2 were waited for; matrix products, arithmetic and copies ran while one was open for 0% of the time, Pallas kernels for 0%

commit v1 on v0

v1 whole, which is shorter than its diff:
```python
import math

import jax
import jax.numpy as jnp
from jax import lax
from jax.sharding import PartitionSpec as P

KDIM = 128
VDIM = 192
BIN = 128
BASES = 4
F32 = jnp.float32
BF16 = jnp.bfloat16


def shifted(value, axis, distance):
    size = lax.axis_size(axis)
    return lax.ppermute(value, axis, [(i, (i + distance) % size) for i in range(size)])


def matmul(a, b):
    return jnp.dot(a, b, preferred_element_type=F32)


def share_over_strand(value, axis, strand_idx):
    size = lax.axis_size(axis)
    half = value.shape[0] // 2
    own_half = lax.dynamic_slice_in_dim(value, strand_idx * half, half, 0)
    parts = [value]
    for step in range(1, size):
        mine = shifted(own_half, axis, step)
        theirs = shifted(mine, "strand", 1)
        low = jnp.where(strand_idx == 0, mine, theirs)
        high = jnp.where(strand_idx == 0, theirs, mine)
        parts.append(jnp.concatenate([low, high], axis=0))
    return parts


def in_order(parts, axis):
    size = lax.axis_size(axis)
    if size == 2:
        own = lax.axis_index(axis) == 0
        return jnp.stack([jnp.where(own, parts[0], parts[1]), jnp.where(own, parts[1], parts[0])])
    stacked = jnp.stack(parts)
    return jnp.take(stacked, (lax.axis_index(axis) - jnp.arange(size)) % size, axis=0)


def rotate(values, cosine, sine):
    half = KDIM // 2
    heads = values.shape[1] // KDIM
    shaped = values.astype(BF16).astype(F32).reshape(values.shape[0], heads, KDIM)
    low, high = shaped[:, :, :half], shaped[:, :, half:]
    cosine, sine = cosine[:, None, :], sine[:, None, :]
    turned = jnp.concatenate([low * cosine - high * sine, high * cosine + low * sine], axis=2)
    return turned.astype(BF16)


def body(
    base_codes,
    embed_table,
    attn_gain,
    w_query,
    w_key,
    w_value,
    w_out,
    head_gain,
    w_tracks,
    track_pairs,
):
    rows = base_codes.shape[0] // BIN
    pos_total = lax.axis_size("pos")
    head_total = lax.axis_size("heads")
    strand_idx = lax.axis_index("strand")
    pos_idx = lax.axis_index("pos")
    features = w_query.shape[0]
    key_cols = w_key.shape[1]

    kv_parts = share_over_strand(
        jnp.concatenate([w_key.T, w_value.T], axis=0), "heads", strand_idx
    )
    embed_parts = share_over_strand(embed_table, "heads", strand_idx)
    own_codes = base_codes.reshape(rows, BIN).astype(BF16)
    code_blocks = [own_codes] + [shifted(own_codes, "pos", k) for k in range(1, pos_total)]
    codes = jnp.concatenate(code_blocks, axis=0)

    column = jnp.arange(BIN * BASES, dtype=jnp.int32)
    column = jnp.where(strand_idx == 0, column, BIN * BASES - 1 - column)
    spread = (jnp.arange(BIN, dtype=jnp.int32)[:, None] == column[None, :] // BASES).astype(BF16)
    onehot = (matmul(codes, spread) == (column % BASES).astype(F32)[None, :]).astype(BF16)

    block_idx = (pos_idx - jnp.arange(pos_total, dtype=jnp.int32)) % pos_total
    places = (block_idx[:, None] * rows + jnp.arange(rows, dtype=jnp.int32)[None, :]).reshape(-1)
    places = jnp.where(strand_idx == 0, places, pos_total * rows - 1 - places)
    half = KDIM // 2
    inverse = jnp.exp(jnp.arange(half, dtype=F32) * (-math.log(10000.0) / half))
    angles = places.astype(F32)[:, None] * inverse[None, :]
    cosine, sine = jnp.cos(angles), jnp.sin(angles)

    embed = in_order(embed_parts, "heads")
    inputs = jnp.concatenate(
        [matmul(onehot, embed[i]).astype(BF16) for i in range(head_total)], axis=1
    )
    floats = inputs.astype(F32)
    square = jnp.mean(floats * floats, axis=1, keepdims=True)
    normed = (floats * lax.rsqrt(square + 1e-06) * attn_gain).astype(BF16)
    kv_rows = in_order(kv_parts, "heads")
    key_rows = kv_rows[:, :key_cols].reshape(KDIM, features)
    value_rows = kv_rows[:, key_cols:].reshape(VDIM, features)
    contract = (((1,), (1,)), ((), ()))
    keys = lax.dot_general(normed, key_rows, contract, preferred_element_type=F32)
    keys = rotate(keys, cosine, sine)[:, 0]
    values = lax.dot_general(normed, value_rows, contract, preferred_element_type=F32).astype(BF16)
    queries = rotate(matmul(normed[:rows], w_query), cosine[:rows], sine[:rows])
    own_heads = []
    for head in range(queries.shape[1]):
        scores = lax.dot_general(
            queries[:, head], keys, contract, preferred_element_type=F32
        ) * KDIM ** (-0.5)
        weights = jnp.exp(scores - jnp.max(scores, axis=1, keepdims=True))
        total = jnp.sum(weights, axis=1, keepdims=True)
        own_heads.append((matmul(weights.astype(BF16), values) / total).astype(BF16))
    merged = jnp.concatenate(own_heads, axis=1)

    chunks = 2
    width = features // chunks
    shares = [
        matmul(merged, w_out[:, c * width : (c + 1) * width]).astype(BF16) for c in range(chunks)
    ]
    gained = []
    square = jnp.zeros((rows, 1), F32)
    for c in range(chunks):
        total = shares[c].astype(F32)
        for step in range(1, head_total):
            total = total + shifted(shares[c], "heads", step).astype(F32)
        hidden = inputs[:rows, c * width : (c + 1) * width].astype(F32) + total
        hidden = hidden.astype(BF16).astype(F32)
        square = square + jnp.sum(hidden * hidden, axis=1, keepdims=True)
        gained.append((hidden * head_gain[c * width : (c + 1) * width]).astype(BF16))
    scale = lax.rsqrt(square / features + 1e-06)
    tracks = w_tracks.transpose(1, 0, 2)

    def predict(which):
        weight = lax.dynamic_index_in_dim(tracks, which, 0, keepdims=False)
        logits = sum(
            matmul(gained[c], weight[c * width : (c + 1) * width]) for c in range(chunks)
        )
        return jax.nn.softplus(logits * scale).astype(BF16)

    received = shifted(predict(1 - strand_idx), "strand", 1)
    kept = predict(strand_idx)
    forward = jnp.where(strand_idx == 0, kept, received).astype(F32)
    reverse = jnp.where(strand_idx == 0, received, kept).astype(F32)
    index = jnp.arange(track_pairs.shape[0], dtype=jnp.int32)
    swapped = (track_pairs - index) % track_pairs.shape[0] != 0
    after = jnp.roll(reverse, -1, axis=1)
    before = jnp.roll(reverse, 1, axis=1)
    partner = jnp.where(index % 2 == 0, after, before)
    return 0.5 * (forward + jnp.where(swapped, partner, reverse))


def solution(mesh):
    placed = (
        P(("groups", "pos")),
        P(None, "heads"),
        P(),
        P(None, "heads"),
        P(None, "heads"),
        P(None, "heads"),
        P("heads", None),
        P(),
        P(None, None, "heads"),
        P(("strand", "heads")),
    )
    return jax.shard_map(
        body,
        mesh=mesh,
        in_specs=placed,
        out_specs=P(("groups", "pos"), ("strand", "heads")),
        check_vma=False,
    )
```

time: 96.4 us -> 64.5 us (0.67)
  blocking collectives: 50.2 us -> 0 us
  local copies, waits for them, and re-layouts: 5.26 us -> 26 us
  between operations: 13.7 us -> 0.37 us
  starting transfers between devices: 0.07 us -> 11.1 us
  other arithmetic: 4.38 us -> 9.77 us
  waiting for transfers between devices: 13 us -> 8.05 us
    all_gather x6 -> x0, blocking collectives: 50.2 us -> none  [the longest x1 13 us: body(): lax.all_gather(keys_rot, 'pos', axis=0, tiled=True)]
    another operation x0 -> x1, local copies, waits for them, and re-layouts: none -> 12.4 us
    reduce_scatter x1 -> x0, waiting for transfers between devices: 11.7 us -> none  [body(): lax.psum_scatter(jnp.dot(merged, w_out, preferred_element_type=jnp.float3...]
    ppermute x1 -> x10, starting transfers between devices: 0.07 us -> 11.1 us  [shifted(): lax.ppermute(value, axis, [(i, (i + distance) % size) for i in range(size)])]
    unnamed x12 -> x28, local copies, waits for them, and re-layouts: 0.03 us -> 10.2 us
    ppermute x1 -> x10, waiting for transfers between devices: 1.24 us -> 8.05 us  [shifted(): lax.ppermute(value, axis, [(i, (i + distance) % size) for i in range(size)])]
    gather x1 -> x0, local copies, waits for them, and re-layouts: 1.88 us -> none  [body(): paired = jnp.take(reverse_vals, local_pairs, axis=1)]
    reduce_sum x3 -> x7, other arithmetic: 1.58 us -> 3.35 us  [the longest x2 2.22 us: body(): square = square + jnp.sum(hidden * hidden, axis=1, keepdims=True)]
  transfers between devices with their start and end apart: 2 -> 10, of which waited for: 2 -> 3; matrix products, arithmetic and copies ran while one was open for 0% -> 42% of each run, Pallas kernels for 0% -> 0%
where the time goes in v1:
time: 64.5 us; the launch traced here: 64 us
  local copies, waits for them, and re-layouts  26 us (40%)
  starting transfers between devices  11.1 us (17%)
  other arithmetic  9.77 us (15%)
  matrix products  8.69 us (13%)
  waiting for transfers between devices  8.05 us (12%)
    another operation x1, local copies, waits for them, and re-layouts  12.4 us
    ppermute x10, starting transfers between devices, shifted(): lax.ppermute(value, axis, [(i, (i + distance) % size) for i in range(size)])  11.1 us
    unnamed x28, local copies, waits for them, and re-layouts  10.2 us
    ppermute x10, waiting for transfers between devices, shifted(): lax.ppermute(value, axis, [(i, (i + distance) % size) for i in range(size)])  8.05 us
    dot_general x14, matrix products, matmul(): return jnp.dot(a, b, preferred_element_type=F32)  6.11 us
    reduce_sum x2, other arithmetic, body(): square = square + jnp.sum(hidden * hidden, axis=1, keepdims=True)  2.22 us
  transfers between devices with their start and end apart: 10, of which 3 were waited for; matrix products, arithmetic and copies ran while one was open for 42% of the time, Pallas kernels for 0%

profile of v1, /device:TPU:0, one launch (start us, length us, event | category | flops | bytes accessed | tf_op | source)
XLA Modules:
  0.0 64.0 jit_solution(3204780221214830137)
XLA Ops:
  0.0 1.0 %convert_bitcast_fusion = bf16[128,128]{1,0:T(8,128)(2,1)S(1)} fusion(s32[16384]{0:T(1024)} %param.10), kind=kLoop, calls=%fused_computation.142 | loop fusion | flops 16384 | bytes 98304 | tf_op jit(solution)/shard_map/convert_element_type | solution.py:82
  1.0 5.0 %collective-permute-start.2 = (bf16[128,128]{1,0:T(8,128)(2,1)S(1)}, bf16[128,128]{1,0:T(8,128)(2,1)S(1)}, u32[]{:S(2)}, u32[]{:S(2)}) collective-permute-start(bf16[128,128]{1,0:T(8,128)(2,1)S(1)} %convert_bitcast_fusion), channel_id=1, source_target_pairs={{0,12},{4,0},{8,4},{12,8},{1,13},{5,1},{9,5},{13,9},{2,14},{6,2},{... | collective-permute-start | bytes 98312 | tf_op jit(solution)/shard_map/ppermute | solution.py:18
  6.0 1.0 %collective-permute-start = (bf16[128,128]{1,0:T(8,128)(2,1)S(1)}, bf16[128,128]{1,0:T(8,128)(2,1)S(1)}, u32[]{:S(2)}, u32[]{:S(2)}) collective-permute-start(bf16[128,128]{1,0:T(8,128)(2,1)S(1)} %convert_bitcast_fusion), channel_id=1, source_target_pairs={{0,4},{4,8},{8,12},{12,0},{1,5},{5,9},{9,13},{13,1},{2,6},{6,10},{... | collective-permute-start | bytes 98312 | tf_op jit(solution)/shard_map/ppermute | solution.py:18
  7.0 1.0 %constant_dynamic-slice_fusion.2 = bf16[256,768]{1,0:T(8,128)(2,1)S(1)} fusion(bf16[512,768]{1,0:T(8,128)(2,1)} %param.11, s32[]{:T(128)S(6)} %select_n.172), kind=kLoop, calls=%fused_computation.170 | loop fusion | bytes 786436 | tf_op jit(solution)/shard_map/dynamic_slice | solution.py:28
  8.1 1.6 %collective-permute-start.3 = (bf16[256,768]{1,0:T(8,128)(2,1)S(1)}, bf16[256,768]{1,0:T(8,128)(2,1)S(1)}, u32[]{:S(2)}, u32[]{:S(2)}) collective-permute-start(bf16[256,768]{1,0:T(8,128)(2,1)S(1)} %constant_dynamic-slice_fusion.2), channel_id=1, source_target_pairs={{0,1},{1,0},{2,3},{3,2},{4,5},{5,4},{6,7},{7,6},{8,9},{9,8},{10,11... | collective-permute-start | bytes 1179656 | tf_op jit(solution)/shard_map/ppermute | solution.py:18
  9.6 1.0 %fusion.38 = bf16[80,1536]{1,0:T(8,128)(2,1)S(1)} fusion(s32[]{:T(128)S(6)} %select_n.181, bf16[64,1536]{1,0:T(8,128)(2,1)} %bitcast.87, bf16[96,1536]{1,0:T(8,128)(2,1)} %bitcast.85), kind=kLoop, calls=%fused_computation.86 | loop fusion | flops 491520 | bytes 737284 | tf_op jit(solution)/shard_map/concatenate | solution.py:79
  10.6 0.6 collective-permute-start.5
  11.5 0.9 %slice_cosine_fusion = (f32[128,64]{1,0:T(8,128)}, f32[128,64]{1,0:T(8,128)}) fusion(f32[512,64]{1,0:T(8,128)S(1)} %broadcast_multiply_fusion), kind=kLoop, calls=%fused_computation.132 | loop fusion | bytes 98304 | tf_op jit(solution)/shard_map/cos | solution.py:97
  12.4 12.4 %constant_dynamic-slice_fusion.1 = (bf16[1536,1,768]{2,1,0:T(2,128)(2,1)}, bf16[1536,1,768]{2,1,0:T(2,128)(2,1)}) fusion(bf16[1536,2,768]{2,1,0:T(2,128)(2,1)} %param.18, s32[]{:T(128)S(6)} %select_n.186, s32[]{:T(128)S(6)} %select_n.188), kind=kLoop, calls=%fused_computation.169 | loop fusion | bytes 9437192 | tf_op jit(solution)/shard_map/dynamic-slice
  24.9 4.1 %copy.25 = bf16[1536,1,768]{2,0,1:T(8,128)(2,1)} copy(bf16[1536,1,768]{2,1,0:T(2,128)(2,1)} %get-tuple-element.10) | data formatting | bytes 4718592
  29.0 4.2 %copy.26 = bf16[1536,1,768]{2,0,1:T(8,128)(2,1)} copy(bf16[1536,1,768]{2,1,0:T(2,128)(2,1)} %get-tuple-element.9) | data formatting | bytes 4718592
  33.5 0.6 collective-permute-start.4
  34.4 0.9 %pad_maximum_fusion.2 = bf16[2,96,1536]{2,1,0:T(8,128)(2,1)} fusion(bf16[1,160,1536]{2,1,0:T(8,128)(2,1)S(1)} %get-tuple-element.12, bf16[1,160,1536]{2,1,0:T(8,128)(2,1)S(1)} %get-tuple-element.11), kind=kLoop, calls=%fused_computation.52 | loop fusion | flops 1179648 | bytes 1572864 | tf_op jit(solution)/shard_map/stack | solution.py:43
  35.7 0.6 convolution_convert_fusion
  36.4 0.6 convolution_convert_fusion.1
  37.7 0.4 fusion.2
  38.2 0.6 %fusion.19 = f32[512,1,128]{0,2,1:T(8,128)S(1)} fusion(bf16[512,1536]{1,0:T(8,128)(2,1)S(1)} %fusion.2, bf16[128,1536]{1,0:T(8,128)(2,1)S(1)} %bitcast.84), kind=kOutput, calls=%fused_computation.38 | convolution fusion | flops 201457664 | bytes 2228224 | tf_op jit(solution)/shard_map/dot_general | solution.py:110
  38.8 0.6 fusion.76
  39.4 1.1 %fusion.17 = f32[128,512]{1,0:T(8,128)} fusion(bf16[1536,512]{1,0:T(8,128)(2,1)S(1)} %copy-done, bf16[512,1536]{1,0:T(8,128)(2,1)S(1)} %fusion.2), kind=kOutput, calls=%fused_computation.36 | convolution fusion | flops 201457664 | bytes 2228224 | tf_op jit(solution)/shard_map/dot_general | solution.py:22
  40.5 1.0 %reshape.361 = f32[128,4,128]{2,1,0:T(4,128)S(1)} reshape(f32[128,512]{1,0:T(8,128)} %fusion.17) | data formatting | bytes 524288 | tf_op jit(solution)/shard_map/reshape | solution.py:51
  41.7 1.0 %subtract_convert_fusion = (bf16[128,4,64]{2,0,1:T(8,128)(2,1)S(1)}, bf16[128,4,64]{2,0,1:T(8,128)(2,1)S(1)}) fusion(f32[128,4,64]{2,1,0:T(4,128)S(1)} %get-tuple-element.28, f32[128,4,64]{2,1,0:T(4,128)S(1)} %get-tuple-element.27, f32[128,64]{1,0:T(8,128)} %get-tuple-element.26, f32[128,64]{1,0:T(8,128)} %get-tuple-element.25), kind=kLoop, calls=%fused_computation.84 | loop fusion | flops 262144 | bytes 458752 | tf_op jit(solution)/shard_map/convert.6
  44.0 0.7 %convolution_convert_fusion.2 = bf16[512,192]{0,1:T(8,128)(2,1)S(1)} fusion(bf16[512,1536]{1,0:T(8,128)(2,1)S(1)} %fusion.2, bf16[192,1536]{1,0:T(8,128)(2,1)S(1)} %bitcast.89), kind=kOutput, calls=%fused_computation.27 | convolution fusion | flops 302088192 | bytes 2359296 | tf_op jit(solution)/shard_map/dot_general | solution.py:112
  47.2 1.5 %collective-permute-start.7 = (bf16[128,768]{1,0:T(8,128)(2,1)S(1)}, bf16[128,768]{1,0:T(8,128)(2,1)S(1)}, u32[]{:S(2)}, u32[]{:S(2)}) collective-permute-start(bf16[128,768]{1,0:T(8,128)(2,1)S(1)} %fusion.11), channel_id=1, source_target_pairs={{0,1},{1,0},{2,3},{3,2},{4,5},{5,4},{6,7},{7,6},{8,9},{9,8},{10,11... | collective-permute-start | bytes 589832 | tf_op jit(solution)/shard_map/ppermute | solution.py:18
  49.1 0.6 collective-permute-start.8
  49.7 5.2 %collective-permute-done.7 = bf16[128,768]{1,0:T(8,128)(2,1)S(1)} collective-permute-done((bf16[128,768]{1,0:T(8,128)(2,1)S(1)}, bf16[128,768]{1,0:T(8,128)(2,1)S(1)}, u32[]{:S(2)}, u32[]{:S(2)}) %collective-permute-start.7) | collective-permute-done | bytes 196640 | tf_op jit(solution)/shard_map/ppermute | solution.py:18
  55.0 1.1 %fusion.29 = (f32[128]{0:T(128)S(1)}, bf16[128,768]{1,0:T(8,128)(2,1)S(1)}) fusion(bf16[128,768]{1,0:T(8,128)(2,1)S(1)} %collective-permute-done.7, bf16[128,768]{1,0:T(8,128)(2,1)S(1)} %fusion.11, bf16[512,768]{1,0:T(8,128)(2,1)} %copy-done.2), kind=kLoop, calls=%fused_computation.64 | loop fusion | flops 884608 | bytes 786944 | tf_op jit(solution)/shard_map/reduce_sum | solution.py:137
  56.1 2.7 %collective-permute-done.8 = bf16[128,768]{1,0:T(8,128)(2,1)S(1)} collective-permute-done((bf16[128,768]{1,0:T(8,128)(2,1)S(1)}, bf16[128,768]{1,0:T(8,128)(2,1)S(1)}, u32[]{:S(2)}, u32[]{:S(2)}) %collective-permute-start.8) | collective-permute-done | bytes 196640 | tf_op jit(solution)/shard_map/ppermute | solution.py:18
  58.8 1.1 %fusion.31 = (f32[128]{0:T(128)S(1)}, bf16[128,768]{1,0:T(8,128)(2,1)S(1)}) fusion(bf16[128,768]{1,0:T(8,128)(2,1)S(1)} %collective-permute-done.8, bf16[128,768]{1,0:T(8,128)(2,1)S(1)} %fusion.14, bf16[512,768]{1,0:T(8,128)(2,1)} %copy-done.1), kind=kLoop, calls=%fused_computation.66 | loop fusion | flops 884608 | bytes 786944 | tf_op jit(solution)/shard_map/reduce_sum | solution.py:137
  60.3 0.5 fusion.33
  60.8 1.1 %copy-done.3 = bf16[1536,1,768]{2,0,1:T(8,128)(2,1)S(1)} copy-done((bf16[1536,1,768]{2,0,1:T(8,128)(2,1)S(1)}, bf16[1536,1,768]{2,0,1:T(8,128)(2,1)}, u32[]{:S(2)}) %copy-start.3) | copy-done | bytes 2359320
  62.3 0.5 select_convert_fusion
  63.0 0.9 %fusion.37 = f32[128,768]{1,0:T(8,128)} fusion(f32[128,1]{1,0:T(8,128)S(1)} %get-tuple-element.20, f32[128,767]{1,0:T(8,128)S(1)} %get-tuple-element.22, f32[128,767]{1,0:T(8,128)S(1)} %get-tuple-element.21, f32[128,1]{1,0:T(8,128)S(1)} %get-tuple-element.19, bf16[128,768]{1,0:T(8,128)(2,1)S(1)} %get-tuple-element.40, ...), kind=kLoop, calls=%fused_computation.74 | loop fusion | flops 983040 | bytes 1574401 | tf_op jit(solution)/shard_map/mul | solution.py:158
  (70 shorter events, 7.4 us)
Async XLA Ops:
  0.0 39.4 %copy-start = (bf16[1536,512]{1,0:T(8,128)(2,1)S(1)}, bf16[1536,512]{1,0:T(8,128)(2,1)}, u32[]{:S(2)}) copy-start(bf16[1536,512]{1,0:T(8,128)(2,1)} %param.13) | copy-start | bytes 4718596
  1.0 32.2 %collective-permute-start.2 = (bf16[128,128]{1,0:T(8,128)(2,1)S(1)}, bf16[128,128]{1,0:T(8,128)(2,1)S(1)}, u32[]{:S(2)}, u32[]{:S(2)}) collective-permute-start(bf16[128,128]{1,0:T(8,128)(2,1)S(1)} %convert_bitcast_fusion), channel_id=1, source_target_pairs={{0,12},{4,0},{8,4},{12,8},{1,13},{5,1},{9,5},{13,9},{2,14},{6,2},{... | collective-permute-start | bytes 98312 | tf_op jit(solution)/shard_map/ppermute | solution.py:18
  6.0 27.1 %collective-permute-start.1 = (bf16[128,128]{1,0:T(8,128)(2,1)S(1)}, bf16[128,128]{1,0:T(8,128)(2,1)S(1)}, u32[]{:S(2)}, u32[]{:S(2)}) collective-permute-start(bf16[128,128]{1,0:T(8,128)(2,1)S(1)} %convert_bitcast_fusion), channel_id=1, source_target_pairs={{0,8},{4,12},{8,0},{12,4},{1,9},{5,13},{9,1},{13,5},{2,10},{6,14},... | collective-permute-start | bytes 98312 | tf_op jit(solution)/shard_map/ppermute | solution.py:18
  6.0 27.1 %collective-permute-start = (bf16[128,128]{1,0:T(8,128)(2,1)S(1)}, bf16[128,128]{1,0:T(8,128)(2,1)S(1)}, u32[]{:S(2)}, u32[]{:S(2)}) collective-permute-start(bf16[128,128]{1,0:T(8,128)(2,1)S(1)} %convert_bitcast_fusion), channel_id=1, source_target_pairs={{0,4},{4,8},{8,12},{12,0},{1,5},{5,9},{9,13},{13,1},{2,6},{6,10},{... | collective-permute-start | bytes 98312 | tf_op jit(solution)/shard_map/ppermute | solution.py:18
  8.1 25.5 %collective-permute-start.3 = (bf16[256,768]{1,0:T(8,128)(2,1)S(1)}, bf16[256,768]{1,0:T(8,128)(2,1)S(1)}, u32[]{:S(2)}, u32[]{:S(2)}) collective-permute-start(bf16[256,768]{1,0:T(8,128)(2,1)S(1)} %constant_dynamic-slice_fusion.2), channel_id=1, source_target_pairs={{0,1},{1,0},{2,3},{3,2},{4,5},{5,4},{6,7},{7,6},{8,9},{9,8},{10,11... | collective-permute-start | bytes 1179656 | tf_op jit(solution)/shard_map/ppermute | solution.py:18
  10.6 14.2 %collective-permute-start.5 = (bf16[80,1536]{1,0:T(8,128)(2,1)S(1)}, bf16[80,1536]{1,0:T(8,128)(2,1)S(1)}, u32[]{:S(2)}, u32[]{:S(2)}) collective-permute-start(bf16[80,1536]{1,0:T(8,128)(2,1)S(1)} %fusion.38), channel_id=1, source_target_pairs={{0,1},{1,0},{2,3},{3,2},{4,5},{5,4},{6,7},{7,6},{8,9},{9,8},{10,11... | collective-permute-start | bytes 737288 | tf_op jit(solution)/shard_map/ppermute | solution.py:18
  12.4 12.4 %copy-start.10 = (f32[1536]{0:T(1024)S(1)}, f32[1536]{0:T(1024)}, u32[]{:S(2)}) copy-start(f32[1536]{0:T(1024)} %param.17) | copy-start | bytes 18436
  12.4 12.4 %copy-start.11 = (s32[768]{0:T(1024)S(1)}, s32[768]{0:T(1024)}, u32[]{:S(2)}) copy-start(s32[768]{0:T(1024)} %param.19) | copy-start | bytes 9220
  24.8 9.3 %collective-permute-start.6 = (bf16[80,1536]{1,0:T(8,128)(2,1)S(1)}, bf16[80,1536]{1,0:T(8,128)(2,1)S(1)}, u32[]{:S(2)}, u32[]{:S(2)}) collective-permute-start(bf16[80,1536]{1,0:T(8,128)(2,1)S(1)} %collective-permute-done.5), channel_id=1, source_target_pairs={{0,2},{2,0},{1,3},{3,1},{4,6},{6,4},{5,7},{7,5},{8,10},{10,8},{9,1... | collective-permute-start | bytes 737288 | tf_op jit(solution)/shard_map/ppermute | solution.py:18
  33.2 1.0 %copy-start.5 = (bf16[1536,96]{0,1:T(8,128)(2,1)S(1)}, bf16[1536,96]{0,1:T(8,128)(2,1)}, u32[]{:S(2)}) copy-start(bf16[1536,96]{0,1:T(8,128)(2,1)} %param.15) | copy-start | bytes 884740
  33.2 1.0 %copy-start.6 = (bf16[1536,64]{0,1:T(8,128)(2,1)S(1)}, bf16[1536,64]{0,1:T(8,128)(2,1)}, u32[]{:S(2)}) copy-start(bf16[1536,64]{0,1:T(8,128)(2,1)} %param.14) | copy-start | bytes 589828
  33.5 1.9 %collective-permute-start.4 = (bf16[256,768]{1,0:T(8,128)(2,1)S(1)}, bf16[256,768]{1,0:T(8,128)(2,1)S(1)}, u32[]{:S(2)}, u32[]{:S(2)}) collective-permute-start(bf16[256,768]{1,0:T(8,128)(2,1)S(1)} %collective-permute-done.3), channel_id=1, source_target_pairs={{0,2},{2,0},{1,3},{3,1},{4,6},{6,4},{5,7},{7,5},{8,10},{10,8},{9,1... | collective-permute-start | bytes 1179656 | tf_op jit(solution)/shard_map/ppermute | solution.py:18
  34.4 1.3 %copy-start.8 = (bf16[512,768]{1,0:T(8,128)(2,1)S(1)}, bf16[512,768]{1,0:T(8,128)(2,1)}, u32[]{:S(2)}) copy-start(bf16[512,768]{1,0:T(8,128)(2,1)} %param.11) | copy-start | bytes 2359300
  36.4 1.1 %copy-start.1 = (bf16[512,768]{1,0:T(8,128)(2,1)}, bf16[512,768]{1,0:T(8,128)(2,1)S(1)}, u32[]{:S(2)}) copy-start(bf16[512,768]{1,0:T(8,128)(2,1)S(1)} %convolution_convert_fusion) | copy-start | bytes 2359300
  37.0 1.2 %copy-start.2 = (bf16[512,768]{1,0:T(8,128)(2,1)}, bf16[512,768]{1,0:T(8,128)(2,1)S(1)}, u32[]{:S(2)}) copy-start(bf16[512,768]{1,0:T(8,128)(2,1)S(1)} %convolution_convert_fusion.1) | copy-start | bytes 2359300
  37.0 0.7 %copy-start.9 = (f32[1536]{0:T(1024)S(1)}, f32[1536]{0:T(1024)}, u32[]{:S(2)}) copy-start(f32[1536]{0:T(1024)} %param.12) | copy-start | bytes 18436
  41.7 2.3 %copy-start.7 = (bf16[2,96,1536]{2,1,0:T(8,128)(2,1)S(1)}, bf16[2,96,1536]{2,1,0:T(8,128)(2,1)}, u32[]{:S(2)}) copy-start(bf16[2,96,1536]{2,1,0:T(8,128)(2,1)} %pad_maximum_fusion.2) | copy-start | bytes 1769476
  45.2 1.7 %copy-start.12 = (bf16[768,1536]{1,0:T(8,128)(2,1)S(1)}, bf16[768,1536]{1,0:T(8,128)(2,1)}, u32[]{:S(2)}) copy-start(bf16[768,1536]{1,0:T(8,128)(2,1)} %param.16) | copy-start | bytes 7077892
  47.2 12.7 %copy-start.4 = (bf16[1536,1,768]{2,0,1:T(8,128)(2,1)S(1)}, bf16[1536,1,768]{2,0,1:T(8,128)(2,1)}, u32[]{:S(2)}) copy-start(bf16[1536,1,768]{2,0,1:T(8,128)(2,1)} %copy.25) | copy-start | bytes 7077892
  47.2 7.8 %collective-permute-start.7 = (bf16[128,768]{1,0:T(8,128)(2,1)S(1)}, bf16[128,768]{1,0:T(8,128)(2,1)S(1)}, u32[]{:S(2)}, u32[]{:S(2)}) collective-permute-start(bf16[128,768]{1,0:T(8,128)(2,1)S(1)} %fusion.11), channel_id=1, source_target_pairs={{0,1},{1,0},{2,3},{3,2},{4,5},{5,4},{6,7},{7,6},{8,9},{9,8},{10,11... | collective-permute-start | bytes 589832 | tf_op jit(solution)/shard_map/ppermute | solution.py:18
  49.1 9.7 %collective-permute-start.8 = (bf16[128,768]{1,0:T(8,128)(2,1)S(1)}, bf16[128,768]{1,0:T(8,128)(2,1)S(1)}, u32[]{:S(2)}, u32[]{:S(2)}) collective-permute-start(bf16[128,768]{1,0:T(8,128)(2,1)S(1)} %fusion.14), channel_id=1, source_target_pairs={{0,1},{1,0},{2,3},{3,2},{4,5},{5,4},{6,7},{7,6},{8,9},{9,8},{10,11... | collective-permute-start | bytes 589832 | tf_op jit(solution)/shard_map/ppermute | solution.py:18
  60.3 1.7 %copy-start.3 = (bf16[1536,1,768]{2,0,1:T(8,128)(2,1)S(1)}, bf16[1536,1,768]{2,0,1:T(8,128)(2,1)}, u32[]{:S(2)}) copy-start(bf16[1536,1,768]{2,0,1:T(8,128)(2,1)} %copy.26) | copy-start | bytes 7077892
  60.7 1.5 %collective-permute-start.9 = (bf16[128,768]{1,0:T(8,128)(2,1)S(1)}, bf16[128,768]{1,0:T(8,128)(2,1)S(1)}, u32[]{:S(2)}, u32[]{:S(2)}) collective-permute-start(bf16[128,768]{1,0:T(8,128)(2,1)S(1)} %fusion.33), channel_id=1, source_target_pairs={{0,2},{2,0},{1,3},{3,1},{4,6},{6,4},{5,7},{7,5},{8,10},{10,8},{9,1... | collective-permute-start | bytes 589832 | tf_op jit(solution)/shard_map/ppermute | solution.py:18

commit v2 on v1

v2 whole, which is shorter than its diff:
```python
import functools
import math

import jax
import jax.experimental.pallas as pl
import jax.experimental.pallas.tpu as pltpu
import jax.numpy as jnp
from jax import lax
from jax.sharding import PartitionSpec as P

KDIM = 128
VDIM = 192
BIN = 128
BASES = 4
LANES = 128
VMEM_LIMIT = 48 * 2**20
F32 = jnp.float32
BF16 = jnp.bfloat16


def shifted(value, axis, distance):
    size = lax.axis_size(axis)
    return lax.ppermute(value, axis, [(i, (i + distance) % size) for i in range(size)])


def matmul(a, b):
    return jnp.dot(a, b, preferred_element_type=F32)


def matmul_t(a, b):
    return lax.dot_general(a, b, (((1,), (1,)), ((), ())), preferred_element_type=F32)


def call(kernel, outs, operands, name, scratch=(), spaces=None, flops=0):
    vmem = pl.BlockSpec(memory_space=pltpu.VMEM)
    specs = [vmem if space is None else pl.BlockSpec(memory_space=space) for space in (spaces or [None] * len(operands))]
    moved = sum(math.prod(v.shape) * v.dtype.itemsize for v in list(operands) + list(outs))
    return pl.pallas_call(
        kernel,
        out_shape=list(outs),
        in_specs=specs,
        out_specs=[vmem] * len(outs),
        scratch_shapes=list(scratch),
        compiler_params=pltpu.CompilerParams(vmem_limit_bytes=VMEM_LIMIT),
        cost_estimate=pl.CostEstimate(flops=flops, bytes_accessed=moved, transcendentals=0),
        name=name,
    )(*operands)


def shape(dims, dtype):
    return jax.ShapeDtypeStruct(tuple(dims), dtype)


def over_blocks(total, block, step):
    if total == block:
        step(0)
    else:

        def one(i, carry):
            step(pl.multiple_of(i * block, block))
            return carry

        lax.fori_loop(0, total // block, one, 0)


def stage_kernel(embed, key_t, value_t, codes, half_kv, first, second, codes_out, sems):
    strand = lax.axis_index("strand")
    key_cols, value_cols = key_t.shape[0], value_t.shape[0]
    width = half_kv.shape[1]
    quarter = first.shape[0]
    cols = pl.ds(pl.multiple_of(strand * width, LANES), width)
    row = pl.multiple_of(strand * (2 * quarter), quarter)
    copies = [
        pltpu.make_async_copy(key_t.at[:, cols], half_kv.at[pl.ds(0, key_cols)], sems.at[0]),
        pltpu.make_async_copy(value_t.at[:, cols], half_kv.at[pl.ds(key_cols, value_cols)], sems.at[1]),
        pltpu.make_async_copy(embed.at[pl.ds(row, quarter)], first, sems.at[2]),
        pltpu.make_async_copy(embed.at[pl.ds(row + quarter, quarter)], second, sems.at[3]),
    ]
    for copy in copies:
        copy.start()
    codes_out[...] = codes[...].astype(F32).astype(BF16)
    for copy in copies:
        copy.wait()


def own_kernel(blocks, others, *refs):
    codes = refs[:blocks]
    embed, key_t, value_t = refs[blocks : blocks + 3]
    halves = refs[blocks + 3 : blocks + 3 + 2 * others]
    w_query, gain, onehot, kv_t, own, square, kv_sum, q_sum, table, all_codes = refs[blocks + 3 + 2 * others :]
    strand, mine = lax.axis_index("strand"), lax.axis_index("heads")
    size = others + 1
    key_cols, value_cols = key_t.shape[0], value_t.shape[0]
    features, width = w_query.shape[0], embed.shape[1]
    entries = embed.shape[0]
    quarter = entries // 4
    rows = codes[0].shape[0]
    total = blocks * rows
    for i in range(blocks):
        all_codes[i * rows : (i + 1) * rows, :] = codes[i][...]
    for i in range(4):
        part = strand if i % 2 == 0 else 1 - strand
        start = pl.multiple_of(part * (2 * quarter) + (i // 2) * quarter, quarter)
        table[i * quarter : (i + 1) * quarter, :] = embed[pl.ds(start, quarter), :]
    for step in range(size):
        owner = lax.rem(mine + size - step, size)
        key_rows = pl.ds(pl.multiple_of(owner * key_cols, 16), key_cols)
        value_rows = pl.ds(pl.multiple_of(KDIM + owner * value_cols, 16), value_cols)
        if step == 0:
            kv_t[key_rows, :] = key_t[...]
            kv_t[value_rows, :] = value_t[...]
        else:
            for k in range(2):
                piece = halves[2 * (step - 1) + k]
                part = strand if k == 0 else 1 - strand
                cols = pl.ds(pl.multiple_of(part * (features // 2), LANES), features // 2)
                kv_t[key_rows, cols] = piece[:key_cols, :]
                kv_t[value_rows, cols] = piece[key_cols:, :]
    spot = lax.broadcasted_iota(jnp.int32, (BIN, entries), 1)
    piece = spot // quarter
    half = jnp.where(piece % 2 == 0, strand, 1 - strand)
    entry = half * (2 * quarter) + (piece // 2) * quarter + spot % quarter
    entry = jnp.where(strand == 0, entry, entries - 1 - entry)
    place = lax.broadcasted_iota(jnp.int32, (BIN, entries), 0)
    spread = jnp.where(place == entry // BASES, 1.0, 0.0).astype(BF16)
    wanted = (entry[:1] % BASES).astype(F32)
    mine_cols = pl.ds(pl.multiple_of(mine * width, LANES), width)
    mine_gain = gain[:, mine_cols]

    def step(start):
        here = pl.ds(start, min(total, 4 * rows))
        hot = jnp.where(matmul(all_codes[here, :], spread) == wanted, 1.0, 0.0).astype(BF16)
        onehot[here, :] = hot
        values = matmul(hot, table[...]).astype(BF16)
        floats = values.astype(F32)
        square[here, :] = jnp.sum(floats * floats, axis=1, keepdims=True)
        gained = (floats * mine_gain).astype(BF16)
        kv_sum[here, :] = matmul_t(gained, kv_t[:, mine_cols])
        return values, gained

    if total <= 4 * rows:
        values, gained = step(0)
        own[...] = values[:rows]
        gained = gained[:rows]
    else:
        over_blocks(total, 4 * rows, lambda start: step(start) and None)
        values = matmul(onehot[:rows, :], table[...]).astype(BF16)
        own[...] = values
        gained = (values.astype(F32) * mine_gain).astype(BF16)
    q_sum[...] = matmul(gained, w_query[pl.ds(pl.multiple_of(mine * width, LANES), width), :])


def turn(values, cosine, sine):
    floats = values.astype(BF16).astype(F32)
    return (floats * cosine + pltpu.roll(floats, KDIM // 2, 1) * sine).astype(BF16)


def attend_kernel(others, *refs):
    pieces = refs[: 4 * others]
    (onehot, kv_t, own, square, kv_sum, q_sum, w_query, gain, cosine, sine, w_out) = refs[4 * others : 4 * others + 11]
    share, merged, inputs, table, squares, sums, keys, values = refs[4 * others + 11 :]
    mine = lax.axis_index("heads")
    size = others + 1
    rows, width = own.shape
    quarter = pieces[0].shape[0]
    total = onehot.shape[0]
    features = size * width
    block = min(total, 4 * rows)
    inputs[:, pl.ds(pl.multiple_of(mine * width, LANES), width)] = own[...]
    queries = q_sum[...]
    over_blocks(total, block, lambda start: squares.__setitem__((pl.ds(start, block), slice(None)), square[pl.ds(start, block), :]))
    for step in range(1, size):
        owner = lax.rem(mine + size - step, size)
        cols = pl.ds(pl.multiple_of(owner * width, LANES), width)
        for i in range(4):
            table[i * quarter : (i + 1) * quarter, :] = pieces[4 * (step - 1) + i][...]
        last = step == size - 1

        def add(start):
            here = pl.ds(start, block)
            found = matmul(onehot[here, :], table[...]).astype(BF16)
            floats = found.astype(F32)
            squares[here, :] = squares[here, :] + jnp.sum(floats * floats, axis=1, keepdims=True)
            gained = (floats * gain[:, cols]).astype(BF16)
            before = kv_sum[here, :] if step == 1 else sums[here, :]
            sums[here, :] = before + matmul_t(gained, kv_t[:, cols])
            return found, gained

        if total == block:
            found, gained = add(0)
            found, gained = found[:rows], gained[:rows]
        else:
            over_blocks(total, block, lambda start: add(start) and None)
            found = matmul(onehot[:rows, :], table[...]).astype(BF16)
            gained = (found.astype(F32) * gain[:, cols]).astype(BF16)
        inputs[:, cols] = found
        queries = queries + matmul(gained, w_query[cols, :])

    def finish(start):
        here = pl.ds(start, block)
        scale = lax.rsqrt(squares[here, :] / features + 1e-06)
        scaled = (sums[here, :] if others else kv_sum[here, :]) * scale
        keys[here, :] = turn(scaled[:, :KDIM], cosine[here, :], sine[here, :])
        values[here, :] = scaled[:, KDIM:].astype(BF16)

    over_blocks(total, block, finish)
    queries = queries * lax.rsqrt(squares[:rows, :] / features + 1e-06)
    result = None
    half = w_out.shape[1] // 2
    for head in range(queries.shape[1] // KDIM):
        query = turn(queries[:, head * KDIM : (head + 1) * KDIM], cosine[:rows, :], sine[:rows, :])
        scores = matmul_t(query, keys[...]) * KDIM ** (-0.5)
        weights = jnp.exp(scores - jnp.max(scores, axis=1, keepdims=True))
        weight_sum = jnp.sum(weights, axis=1, keepdims=True)
        found = (matmul(weights.astype(BF16), values[...]) / weight_sum).astype(BF16)
        merged[:, head * VDIM : (head + 1) * VDIM] = found
    share[...] = matmul(merged[...], w_out[:, :half]).astype(BF16)


def second_kernel(merged, w_out, share):
    half = w_out.shape[1] // 2
    share[...] = matmul(merged[...], w_out[:, half:]).astype(BF16)


def gather_hidden(shares, inputs, gain, chunk):
    width = shares[0].shape[1]
    cols = slice(chunk * width, (chunk + 1) * width)
    total = shares[0][...].astype(F32)
    for other in shares[1:]:
        total = total + other[...].astype(F32)
    hidden = (inputs[:, cols].astype(F32) + total).astype(BF16).astype(F32)
    return jnp.sum(hidden * hidden, axis=1, keepdims=True), (hidden * gain[:, cols]).astype(BF16)


def soft(logits):
    return jnp.maximum(logits, 0.0) + jnp.log1p(jnp.exp(-jnp.abs(logits)))


def first_tracks_kernel(size, *refs):
    shares = refs[:size]
    inputs, gain, tracks, square, to_send, to_keep = refs[size:]
    strand = lax.axis_index("strand")
    width = shares[0].shape[1]
    square[...], gained = gather_hidden(shares, inputs, gain, 0)
    to_send[...] = matmul(gained, tracks[1 - strand, :width, :])
    to_keep[...] = matmul(gained, tracks[strand, :width, :])


def send_kernel(size, *refs):
    shares = refs[:size]
    inputs, gain, tracks, square, to_send, sent, gained_out, scale_out = refs[size:]
    strand = lax.axis_index("strand")
    width = shares[0].shape[1]
    total, gained = gather_hidden(shares, inputs, gain, 1)
    scale = lax.rsqrt((square[...] + total) / (2 * width) + 1e-06)
    logits = to_send[...] + matmul(gained, tracks[1 - strand, width:, :])
    sent[...] = soft(logits * scale).astype(BF16)
    gained_out[...] = gained
    scale_out[...] = scale


def keep_kernel(gained, tracks, to_keep, scale, kept):
    strand = lax.axis_index("strand")
    width = gained.shape[1]
    logits = to_keep[...] + matmul(gained[...], tracks[strand, width:, :])
    kept[...] = soft(logits * scale[...]).astype(BF16)


def average_kernel(kept, received, pairs, out):
    strand = lax.axis_index("strand")
    count = kept.shape[1]
    mine, theirs = kept[...].astype(F32), received[...].astype(F32)
    forward = jnp.where(strand == 0, mine, theirs)
    reverse = jnp.where(strand == 0, theirs, mine)
    index = lax.broadcasted_iota(jnp.int32, (1, count), 1)
    even = index % 2 == 0
    swapped = (pairs[...] % 2 == 0) != even
    partner = jnp.where(even, pltpu.roll(reverse, count - 1, 1), pltpu.roll(reverse, 1, 1))
    out[...] = 0.5 * (forward + jnp.where(swapped, partner, reverse))


def body(
    base_codes,
    embed_table,
    attn_gain,
    w_query,
    w_key,
    w_value,
    w_out,
    head_gain,
    w_tracks,
    track_pairs,
):
    rows = base_codes.shape[0] // BIN
    blocks = lax.axis_size("pos")
    size = lax.axis_size("heads")
    strand = lax.axis_index("strand")
    pos = lax.axis_index("pos")
    features, q_cols = w_query.shape
    entries, width = embed_table.shape
    key_t, value_t = w_key.T, w_value.T
    kv_cols = key_t.shape[0] + value_t.shape[0]
    kv_all = KDIM + VDIM
    quarter = entries // 4
    total = blocks * rows
    tracks_half = w_tracks.shape[2]

    half_kv, first, second, own_codes = call(
        stage_kernel,
        [
            shape((kv_cols, features // 2), BF16),
            shape((quarter, width), BF16),
            shape((quarter, width), BF16),
            shape((rows, BIN), BF16),
        ],
        [embed_table, key_t, value_t, base_codes.reshape(rows, BIN)],
        "stage",
        scratch=[pltpu.SemaphoreType.DMA((4,))],
        spaces=[pl.ANY, pl.ANY, pl.ANY, None],
    )
    halves, pieces = [], []
    for step in range(1, size):
        here = [shifted(v, "heads", step) for v in (half_kv, first, second)]
        there = [shifted(v, "strand", 1) for v in here]
        halves += [here[0], there[0]]
        pieces += [here[1], there[1], here[2], there[2]]
    codes = [own_codes] + [shifted(own_codes, "pos", k) for k in range(1, blocks)]

    block_idx = (pos - jnp.arange(blocks, dtype=jnp.int32)) % blocks
    places = (block_idx[:, None] * rows + jnp.arange(rows, dtype=jnp.int32)[None, :]).reshape(-1)
    places = jnp.where(strand == 0, places, total - 1 - places)
    lane = jnp.arange(KDIM, dtype=jnp.int32)
    half = KDIM // 2
    inverse = jnp.exp((lane % half).astype(F32) * (-math.log(10000.0) / half))
    angles = places.astype(F32)[:, None] * inverse[None, :]
    cosine = jnp.cos(angles)
    sine = jnp.sin(angles) * jnp.where(lane < half, -1.0, 1.0)

    gain = attn_gain.reshape(1, features)
    onehot, kv_t, own, square, kv_sum, q_sum = call(
        functools.partial(own_kernel, blocks, size - 1),
        [
            shape((total, entries), BF16),
            shape((kv_all, features), BF16),
            shape((rows, width), BF16),
            shape((total, 1), F32),
            shape((total, kv_all), F32),
            shape((rows, q_cols), F32),
        ],
        codes + [embed_table, key_t, value_t] + halves + [w_query, gain],
        "own_features",
        scratch=[pltpu.VMEM((entries, width), BF16), pltpu.VMEM((total, BIN), BF16)],
        flops=2 * total * width * (entries + kv_all),
    )
    o_cols = q_cols // KDIM * VDIM
    share_one, merged, inputs = call(
        functools.partial(attend_kernel, size - 1),
        [
            shape((rows, features // 2), BF16),
            shape((rows, o_cols), BF16),
            shape((rows, features), BF16),
        ],
        pieces + [onehot, kv_t, own, square, kv_sum, q_sum, w_query, gain, cosine, sine, w_out],
        "attend",
        scratch=[
            pltpu.VMEM((entries, width), BF16),
            pltpu.VMEM((total, 1), F32),
            pltpu.VMEM((total, kv_all), F32),
            pltpu.VMEM((total, KDIM), BF16),
            pltpu.VMEM((total, VDIM), BF16),
        ],
        flops=2 * total * width * (entries + kv_all) * 2,
    )
    (share_two,) = call(
        second_kernel,
        [shape((rows, features // 2), BF16)],
        [merged, w_out],
        "second_share",
        flops=rows * o_cols * features,
    )
    ones = [share_one] + [shifted(share_one, "heads", k) for k in range(1, size)]
    twos = [share_two] + [shifted(share_two, "heads", k) for k in range(1, size)]
    weights, _ = lax.optimization_barrier((w_tracks, share_two))
    tracks = lax.optimization_barrier(weights.transpose(1, 0, 2))
    gain = head_gain.reshape(1, features)
    square, to_send, to_keep = call(
        functools.partial(first_tracks_kernel, size),
        [
            shape((rows, 1), F32),
            shape((rows, tracks_half), F32),
            shape((rows, tracks_half), F32),
        ],
        ones + [inputs, gain, tracks],
        "first_tracks",
        flops=2 * rows * features * tracks_half,
    )
    sent, gained, scale = call(
        functools.partial(send_kernel, size),
        [
            shape((rows, tracks_half), BF16),
            shape((rows, features // 2), BF16),
            shape((rows, 1), F32),
        ],
        twos + [inputs, gain, tracks, square, to_send],
        "sent_tracks",
        flops=rows * features * tracks_half,
    )
    received = shifted(sent, "strand", 1)
    (kept,) = call(
        keep_kernel,
        [shape((rows, tracks_half), BF16)],
        [gained, tracks, to_keep, scale],
        "kept_tracks",
        flops=rows * features * tracks_half,
    )
    (out,) = call(
        average_kernel,
        [shape((rows, tracks_half), F32)],
        [kept, received, track_pairs.reshape(1, tracks_half)],
        "average",
    )
    return out


def solution(mesh):
    placed = (
        P(("groups", "pos")),
        P(None, "heads"),
        P(),
        P(None, "heads"),
        P(None, "heads"),
        P(None, "heads"),
        P("heads", None),
        P(),
        P(None, None, "heads"),
        P(("strand", "heads")),
    )
    return jax.shard_map(
        body,
        mesh=mesh,
        in_specs=placed,
        out_specs=P(("groups", "pos"), ("strand", "heads")),
        check_vma=False,
    )
```

time: 64.5 us -> 55.3 us (0.86)
  Pallas kernels: 0 us -> 15.6 us
  local copies, waits for them, and re-layouts: 26 us -> 10.4 us
  matrix products: 8.69 us -> 0 us
  other arithmetic: 9.77 us -> 1.08 us
  waiting for transfers between devices: 8.05 us -> 14.8 us
  starting transfers between devices: 11.1 us -> 12.8 us
    pallas_call x0 -> x8, Pallas kernels: none -> 15.6 us  [call(): pl.pallas_call(kernel, out_shape=list(outs), in_specs=specs, out_specs=[v...]
    another operation x1 -> x0, local copies, waits for them, and re-layouts: 12.4 us -> none
    dot_general x20 -> x0, matrix products: 8.69 us -> none  [the longest x14 6.11 us: matmul(): return jnp.dot(a, b, preferred_element_type=F32)]
    ppermute x10 -> x12, waiting for transfers between devices: 8.05 us -> 14.8 us  [shifted(): lax.ppermute(value, axis, [(i, (i + distance) % size) for i in range(size)])]
    reduce_sum x7 -> x0, other arithmetic: 3.35 us -> none  [the longest x2 2.22 us: body(): square = square + jnp.sum(hidden * hidden, axis=1, keepdims=True)]
    unnamed x28 -> x26, local copies, waits for them, and re-layouts: 10.2 us -> 6.91 us
    optimization_barrier x0 -> x1, local copies, waits for them, and re-layouts: none -> 2.75 us  [body(): weights, _ = lax.optimization_barrier((w_tracks, share_two))]
    another operation x2 -> x0, other arithmetic: 1.96 us -> none
  transfers between devices with their start and end apart: 10 -> 12, of which waited for: 3 -> 6; matrix products, arithmetic and copies ran while one was open for 42% -> 8% of each run, Pallas kernels for 0% -> 12%
where the time goes in v2:
time: 55.3 us; the launch traced here: 54.8 us
  Pallas kernels  15.6 us (28%)
  waiting for transfers between devices  14.8 us (27%)
  starting transfers between devices  12.8 us (23%)
  local copies, waits for them, and re-layouts  10.4 us (19%)
  other arithmetic  1.08 us (2%)
    pallas_call x8, Pallas kernels, call(): pl.pallas_call(kernel, out_shape=list(outs), in_specs=specs, out_specs=[v...  15.6 us
    ppermute x12, waiting for transfers between devices, shifted(): lax.ppermute(value, axis, [(i, (i + distance) % size) for i in range(size)])  14.8 us
    ppermute x12, starting transfers between devices, shifted(): lax.ppermute(value, axis, [(i, (i + distance) % size) for i in range(size)])  12.8 us
    unnamed x26, local copies, waits for them, and re-layouts  6.91 us
    optimization_barrier x1, local copies, waits for them, and re-layouts, body(): weights, _ = lax.optimization_barrier((w_tracks, share_two))  2.75 us
  transfers between devices with their start and end apart: 12, of which 6 were waited for; matrix products, arithmetic and copies ran while one was open for 8% of the time, Pallas kernels for 12%

profile of v2, /device:TPU:0, one launch (start us, length us, event | category | flops | bytes accessed | tf_op | source)
XLA Modules:
  0.0 54.8 jit_solution(14730095425076232500)
XLA Ops:
  0.0 1.1 %copy-done.2 = bf16[512,768]{1,0:T(8,128)(2,1)S(1)} copy-done((bf16[512,768]{1,0:T(8,128)(2,1)S(1)}, bf16[512,768]{1,0:T(8,128)(2,1)}, u32[]{:S(2)}) %copy-start.2) | copy-done | bytes 786456
  1.1 1.0 %copy-done.4 = bf16[1536,96]{0,1:T(8,128)(2,1)S(1)} copy-done((bf16[1536,96]{0,1:T(8,128)(2,1)S(1)}, bf16[1536,96]{0,1:T(8,128)(2,1)}, u32[]{:S(2)}) %copy-start.4) | copy-done | bytes 294936
  2.1 0.9 %copy-done.6 = bf16[1536,64]{0,1:T(8,128)(2,1)S(1)} copy-done((bf16[1536,64]{0,1:T(8,128)(2,1)S(1)}, bf16[1536,64]{0,1:T(8,128)(2,1)}, u32[]{:S(2)}) %copy-start.6) | copy-done | bytes 196632
  3.0 0.8 %copy-done.8 = s32[16384]{0:T(1024)S(1)} copy-done((s32[16384]{0:T(1024)S(1)}, s32[16384]{0:T(1024)}, u32[]{:S(2)}) %copy-start.8) | copy-done | bytes 65560
  3.9 0.6 %stage.1 = (bf16[160,768]{1,0:T(8,128)(2,1)S(1)}, bf16[128,768]{1,0:T(8,128)(2,1)S(1)}, bf16[128,768]{1,0:T(8,128)(2,1)S(1)}, bf16[128,128]{1,0:T(8,128)(2,1)S(1)}) custom-call(bf16[512,768]{1,0:T(8,128)(2,1)S(1)} %copy-done.2, bf16[64,1536]{1,0:T(8,128)(2,1)S(1)} %bitcast.13, bf16[96,1536]{1,0:T(8,128)(2,1)S(1)} %bitcast.11, s32[128,128]{1,0:T(8,128)S(1)} %bitcast.15), custom_call_target="tpu_custom_call" | custom-call | bytes 2015232 | tf_op jit(solution)/shard_map/stage/pallas_call | solution.py:38
  4.4 3.1 %collective-permute-start.4 = (bf16[128,128]{1,0:T(8,128)(2,1)S(1)}, bf16[128,128]{1,0:T(8,128)(2,1)S(1)}, u32[]{:S(2)}, u32[]{:S(2)}) collective-permute-start(bf16[128,128]{1,0:T(8,128)(2,1)S(1)} %get-tuple-element.27.refs_0_), channel_id=1, source_target_pairs={{0,4},{4,8},{8,12},{12,0},{1,5},{5,9},{9,13},{13,1},{2,6},{6,10},{... | collective-permute-start | bytes 98312 | tf_op jit(solution)/shard_map/ppermute | solution.py:23
  7.5 2.6 %collective-permute-start.5 = (bf16[128,128]{1,0:T(8,128)(2,1)S(1)}, bf16[128,128]{1,0:T(8,128)(2,1)S(1)}, u32[]{:S(2)}, u32[]{:S(2)}) collective-permute-start(bf16[128,128]{1,0:T(8,128)(2,1)S(1)} %get-tuple-element.27.refs_0_), channel_id=1, source_target_pairs={{0,8},{4,12},{8,0},{12,4},{1,9},{5,13},{9,1},{13,5},{2,10},{6,14},... | collective-permute-start | bytes 98312 | tf_op jit(solution)/shard_map/ppermute | solution.py:23
  10.1 1.5 %collective-permute-start.7 = (bf16[160,768]{1,0:T(8,128)(2,1)S(1)}, bf16[160,768]{1,0:T(8,128)(2,1)S(1)}, u32[]{:S(2)}, u32[]{:S(2)}) collective-permute-start(bf16[160,768]{1,0:T(8,128)(2,1)S(1)} %get-tuple-element.28), channel_id=1, source_target_pairs={{0,1},{1,0},{2,3},{3,2},{4,5},{5,4},{6,7},{7,6},{8,9},{9,8},{10,11... | collective-permute-start | bytes 737288 | tf_op jit(solution)/shard_map/ppermute | solution.py:23
  11.6 0.5 collective-permute-start
  12.1 1.5 %collective-permute-start.2 = (bf16[128,768]{1,0:T(8,128)(2,1)S(1)}, bf16[128,768]{1,0:T(8,128)(2,1)S(1)}, u32[]{:S(2)}, u32[]{:S(2)}) collective-permute-start(bf16[128,768]{1,0:T(8,128)(2,1)S(1)} %get-tuple-element.26), channel_id=1, source_target_pairs={{0,1},{1,0},{2,3},{3,2},{4,5},{5,4},{6,7},{7,6},{8,9},{9,8},{10,11... | collective-permute-start | bytes 589832 | tf_op jit(solution)/shard_map/ppermute | solution.py:23
  13.7 5.3 %collective-permute-done.7.refs_7_ = bf16[160,768]{1,0:T(8,128)(2,1)S(1)} collective-permute-done((bf16[160,768]{1,0:T(8,128)(2,1)S(1)}, bf16[160,768]{1,0:T(8,128)(2,1)S(1)}, u32[]{:S(2)}, u32[]{:S(2)}) %collective-permute-start.7) | collective-permute-done | bytes 245792 | tf_op jit(solution)/shard_map/ppermute | solution.py:23
  19.0 1.4 %collective-permute-start.6 = (bf16[128,128]{1,0:T(8,128)(2,1)S(1)}, bf16[128,128]{1,0:T(8,128)(2,1)S(1)}, u32[]{:S(2)}, u32[]{:S(2)}) collective-permute-start(bf16[128,128]{1,0:T(8,128)(2,1)S(1)} %get-tuple-element.27.refs_0_), channel_id=1, source_target_pairs={{0,12},{4,0},{8,4},{12,8},{1,13},{5,1},{9,5},{13,9},{2,14},{6,2},{... | collective-permute-start | bytes 98312 | tf_op jit(solution)/shard_map/ppermute | solution.py:23
  20.4 2.8 %collective-permute-done.refs_0_ = bf16[128,768]{1,0:T(8,128)(2,1)S(1)} collective-permute-done((bf16[128,768]{1,0:T(8,128)(2,1)S(1)}, bf16[128,768]{1,0:T(8,128)(2,1)S(1)}, u32[]{:S(2)}, u32[]{:S(2)}) %collective-permute-start) | collective-permute-done | bytes 196640 | tf_op jit(solution)/shard_map/ppermute | solution.py:23
  23.2 2.4 %collective-permute-done.2.refs_2_ = bf16[128,768]{1,0:T(8,128)(2,1)S(1)} collective-permute-done((bf16[128,768]{1,0:T(8,128)(2,1)S(1)}, bf16[128,768]{1,0:T(8,128)(2,1)S(1)}, u32[]{:S(2)}, u32[]{:S(2)}) %collective-permute-start.2) | collective-permute-done | bytes 196640 | tf_op jit(solution)/shard_map/ppermute | solution.py:23
  25.7 1.0 %fusion = (f32[512,128]{1,0:T(8,128)S(1)}, f32[512,128]{1,0:T(8,128)S(1)}) fusion(f32[128]{0:T(128)S(1)} %get-tuple-element.47, f32[128]{0:T(128)S(1)} %get-tuple-element.48, f32[512]{0:T(512)S(1)} %fusion.1), kind=kLoop, calls=%fused_computation.3 | loop fusion | flops 131072 | bytes 527360 | tf_op jit(solution)/shard_map/mul | solution.py:337
  26.7 0.7 %reshape.63.refs_10_.refs_11_ = f32[1,1536]{1,0:T(1,128)S(1)} reshape(f32[1536]{0:T(1024)} %param.12) | data formatting | bytes 12288 | tf_op jit(solution)/shard_map/reshape | solution.py:339
  27.4 1.1 %copy-done.3 = bf16[512,768]{1,0:T(8,128)(2,1)S(1)} copy-done((bf16[512,768]{1,0:T(8,128)(2,1)S(1)}, bf16[512,768]{1,0:T(8,128)(2,1)}, u32[]{:S(2)}) %copy-start.3) | copy-done | bytes 786456
  28.5 1.0 %copy-done.5 = bf16[1536,96]{0,1:T(8,128)(2,1)S(1)} copy-done((bf16[1536,96]{0,1:T(8,128)(2,1)S(1)}, bf16[1536,96]{0,1:T(8,128)(2,1)}, u32[]{:S(2)}) %copy-start.5) | copy-done | bytes 294936
  29.5 0.9 %copy-done.7 = bf16[1536,64]{0,1:T(8,128)(2,1)S(1)} copy-done((bf16[1536,64]{0,1:T(8,128)(2,1)S(1)}, bf16[1536,64]{0,1:T(8,128)(2,1)}, u32[]{:S(2)}) %copy-start.7) | copy-done | bytes 196632
  30.4 2.7 %own_features.1 = (bf16[512,512]{1,0:T(8,128)(2,1)S(1)}, bf16[320,1536]{1,0:T(8,128)(2,1)S(1)}, bf16[128,768]{1,0:T(8,128)(2,1)S(1)}, f32[512,1]{1,0:T(8,128)S(1...) custom-call(bf16[128,128]{1,0:T(8,128)(2,1)S(1)} %get-tuple-element.27.refs_0_, ...), custom_call_target="tpu_custom_call" | custom-call | flops 654311424 | bytes 6103040 | tf_op jit(solution)/shard_map/own_features/pallas_call | solution.py:38
  33.2 4.7 %attend.1 = (bf16[128,768]{1,0:T(8,128)(2,1)S(1)}, bf16[128,768]{1,0:T(8,128)(2,1)S(1)}, bf16[128,1536]{1,0:T(8,128)(2,1)S(1)}) custom-call(bf16[128,768]{1,0:T(8,128)(2,1)S(1)} %collective-permute-done.refs_0_, bf16[128,768]{1,0:T(8,128)(2,1)S(1)} %collective-permute-done.1.refs_1_, bf16[128,768]{1,0:T(8,128)(2,1)S(1)} %collective-permute-done.2.refs_2_, ...), custom_call_target="tpu_custom_call" | custom-call | flops 1308622848 | bytes 8658944 | tf_op jit(solution)/shard_map/attend/pallas_call | solution.py:38
  37.9 1.6 %collective-permute-start.10 = (bf16[128,768]{1,0:T(8,128)(2,1)S(1)}, bf16[128,768]{1,0:T(8,128)(2,1)S(1)}, u32[]{:S(2)}, u32[]{:S(2)}) collective-permute-start(bf16[128,768]{1,0:T(8,128)(2,1)S(1)} %get-tuple-element.38.refs_0_), channel_id=1, source_target_pairs={{0,1},{1,0},{2,3},{3,2},{4,5},{5,4},{6,7},{7,6},{8,9},{9,8},{10,11... | collective-permute-start | bytes 589832 | tf_op jit(solution)/shard_map/ppermute | solution.py:23
  39.4 0.3 second_share.1.refs_0_
  39.8 0.6 %collective-permute-start.9 = (bf16[128,768]{1,0:T(8,128)(2,1)S(1)}, bf16[128,768]{1,0:T(8,128)(2,1)S(1)}, u32[]{:S(2)}, u32[]{:S(2)}) collective-permute-start(bf16[128,768]{1,0:T(8,128)(2,1)S(1)} %second_share.1.refs_0_), channel_id=1, source_target_pairs={{0,1},{1,0},{2,3},{3,2},{4,5},{5,4},{6,7},{7,6},{8,9},{9,8},{10,11... | collective-permute-start | bytes 589832 | tf_op jit(solution)/shard_map/ppermute | solution.py:23
  40.4 2.7 %copy.13 = bf16[1536,2,768]{2,0,1:T(8,128)(2,1)} copy(bf16[1536,2,768]{2,1,0:T(2,128)(2,1)S(1)} %bitcast.17) | data formatting | bytes 9437184 | tf_op jit(solution)/shard_map/optimization_barrier | solution.py:383
  43.1 2.5 %collective-permute-done.10.refs_1_ = bf16[128,768]{1,0:T(8,128)(2,1)S(1)} collective-permute-done((bf16[128,768]{1,0:T(8,128)(2,1)S(1)}, bf16[128,768]{1,0:T(8,128)(2,1)S(1)}, u32[]{:S(2)}, u32[]{:S(2)}) %collective-permute-start.10) | collective-permute-done | bytes 196640 | tf_op jit(solution)/shard_map/ppermute | solution.py:23
  45.6 3.0 %first_tracks.1 = (f32[128,1]{1,0:T(8,128)S(1)}, f32[128,768]{1,0:T(8,128)S(1)}, f32[128,768]{1,0:T(8,128)S(1)}) custom-call(bf16[128,768]{1,0:T(8,128)(2,1)S(1)} %get-tuple-element.38.refs_0_, bf16[128,768]{1,0:T(8,128)(2,1)S(1)} %collective-permute-done.10.refs_1_, bf16[128,1536]{1,0:T(8,128)(2,1)S(1)} %get-tuple-element.36.refs_2_, ...), custom_call_target="tpu_custom_call" | custom-call | flops 301989888 | bytes 6298112 | tf_op jit(solution)/shard_map/first_tracks/pallas_call | solution.py:38
  48.6 0.8 %collective-permute-done.9.refs_1_ = bf16[128,768]{1,0:T(8,128)(2,1)S(1)} collective-permute-done((bf16[128,768]{1,0:T(8,128)(2,1)S(1)}, bf16[128,768]{1,0:T(8,128)(2,1)S(1)}, u32[]{:S(2)}, u32[]{:S(2)}) %collective-permute-start.9) | collective-permute-done | bytes 196640 | tf_op jit(solution)/shard_map/ppermute | solution.py:23
  49.5 2.8 %sent_tracks.1 = (bf16[128,768]{1,0:T(8,128)(2,1)S(1)}, bf16[128,768]{1,0:T(8,128)(2,1)S(1)}, f32[128,1]{1,0:T(8,128)S(1)}) custom-call(bf16[128,768]{1,0:T(8,128)(2,1)S(1)} %second_share.1.refs_0_, bf16[128,768]{1,0:T(8,128)(2,1)S(1)} %collective-permute-done.9.refs_1_, bf16[128,1536]{1,0:T(8,128)(2,1)S(1)} %get-tuple-element.36.refs_2_, ...), custom_call_target="tpu_custom_call" | custom-call | flops 150994944 | bytes 6298624 | tf_op jit(solution)/shard_map/sent_tracks/pallas_call | solution.py:38
  52.4 0.5 kept_tracks.1.kept
  52.9 0.9 %collective-permute-done.11.received = bf16[128,768]{1,0:T(8,128)(2,1)S(1)} collective-permute-done((bf16[128,768]{1,0:T(8,128)(2,1)S(1)}, bf16[128,768]{1,0:T(8,128)(2,1)S(1)}, u32[]{:S(2)}, u32[]{:S(2)}) %collective-permute-start.11) | collective-permute-done | bytes 196640 | tf_op jit(solution)/shard_map/ppermute | solution.py:23
  53.8 1.0 %average.1 = f32[128,768]{1,0:T(8,128)} custom-call(bf16[128,768]{1,0:T(8,128)(2,1)S(1)} %kept_tracks.1.kept, bf16[128,768]{1,0:T(8,128)(2,1)S(1)} %collective-permute-done.11.received, s32[1,768]{1,0:T(1,128)S(1)} %reshape.65.pairs), custom_call_target="tpu_custom_call" | custom-call | bytes 789504 | tf_op jit(solution)/shard_map/average/pallas_call | solution.py:38
  (35 shorter events, 0.2 us)
Async XLA Ops:
  0.0 1.1 %copy-start.2 = (bf16[512,768]{1,0:T(8,128)(2,1)S(1)}, bf16[512,768]{1,0:T(8,128)(2,1)}, u32[]{:S(2)}) copy-start(bf16[512,768]{1,0:T(8,128)(2,1)} %refs_4_.1) | copy-start | bytes 2359300
  1.1 1.0 %copy-start.4 = (bf16[1536,96]{0,1:T(8,128)(2,1)S(1)}, bf16[1536,96]{0,1:T(8,128)(2,1)}, u32[]{:S(2)}) copy-start(bf16[1536,96]{0,1:T(8,128)(2,1)} %param.15) | copy-start | bytes 884740
  2.1 0.9 %copy-start.6 = (bf16[1536,64]{0,1:T(8,128)(2,1)S(1)}, bf16[1536,64]{0,1:T(8,128)(2,1)}, u32[]{:S(2)}) copy-start(bf16[1536,64]{0,1:T(8,128)(2,1)} %param.14) | copy-start | bytes 589828
  3.0 0.8 %copy-start.8 = (s32[16384]{0:T(1024)S(1)}, s32[16384]{0:T(1024)}, u32[]{:S(2)}) copy-start(s32[16384]{0:T(1024)} %param.10) | copy-start | bytes 196612
  4.4 14.6 %collective-permute-start.4 = (bf16[128,128]{1,0:T(8,128)(2,1)S(1)}, bf16[128,128]{1,0:T(8,128)(2,1)S(1)}, u32[]{:S(2)}, u32[]{:S(2)}) collective-permute-start(bf16[128,128]{1,0:T(8,128)(2,1)S(1)} %get-tuple-element.27.refs_0_), channel_id=1, source_target_pairs={{0,4},{4,8},{8,12},{12,0},{1,5},{5,9},{9,13},{13,1},{2,6},{6,10},{... | collective-permute-start | bytes 98312 | tf_op jit(solution)/shard_map/ppermute | solution.py:23
  7.5 19.9 %collective-permute-start.5 = (bf16[128,128]{1,0:T(8,128)(2,1)S(1)}, bf16[128,128]{1,0:T(8,128)(2,1)S(1)}, u32[]{:S(2)}, u32[]{:S(2)}) collective-permute-start(bf16[128,128]{1,0:T(8,128)(2,1)S(1)} %get-tuple-element.27.refs_0_), channel_id=1, source_target_pairs={{0,8},{4,12},{8,0},{12,4},{1,9},{5,13},{9,1},{13,5},{2,10},{6,14},... | collective-permute-start | bytes 98312 | tf_op jit(solution)/shard_map/ppermute | solution.py:23
  10.1 8.9 %collective-permute-start.7 = (bf16[160,768]{1,0:T(8,128)(2,1)S(1)}, bf16[160,768]{1,0:T(8,128)(2,1)S(1)}, u32[]{:S(2)}, u32[]{:S(2)}) collective-permute-start(bf16[160,768]{1,0:T(8,128)(2,1)S(1)} %get-tuple-element.28), channel_id=1, source_target_pairs={{0,1},{1,0},{2,3},{3,2},{4,5},{5,4},{6,7},{7,6},{8,9},{9,8},{10,11... | collective-permute-start | bytes 737288 | tf_op jit(solution)/shard_map/ppermute | solution.py:23
  11.6 11.6 %collective-permute-start = (bf16[128,768]{1,0:T(8,128)(2,1)S(1)}, bf16[128,768]{1,0:T(8,128)(2,1)S(1)}, u32[]{:S(2)}, u32[]{:S(2)}) collective-permute-start(bf16[128,768]{1,0:T(8,128)(2,1)S(1)} %get-tuple-element.25), channel_id=1, source_target_pairs={{0,1},{1,0},{2,3},{3,2},{4,5},{5,4},{6,7},{7,6},{8,9},{9,8},{10,11... | collective-permute-start | bytes 589832 | tf_op jit(solution)/shard_map/ppermute | solution.py:23
  12.1 13.5 %collective-permute-start.2 = (bf16[128,768]{1,0:T(8,128)(2,1)S(1)}, bf16[128,768]{1,0:T(8,128)(2,1)S(1)}, u32[]{:S(2)}, u32[]{:S(2)}) collective-permute-start(bf16[128,768]{1,0:T(8,128)(2,1)S(1)} %get-tuple-element.26), channel_id=1, source_target_pairs={{0,1},{1,0},{2,3},{3,2},{4,5},{5,4},{6,7},{7,6},{8,9},{9,8},{10,11... | collective-permute-start | bytes 589832 | tf_op jit(solution)/shard_map/ppermute | solution.py:23
  19.0 8.4 %collective-permute-start.8 = (bf16[160,768]{1,0:T(8,128)(2,1)S(1)}, bf16[160,768]{1,0:T(8,128)(2,1)S(1)}, u32[]{:S(2)}, u32[]{:S(2)}) collective-permute-start(bf16[160,768]{1,0:T(8,128)(2,1)S(1)} %collective-permute-done.7.refs_7_), channel_id=1, source_target_pairs={{0,2},{2,0},{1,3},{3,1},{4,6},{6,4},{5,7},{7,5},{8,10},{10,8},{9,1... | collective-permute-start | bytes 737288 | tf_op jit(solution)/shard_map/ppermute | solution.py:23
  19.0 8.4 %collective-permute-start.6 = (bf16[128,128]{1,0:T(8,128)(2,1)S(1)}, bf16[128,128]{1,0:T(8,128)(2,1)S(1)}, u32[]{:S(2)}, u32[]{:S(2)}) collective-permute-start(bf16[128,128]{1,0:T(8,128)(2,1)S(1)} %get-tuple-element.27.refs_0_), channel_id=1, source_target_pairs={{0,12},{4,0},{8,4},{12,8},{1,13},{5,1},{9,5},{13,9},{2,14},{6,2},{... | collective-permute-start | bytes 98312 | tf_op jit(solution)/shard_map/ppermute | solution.py:23
  23.2 9.9 %collective-permute-start.1 = (bf16[128,768]{1,0:T(8,128)(2,1)S(1)}, bf16[128,768]{1,0:T(8,128)(2,1)S(1)}, u32[]{:S(2)}, u32[]{:S(2)}) collective-permute-start(bf16[128,768]{1,0:T(8,128)(2,1)S(1)} %collective-permute-done.refs_0_), channel_id=1, source_target_pairs={{0,2},{2,0},{1,3},{3,1},{4,6},{6,4},{5,7},{7,5},{8,10},{10,8},{9,1... | collective-permute-start | bytes 589832 | tf_op jit(solution)/shard_map/ppermute | solution.py:23
  25.7 7.5 %collective-permute-start.3 = (bf16[128,768]{1,0:T(8,128)(2,1)S(1)}, bf16[128,768]{1,0:T(8,128)(2,1)S(1)}, u32[]{:S(2)}, u32[]{:S(2)}) collective-permute-start(bf16[128,768]{1,0:T(8,128)(2,1)S(1)} %collective-permute-done.2.refs_2_), channel_id=1, source_target_pairs={{0,2},{2,0},{1,3},{3,1},{4,6},{6,4},{5,7},{7,5},{8,10},{10,8},{9,1... | collective-permute-start | bytes 589832 | tf_op jit(solution)/shard_map/ppermute | solution.py:23
  27.4 1.1 %copy-start.3 = (bf16[512,768]{1,0:T(8,128)(2,1)S(1)}, bf16[512,768]{1,0:T(8,128)(2,1)}, u32[]{:S(2)}) copy-start(bf16[512,768]{1,0:T(8,128)(2,1)} %refs_4_.1) | copy-start | bytes 2359300
  28.5 1.0 %copy-start.5 = (bf16[1536,96]{0,1:T(8,128)(2,1)S(1)}, bf16[1536,96]{0,1:T(8,128)(2,1)}, u32[]{:S(2)}) copy-start(bf16[1536,96]{0,1:T(8,128)(2,1)} %param.15) | copy-start | bytes 884740
  29.5 0.9 %copy-start.7 = (bf16[1536,64]{0,1:T(8,128)(2,1)S(1)}, bf16[1536,64]{0,1:T(8,128)(2,1)}, u32[]{:S(2)}) copy-start(bf16[1536,64]{0,1:T(8,128)(2,1)} %param.14) | copy-start | bytes 589828
  33.1 6.3 %copy-start.1 = (bf16[768,1536]{1,0:T(8,128)(2,1)S(1)}, bf16[768,1536]{1,0:T(8,128)(2,1)}, u32[]{:S(2)}) copy-start(bf16[768,1536]{1,0:T(8,128)(2,1)} %w_out.1) | copy-start | bytes 7077892
  33.2 7.2 %slice-start = ((s8[4718592]{0:T(1024)(128)(4,1)}), s8[4194304]{0:T(1024)(128)(4,1)S(1)}, s32[]{:S(2)}) async-start(s8[4718592]{0:T(1024)(128)(4,1)} %bitcast.16), calls=%async_computation | async-start | bytes 8388608
  33.2 7.2 %copy-start.9 = (f32[1536]{0:T(1024)S(1)}, f32[1536]{0:T(1024)}, u32[]{:S(2)}) copy-start(f32[1536]{0:T(1024)} %param.17) | copy-start | bytes 18436
  33.2 7.2 %slice-start.1 = ((s8[4718592]{0:T(1024)(128)(4,1)}), s8[524288]{0:T(1024)(128)(4,1)S(1)}, s32[]{:S(2)}) async-start(s8[4718592]{0:T(1024)(128)(4,1)} %bitcast.16), calls=%async_computation.1 | async-start | bytes 1048576
  37.9 7.8 %collective-permute-start.10 = (bf16[128,768]{1,0:T(8,128)(2,1)S(1)}, bf16[128,768]{1,0:T(8,128)(2,1)S(1)}, u32[]{:S(2)}, u32[]{:S(2)}) collective-permute-start(bf16[128,768]{1,0:T(8,128)(2,1)S(1)} %get-tuple-element.38.refs_0_), channel_id=1, source_target_pairs={{0,1},{1,0},{2,3},{3,2},{4,5},{5,4},{6,7},{7,6},{8,9},{9,8},{10,11... | collective-permute-start | bytes 589832 | tf_op jit(solution)/shard_map/ppermute | solution.py:23
  39.8 9.7 %collective-permute-start.9 = (bf16[128,768]{1,0:T(8,128)(2,1)S(1)}, bf16[128,768]{1,0:T(8,128)(2,1)S(1)}, u32[]{:S(2)}, u32[]{:S(2)}) collective-permute-start(bf16[128,768]{1,0:T(8,128)(2,1)S(1)} %second_share.1.refs_0_), channel_id=1, source_target_pairs={{0,1},{1,0},{2,3},{3,2},{4,5},{5,4},{6,7},{7,6},{8,9},{9,8},{10,11... | collective-permute-start | bytes 589832 | tf_op jit(solution)/shard_map/ppermute | solution.py:23
  45.6 6.7 %copy-start.10 = (s32[768]{0:T(1024)S(1)}, s32[768]{0:T(1024)}, u32[]{:S(2)}) copy-start(s32[768]{0:T(1024)} %param.19) | copy-start | bytes 9220
  45.6 6.8 %copy-start = (bf16[1536,2,768]{2,0,1:T(8,128)(2,1)S(1)}, bf16[1536,2,768]{2,0,1:T(8,128)(2,1)}, u32[]{:S(2)}) copy-start(bf16[1536,2,768]{2,0,1:T(8,128)(2,1)} %copy.13) | copy-start | bytes 14155780
  52.3 1.5 %collective-permute-start.11 = (bf16[128,768]{1,0:T(8,128)(2,1)S(1)}, bf16[128,768]{1,0:T(8,128)(2,1)S(1)}, u32[]{:S(2)}, u32[]{:S(2)}) collective-permute-start(bf16[128,768]{1,0:T(8,128)(2,1)S(1)} %get-tuple-element.44), channel_id=1, source_target_pairs={{0,2},{2,0},{1,3},{3,1},{4,6},{6,4},{5,7},{7,5},{8,10},{10,8},{9,1... | collective-permute-start | bytes 589832 | tf_op jit(solution)/shard_map/ppermute | solution.py:23

commit v3 on v2

v3 whole, which is shorter than its diff:
```python
import functools
import math

import jax
import jax.experimental.pallas as pl
import jax.experimental.pallas.tpu as pltpu
import jax.numpy as jnp
from jax import lax
from jax.sharding import PartitionSpec as P

KDIM = 128
VDIM = 192
BIN = 128
BASES = 4
LANES = 128
VMEM_LIMIT = 48 * 2**20
F32 = jnp.float32
BF16 = jnp.bfloat16


def shifted(value, axis, distance):
    size = lax.axis_size(axis)
    return lax.ppermute(value, axis, [(i, (i + distance) % size) for i in range(size)])


def matmul(a, b):
    return jnp.dot(a, b, preferred_element_type=F32)


def matmul_t(a, b):
    return lax.dot_general(a, b, (((1,), (1,)), ((), ())), preferred_element_type=F32)


def call(kernel, outs, operands, name, scratch=(), spaces=None, flops=0, spare=0):
    vmem = pl.BlockSpec(memory_space=pltpu.VMEM)
    spaces = spaces or [None] * len(operands)
    operands = [
        v if s is None else pltpu.with_memory_space_constraint(v, s) for v, s in zip(operands, spaces)
    ]
    specs = [vmem if s is None else pl.BlockSpec(memory_space=s) for s in spaces]
    held = [v for v, s in zip(operands, spaces) if s is None] + list(outs)
    held += [v for v in scratch if hasattr(v, "shape") and hasattr(v, "dtype") and v.memory_space == pltpu.VMEM]
    moved = sum(math.prod(v.shape[:-1]) * max(v.shape[-1], LANES) * jnp.dtype(v.dtype).itemsize for v in held)
    return pl.pallas_call(
        kernel,
        out_shape=list(outs),
        in_specs=specs,
        out_specs=[vmem] * len(outs),
        scratch_shapes=list(scratch),
        compiler_params=pltpu.CompilerParams(
            vmem_limit_bytes=min(VMEM_LIMIT, moved + moved // 4 + 6 * 2**20 + spare)
        ),
        cost_estimate=pl.CostEstimate(flops=flops, bytes_accessed=moved, transcendentals=0),
        name=name,
    )(*operands)


def shape(dims, dtype):
    return jax.ShapeDtypeStruct(tuple(dims), dtype)


def over_blocks(total, block, step):
    if total == block:
        step(0)
    else:

        def one(i, carry):
            step(pl.multiple_of(i * block, block))
            return carry

        lax.fori_loop(0, total // block, one, 0)


def stage_kernel(chunks, embed, key_t, value_t, *refs):
    part_kv, pieces, sems = refs[0], refs[1 : 1 + chunks], refs[1 + chunks]
    strand = lax.axis_index("strand")
    part = strand * lax.axis_size("groups") + lax.axis_index("groups")
    key_cols, value_cols = key_t.shape[0], value_t.shape[0]
    kv_width = part_kv.shape[1]
    half, width = pieces[0].shape
    cols = pl.ds(pl.multiple_of(part * kv_width, LANES), kv_width)
    rows = pl.ds(pl.multiple_of(strand * half, half), half)
    copies = [
        pltpu.make_async_copy(key_t.at[:, cols], part_kv.at[pl.ds(0, key_cols)], sems.at[0]),
        pltpu.make_async_copy(value_t.at[:, cols], part_kv.at[pl.ds(key_cols, value_cols)], sems.at[1]),
    ]
    for i in range(chunks):
        source = embed.at[rows, pl.ds(i * width, width)]
        copies.append(pltpu.make_async_copy(source, pieces[i], sems.at[2 + i]))
    for copy in copies:
        copy.start()
    for copy in copies:
        copy.wait()


def prepare_kernel(embed, key_t, value_t, w_query, gain, last_gain, codes, *refs):
    table, key_out, value_out, query_out, gain_out, last_out, cosine, sine, codes_out = refs[:9]
    raw_gain, raw_last, raw_codes, sems = refs[9:]
    strand, pos = lax.axis_index("strand"), lax.axis_index("pos")
    half = embed.shape[0] // 2
    pairs = [(codes, raw_codes), (gain, raw_gain), (last_gain, raw_last)]
    for i in range(2):
        part = strand if i == 0 else 1 - strand
        source = embed.at[pl.ds(pl.multiple_of(part * half, half), half)]
        pairs.append((source, table.at[pl.ds(i * half, half)]))
    pairs += [(key_t, key_out), (value_t, value_out), (w_query, query_out)]
    copies = [pltpu.make_async_copy(a, b, sems.at[i]) for i, (a, b) in enumerate(pairs)]
    for copy in copies:
        copy.start()
    total = cosine.shape[0]
    rows = codes.shape[0]
    blocks = total // rows
    lane = lax.broadcasted_iota(jnp.int32, (1, KDIM), 1)
    inverse = jnp.exp((lane % (KDIM // 2)).astype(F32) * (-math.log(10000.0) / (KDIM // 2)))
    sign = jnp.where(lane < KDIM // 2, -1.0, 1.0)
    offset = lax.broadcasted_iota(jnp.int32, (rows, KDIM), 0)
    for copy in copies[:3]:
        copy.wait()
    codes_out[...] = raw_codes[...].astype(F32).astype(BF16)
    gain_out[...] = raw_gain[...].reshape(gain_out.shape)
    last_out[...] = raw_last[...].reshape(last_out.shape)

    def step(begin):
        place = lax.rem(pos + blocks - begin // rows, blocks) * rows + offset
        angle = jnp.where(strand == 0, place, total - 1 - place).astype(F32) * inverse
        cosine[pl.ds(begin, rows), :] = jnp.cos(angle)
        sine[pl.ds(begin, rows), :] = jnp.sin(angle) * sign

    if blocks <= 4:
        for i in range(blocks):
            step(i * rows)
    else:
        over_blocks(total, rows, step)
    for copy in copies[3:]:
        copy.wait()


def absorb(onehot, table, rows, start, width, weights, before, after):
    kv_t, w_query, gain = weights
    total = onehot.shape[0]
    block = min(total, 4 * rows)
    cols = pl.ds(pl.multiple_of(start, LANES), width)

    def some(here):
        found = matmul(onehot[here, :], table[...]).astype(BF16)
        floats = found.astype(F32)
        return found, floats, (floats * gain[:, cols]).astype(BF16)

    def step(begin):
        here = pl.ds(begin, block)
        found, floats, gained = some(here)
        square = jnp.sum(floats * floats, axis=1, keepdims=True)
        kv = matmul_t(gained, kv_t[:, cols])
        after[0][here, :] = square if before is None else before[0][here, :] + square
        after[1][here, :] = kv if before is None else before[1][here, :] + kv
        return found, gained

    if total == block:
        found, gained = step(0)
        found, gained = found[:rows], gained[:rows]
    else:
        over_blocks(total, block, lambda begin: step(begin) and None)
        found, _, gained = some(pl.ds(0, rows))
    query = matmul(gained, w_query[cols, :])
    after[2][...] = query if before is None else before[2][...] + query
    return found


def own_kernel(blocks, kv_steps, *refs):
    codes = refs[:blocks]
    table, key_t, value_t = refs[blocks : blocks + 3]
    parts = refs[blocks + 3 : blocks + 3 + len(kv_steps)]
    w_query, gain, onehot, kv_t, own, square, kv_sum, q_sum, all_codes = refs[blocks + 3 + len(kv_steps) :]
    strand, mine, group = lax.axis_index("strand"), lax.axis_index("heads"), lax.axis_index("groups")
    size, groups = lax.axis_size("heads"), lax.axis_size("groups")
    key_cols, value_cols = key_t.shape[0], value_t.shape[0]
    entries, width = table.shape
    half = entries // 2
    rows = codes[0].shape[0]
    total = blocks * rows
    for i in range(blocks):
        all_codes[i * rows : (i + 1) * rows, :] = codes[i][...]

    def kv_rows(owner):
        key_rows = pl.ds(pl.multiple_of(owner * key_cols, 16), key_cols)
        return key_rows, pl.ds(pl.multiple_of(KDIM + owner * value_cols, 16), value_cols)

    key_rows, value_rows = kv_rows(mine)
    kv_t[key_rows, :] = key_t[...]
    kv_t[value_rows, :] = value_t[...]
    for piece, (step, group_step, core_step) in zip(parts, kv_steps):
        key_rows, value_rows = kv_rows(lax.rem(mine + size - step, size))
        core = strand if core_step == 0 else 1 - strand
        part = core * groups + lax.rem(group + groups - group_step, groups)
        cols = pl.ds(pl.multiple_of(part * piece.shape[1], LANES), piece.shape[1])
        kv_t[key_rows, cols] = piece[:key_cols, :]
        kv_t[value_rows, cols] = piece[key_cols:, :]
    spot = lax.broadcasted_iota(jnp.int32, (BIN, entries), 1)
    owner = jnp.where(spot < half, strand, 1 - strand)
    entry = owner * half + spot % half
    entry = jnp.where(strand == 0, entry, entries - 1 - entry)
    place = lax.broadcasted_iota(jnp.int32, (BIN, entries), 0)
    spread = jnp.where(place == entry // BASES, 1.0, 0.0).astype(BF16)
    wanted = (entry[:1] % BASES).astype(F32)
    block = min(total, 4 * rows)

    def mark(begin):
        here = pl.ds(begin, block)
        found = matmul(all_codes[here, :], spread) == wanted
        onehot[here, :] = jnp.where(found, 1.0, 0.0).astype(BF16)

    over_blocks(total, block, mark)
    own[...] = absorb(
        onehot, table, rows, mine * width, width, (kv_t, w_query, gain), None, (square, kv_sum, q_sum)
    )


def chunk_start(step, index, chunks, width):
    size = lax.axis_size("heads")
    owner = lax.rem(lax.axis_index("heads") + size - step, size)
    return (owner * chunks + index) * width


def chunk_kernel(step, index, chunks, rows, *refs):
    mine, theirs, onehot, kv_t, w_query, gain, square, kv_sum, q_sum = refs[:9]
    found, square_out, kv_out, q_out, table = refs[9:]
    half, width = mine.shape
    table[:half, :] = mine[...]
    table[half:, :] = theirs[...]
    found[...] = absorb(
        onehot,
        table,
        rows,
        chunk_start(step, index, chunks, width),
        width,
        (kv_t, w_query, gain),
        (square, kv_sum, q_sum),
        (square_out, kv_out, q_out),
    )


def turn(values, cosine, sine):
    floats = values.astype(BF16).astype(F32)
    return (floats * cosine + pltpu.roll(floats, KDIM // 2, 1) * sine).astype(BF16)


def attend_kernel(steps, chunks, *refs):
    mine, theirs, onehot, kv_t, w_query, gain, square, kv_sum, q_sum = refs[:9]
    own, cosine, sine, w_out = refs[9:13]
    founds = refs[13 : 13 + len(steps) - 1]
    share, merged, inputs, table, squares, sums, queries, keys, values = refs[12 + len(steps) :]
    half, width = mine.shape
    rows, own_width = own.shape
    features = inputs.shape[1]
    total = onehot.shape[0]
    block = min(total, 4 * rows)
    table[:half, :] = mine[...]
    table[half:, :] = theirs[...]
    start = chunk_start(*steps[-1], chunks, width)
    last = absorb(
        onehot, table, rows, start, width, (kv_t, w_query, gain), (square, kv_sum, q_sum), (squares, sums, queries)
    )
    inputs[:, pl.ds(pl.multiple_of(start, LANES), width)] = last
    for found, spot in zip(founds, steps):
        inputs[:, pl.ds(pl.multiple_of(chunk_start(*spot, chunks, width), LANES), width)] = found[...]
    begin = pl.multiple_of(lax.axis_index("heads") * own_width, LANES)
    inputs[:, pl.ds(begin, own_width)] = own[...]

    def finish(begin):
        here = pl.ds(begin, block)
        scaled = sums[here, :] * lax.rsqrt(squares[here, :] / features + 1e-06)
        keys[here, :] = turn(scaled[:, :KDIM], cosine[here, :], sine[here, :])
        values[here, :] = scaled[:, KDIM:].astype(BF16)

    over_blocks(total, block, finish)
    scaled = queries[...] * lax.rsqrt(squares[:rows, :] / features + 1e-06)
    for head in range(queries.shape[1] // KDIM):
        query = turn(scaled[:, head * KDIM : (head + 1) * KDIM], cosine[:rows, :], sine[:rows, :])
        scores = matmul_t(query, keys[...]) * KDIM ** (-0.5)
        weights = jnp.exp(scores - jnp.max(scores, axis=1, keepdims=True))
        weight_sum = jnp.sum(weights, axis=1, keepdims=True)
        found = (matmul(weights.astype(BF16), values[...]) / weight_sum).astype(BF16)
        merged[:, head * VDIM : (head + 1) * VDIM] = found
    share[...] = matmul(merged[...], w_out[:, : w_out.shape[1] // 2]).astype(BF16)


def second_kernel(merged, w_out, share):
    half = w_out.shape[1] // 2
    share[...] = matmul(merged[...], w_out[:, half:]).astype(BF16)


def gather_hidden(shares, inputs, gain, chunk):
    width = shares[0].shape[1]
    cols = slice(chunk * width, (chunk + 1) * width)
    total = shares[0][...].astype(F32)
    for other in shares[1:]:
        total = total + other[...].astype(F32)
    hidden = (inputs[:, cols].astype(F32) + total).astype(BF16).astype(F32)
    return jnp.sum(hidden * hidden, axis=1, keepdims=True), (hidden * gain[:, cols]).astype(BF16)


def soft(logits):
    return jnp.maximum(logits, 0.0) + jnp.log1p(jnp.exp(-jnp.abs(logits)))


def first_tracks_kernel(size, *refs):
    shares = refs[:size]
    inputs, gain, tracks, square, to_send, to_keep = refs[size:]
    strand = lax.axis_index("strand")
    width = shares[0].shape[1]
    square[...], gained = gather_hidden(shares, inputs, gain, 0)
    to_send[...] = matmul(gained, tracks[1 - strand, :width, :])
    to_keep[...] = matmul(gained, tracks[strand, :width, :])


def send_kernel(size, *refs):
    shares = refs[:size]
    inputs, gain, tracks, square, to_send, sent, gained_out, scale_out = refs[size:]
    strand = lax.axis_index("strand")
    width = shares[0].shape[1]
    total, gained = gather_hidden(shares, inputs, gain, 1)
    scale = lax.rsqrt((square[...] + total) / (2 * width) + 1e-06)
    logits = to_send[...] + matmul(gained, tracks[1 - strand, width:, :])
    sent[...] = soft(logits * scale).astype(BF16)
    gained_out[...] = gained
    scale_out[...] = scale


def keep_kernel(gained, tracks, to_keep, scale, kept):
    strand = lax.axis_index("strand")
    width = gained.shape[1]
    logits = to_keep[...] + matmul(gained[...], tracks[strand, width:, :])
    kept[...] = soft(logits * scale[...]).astype(BF16)


def average_kernel(kept, received, pairs, out):
    strand = lax.axis_index("strand")
    count = kept.shape[1]
    mine, theirs = kept[...].astype(F32), received[...].astype(F32)
    forward = jnp.where(strand == 0, mine, theirs)
    reverse = jnp.where(strand == 0, theirs, mine)
    index = lax.broadcasted_iota(jnp.int32, (1, count), 1)
    even = index % 2 == 0
    swapped = (pairs[...] % 2 == 0) != even
    partner = jnp.where(even, pltpu.roll(reverse, count - 1, 1), pltpu.roll(reverse, 1, 1))
    out[...] = 0.5 * (forward + jnp.where(swapped, partner, reverse))


def body(
    base_codes,
    embed_table,
    attn_gain,
    w_query,
    w_key,
    w_value,
    w_out,
    head_gain,
    w_tracks,
    track_pairs,
):
    rows = base_codes.shape[0] // BIN
    blocks = lax.axis_size("pos")
    size = lax.axis_size("heads")
    features, q_cols = w_query.shape
    entries, width = embed_table.shape
    groups = lax.axis_size("groups")
    key_t, value_t = w_key.T, w_value.T
    kv_cols = key_t.shape[0] + value_t.shape[0]
    kv_all = KDIM + VDIM
    half = entries // 2
    total = blocks * rows
    tracks_half = w_tracks.shape[2]
    chunks = 2 if width % (2 * LANES) == 0 else 1
    wide = width // chunks

    hbm = pltpu.HBM
    part_kv, *own_pieces = call(
        functools.partial(stage_kernel, chunks),
        [shape((kv_cols, features // (2 * groups)), BF16)] + [shape((half, wide), BF16)] * chunks,
        [embed_table, key_t, value_t],
        "stage",
        scratch=[pltpu.SemaphoreType.DMA((2 + chunks,))],
        spaces=[hbm] * 3,
    )
    table, key_own, value_own, query_own, gain, last_gain, cosine, sine, own_codes = call(
        prepare_kernel,
        [
            shape((entries, width), BF16),
            shape(key_t.shape, BF16),
            shape(value_t.shape, BF16),
            shape(w_query.shape, BF16),
            shape((1, features), F32),
            shape((1, features), F32),
            shape((total, KDIM), F32),
            shape((total, KDIM), F32),
            shape((rows, BIN), BF16),
        ],
        [embed_table, key_t, value_t, w_query, attn_gain, head_gain, base_codes.reshape(rows, BIN)],
        "prepare",
        scratch=[
            pltpu.VMEM((features,), F32),
            pltpu.VMEM((features,), F32),
            pltpu.VMEM((rows, BIN), jnp.int32),
            pltpu.SemaphoreType.DMA((8,)),
        ],
        spaces=[hbm] * 7,
    )
    kv_parts, kv_steps, pieces, steps = [], [], [], []
    from_heads = [shifted(part_kv, "heads", step) for step in range(1, size)]
    if from_heads:
        from_heads[0], own_codes = lax.optimization_barrier((from_heads[0], own_codes))
    codes = [own_codes] + [shifted(own_codes, "pos", k) for k in range(1, blocks)]
    for step in range(1, size):
        for k in range(groups):
            here = from_heads[step - 1] if k == 0 else shifted(from_heads[step - 1], "groups", k)
            if step == 1 and k == groups - 1:
                here, *codes = lax.optimization_barrier((here, *codes))
            kv_parts += [here, shifted(here, "strand", 1)]
            kv_steps += [(step, k, 0), (step, k, 1)]
    for step in range(1, size):
        for i in range(chunks):
            here = shifted(own_pieces[i], "heads", step)
            pieces.append((here, shifted(here, "strand", 1)))
            steps.append((step, i))

    sums = [shape((total, 1), F32), shape((total, kv_all), F32), shape((rows, q_cols), F32)]
    onehot, kv_t, own, *state = call(
        functools.partial(own_kernel, blocks, kv_steps),
        [shape((total, entries), BF16), shape((kv_all, features), BF16), shape((rows, width), BF16)] + sums,
        codes + [table, key_own, value_own] + kv_parts + [query_own, gain],
        "own_features",
        scratch=[pltpu.VMEM((total, BIN), BF16)],
        flops=2 * total * width * (entries + kv_all),
        spare=8 * total * entries,
    )
    founds = []
    for (step, i), pair in zip(steps[:-1], pieces[:-1]):
        found, *state = call(
            functools.partial(chunk_kernel, step, i, chunks, rows),
            [shape((rows, wide), BF16)] + sums,
            list(pair) + [onehot, kv_t, query_own, gain] + state,
            "other_features",
            scratch=[pltpu.VMEM((entries, wide), BF16)],
            flops=2 * total * wide * (entries + kv_all),
            spare=8 * total * entries,
        )
        founds.append(found)
    o_cols = q_cols // KDIM * VDIM
    share_one, merged, inputs = call(
        functools.partial(attend_kernel, steps, chunks),
        [
            shape((rows, features // 2), BF16),
            shape((rows, o_cols), BF16),
            shape((rows, features), BF16),
        ],
        list(pieces[-1]) + [onehot, kv_t, query_own, gain] + state + [own, cosine, sine, w_out] + founds,
        "attend",
        scratch=[
            pltpu.VMEM((entries, wide), BF16),
            pltpu.VMEM((total, 1), F32),
            pltpu.VMEM((total, kv_all), F32),
            pltpu.VMEM((rows, q_cols), F32),
            pltpu.VMEM((total, KDIM), BF16),
            pltpu.VMEM((total, VDIM), BF16),
        ],
        flops=2 * total * wide * (entries + kv_all) + 2 * total * q_cols * rows * 3,
        spare=8 * total * entries,
    )
    (share_two,) = call(
        second_kernel,
        [shape((rows, features // 2), BF16)],
        [merged, w_out],
        "second_share",
        flops=rows * o_cols * features,
    )
    ones = [share_one] + [shifted(share_one, "heads", k) for k in range(1, size)]
    twos = [share_two] + [shifted(share_two, "heads", k) for k in range(1, size)]
    weights, _ = lax.optimization_barrier((w_tracks, share_two))
    tracks = lax.optimization_barrier(weights.transpose(1, 0, 2))
    square, to_send, to_keep = call(
        functools.partial(first_tracks_kernel, size),
        [
            shape((rows, 1), F32),
            shape((rows, tracks_half), F32),
            shape((rows, tracks_half), F32),
        ],
        ones + [inputs, last_gain, tracks],
        "first_tracks",
        flops=2 * rows * features * tracks_half,
    )
    sent, gained, scale = call(
        functools.partial(send_kernel, size),
        [
            shape((rows, tracks_half), BF16),
            shape((rows, features // 2), BF16),
            shape((rows, 1), F32),
        ],
        twos + [inputs, last_gain, tracks, square, to_send],
        "sent_tracks",
        flops=rows * features * tracks_half,
    )
    received = shifted(sent, "strand", 1)
    (kept,) = call(
        keep_kernel,
        [shape((rows, tracks_half), BF16)],
        [gained, tracks, to_keep, scale],
        "kept_tracks",
        flops=rows * features * tracks_half,
    )
    (out,) = call(
        average_kernel,
        [shape((rows, tracks_half), F32)],
        [kept, received, track_pairs.reshape(1, tracks_half)],
        "average",
    )
    return out


def solution(mesh):
    placed = (
        P(("groups", "pos")),
        P(None, "heads"),
        P(),
        P(None, "heads"),
        P(None, "heads"),
        P(None, "heads"),
        P("heads", None),
        P(),
        P(None, None, "heads"),
        P(("strand", "heads")),
    )
    return jax.shard_map(
        body,
        mesh=mesh,
        in_specs=placed,
        out_specs=P(("groups", "pos"), ("strand", "heads")),
        check_vma=False,
    )
```

time: 55.3 us -> 41 us (0.74)
  local copies, waits for them, and re-layouts: 10.4 us -> 1.6 us
  Pallas kernels: 15.6 us -> 9.95 us
  starting transfers between devices: 12.8 us -> 16.2 us
  waiting for transfers between devices: 14.8 us -> 12.9 us
  other arithmetic: 1.08 us -> 0.01 us
    unnamed x26 -> x8, local copies, waits for them, and re-layouts: 6.91 us -> 1 us
    pallas_call x8 -> x10, Pallas kernels: 15.6 us -> 9.95 us  [call(): pl.pallas_call(kernel, out_shape=list(outs), in_specs=specs, out_specs=[v...]
    ppermute x12 -> x14, starting transfers between devices: 12.8 us -> 16.2 us  [shifted(): lax.ppermute(value, axis, [(i, (i + distance) % size) for i in range(size)])]
    optimization_barrier x1, local copies, waits for them, and re-layouts: 2.75 us -> 0.6 us  [body(): weights, _ = lax.optimization_barrier((w_tracks, share_two))]
    ppermute x12 -> x14, waiting for transfers between devices: 14.8 us -> 12.9 us  [shifted(): lax.ppermute(value, axis, [(i, (i + distance) % size) for i in range(size)])]
    mul x2 -> x0, other arithmetic: 1 us -> none  [the longest x1 0.99 us: body(): sine = jnp.sin(angles) * jnp.where(lane < half, -1.0, 1.0)]
    reshape x2 -> x0, local copies, waits for them, and re-layouts: 0.71 us -> none  [the longest x1 0.7 us: body(): gain = attn_gain.reshape(1, features)]
  transfers between devices with their start and end apart: 12 -> 14, of which waited for: 6 -> 7; matrix products, arithmetic and copies ran while one was open for 8% -> 1% of each run, Pallas kernels for 12% -> 13%
where the time goes in v3:
time: 41 us; the launch traced here: 40.8 us
  starting transfers between devices  16.2 us (40%)
  waiting for transfers between devices  12.9 us (31%)
  Pallas kernels  9.95 us (24%)
  local copies, waits for them, and re-layouts  1.6 us (4%)
    ppermute x14, starting transfers between devices, shifted(): lax.ppermute(value, axis, [(i, (i + distance) % size) for i in range(size)])  16.2 us
    ppermute x14, waiting for transfers between devices, shifted(): lax.ppermute(value, axis, [(i, (i + distance) % size) for i in range(size)])  12.9 us
    pallas_call x10, Pallas kernels, call(): pl.pallas_call(kernel, out_shape=list(outs), in_specs=specs, out_specs=[v...  9.95 us
    unnamed x8, local copies, waits for them, and re-layouts  1 us
  transfers between devices with their start and end apart: 14, of which 7 were waited for; matrix products, arithmetic and copies ran while one was open for 1% of the time, Pallas kernels for 13%

profile of v3, /device:TPU:0, one launch (start us, length us, event | category | flops | bytes accessed | tf_op | source)
XLA Modules:
  0.0 40.8 jit_solution(11148461919883073708)
XLA Ops:
  0.0 1.1 %stage.1 = (bf16[160,384]{1,0:T(8,128)(2,1)S(1)}, bf16[256,384]{1,0:T(8,128)(2,1)S(1)}, bf16[256,384]{1,0:T(8,128)(2,1)S(1)}) custom-call(bf16[512,768]{1,0:T(8,128)(2,1)} %embed.3, bf16[64,1536]{1,0:T(8,128)(2,1)} %bitcast.13, bf16[96,1536]{1,0:T(8,128)(2,1)} %bitcast.11), custom_call_target="tpu_custom_call" | custom-call | bytes 516096 | tf_op jit(solution)/shard_map/stage/pallas_call | solution.py:44
  1.1 3.0 %collective-permute-start.2 = (bf16[160,384]{1,0:T(8,128)(2,1)S(1)}, bf16[160,384]{1,0:T(8,128)(2,1)S(1)}, u32[]{:S(2)}, u32[]{:S(2)}) collective-permute-start(bf16[160,384]{1,0:T(8,128)(2,1)S(1)} %get-tuple-element.45), channel_id=1, source_target_pairs={{0,1},{1,0},{2,3},{3,2},{4,5},{5,4},{6,7},{7,6},{8,9},{9,8},{10,11... | collective-permute-start | bytes 368648 | tf_op jit(solution)/shard_map/ppermute | solution.py:23
  4.1 0.1 collective-permute-start.9
  4.2 1.9 %collective-permute-start = (bf16[256,384]{1,0:T(8,128)(2,1)S(1)}, bf16[256,384]{1,0:T(8,128)(2,1)S(1)}, u32[]{:S(2)}, u32[]{:S(2)}) collective-permute-start(bf16[256,384]{1,0:T(8,128)(2,1)S(1)} %get-tuple-element.44), channel_id=1, source_target_pairs={{0,1},{1,0},{2,3},{3,2},{4,5},{5,4},{6,7},{7,6},{8,9},{9,8},{10,11... | collective-permute-start | bytes 589832 | tf_op jit(solution)/shard_map/ppermute | solution.py:23
  6.2 1.9 %prepare.1 = (bf16[512,768]{1,0:T(8,128)(2,1)S(1)}, bf16[64,1536]{1,0:T(8,128)(2,1)S(1)}, bf16[96,1536]{1,0:T(8,128)(2,1)S(1)}, bf16[1536,512]{1,0:T(8,128)(2,1)...) custom-call(bf16[512,768]{1,0:T(8,128)(2,1)} %embed.3, ...), custom_call_target="tpu_custom_call" | custom-call | bytes 3497984 | tf_op jit(solution)/shard_map/prepare/pallas_call | solution.py:44
  8.1 0.2 collective-permute-done.2.refs_7_
  8.3 2.1 %collective-permute-start.3 = (bf16[160,384]{1,0:T(8,128)(2,1)S(1)}, bf16[160,384]{1,0:T(8,128)(2,1)S(1)}, u32[]{:S(2)}, u32[]{:S(2)}) collective-permute-start(bf16[160,384]{1,0:T(8,128)(2,1)S(1)} %collective-permute-done.2.refs_7_), channel_id=1, source_target_pairs={{0,16},{16,0},{1,17},{17,1},{2,18},{18,2},{3,19},{19,3},{4,20},{20... | collective-permute-start | bytes 368648 | tf_op jit(solution)/shard_map/ppermute | solution.py:23
  10.4 1.6 %collective-permute-start.4 = (bf16[128,128]{1,0:T(8,128)(2,1)S(1)}, bf16[128,128]{1,0:T(8,128)(2,1)S(1)}, u32[]{:S(2)}, u32[]{:S(2)}) collective-permute-start(bf16[128,128]{1,0:T(8,128)(2,1)S(1)} %get-tuple-element.49.refs_0_), channel_id=1, source_target_pairs={{0,4},{4,8},{8,12},{12,0},{1,5},{5,9},{9,13},{13,1},{2,6},{6,10},{... | collective-permute-start | bytes 98312 | tf_op jit(solution)/shard_map/ppermute | solution.py:23
  11.9 2.6 %collective-permute-start.5 = (bf16[128,128]{1,0:T(8,128)(2,1)S(1)}, bf16[128,128]{1,0:T(8,128)(2,1)S(1)}, u32[]{:S(2)}, u32[]{:S(2)}) collective-permute-start(bf16[128,128]{1,0:T(8,128)(2,1)S(1)} %get-tuple-element.49.refs_0_), channel_id=1, source_target_pairs={{0,8},{4,12},{8,0},{12,4},{1,9},{5,13},{9,1},{13,5},{2,10},{6,14},... | collective-permute-start | bytes 98312 | tf_op jit(solution)/shard_map/ppermute | solution.py:23
  14.5 1.7 %collective-permute-done.4.refs_1_ = bf16[128,128]{1,0:T(8,128)(2,1)S(1)} collective-permute-done((bf16[128,128]{1,0:T(8,128)(2,1)S(1)}, bf16[128,128]{1,0:T(8,128)(2,1)S(1)}, u32[]{:S(2)}, u32[]{:S(2)}) %collective-permute-start.4) | collective-permute-done | bytes 32800 | tf_op jit(solution)/shard_map/ppermute | solution.py:23
  16.2 1.7 %collective-permute-start.6 = (bf16[128,128]{1,0:T(8,128)(2,1)S(1)}, bf16[128,128]{1,0:T(8,128)(2,1)S(1)}, u32[]{:S(2)}, u32[]{:S(2)}) collective-permute-start(bf16[128,128]{1,0:T(8,128)(2,1)S(1)} %get-tuple-element.49.refs_0_), channel_id=1, source_target_pairs={{0,12},{4,0},{8,4},{12,8},{1,13},{5,1},{9,5},{13,9},{2,14},{6,2},{... | collective-permute-start | bytes 98312 | tf_op jit(solution)/shard_map/ppermute | solution.py:23
  17.9 0.5 %collective-permute-start.7 = (bf16[160,384]{1,0:T(8,128)(2,1)S(1)}, bf16[160,384]{1,0:T(8,128)(2,1)S(1)}, u32[]{:S(2)}, u32[]{:S(2)}) collective-permute-start(bf16[160,384]{1,0:T(8,128)(2,1)S(1)} %collective-permute-done.2.refs_7_), channel_id=1, source_target_pairs={{0,2},{2,0},{1,3},{3,1},{4,6},{6,4},{5,7},{7,5},{8,10},{10,8},{9,1... | collective-permute-start | bytes 368648 | tf_op jit(solution)/shard_map/ppermute | solution.py:23
  18.4 1.7 %collective-permute-done.6.refs_3_ = bf16[128,128]{1,0:T(8,128)(2,1)S(1)} collective-permute-done((bf16[128,128]{1,0:T(8,128)(2,1)S(1)}, bf16[128,128]{1,0:T(8,128)(2,1)S(1)}, u32[]{:S(2)}, u32[]{:S(2)}) %collective-permute-start.6) | collective-permute-done | bytes 32800 | tf_op jit(solution)/shard_map/ppermute | solution.py:23
  20.1 0.5 %collective-permute-start.1 = (bf16[256,384]{1,0:T(8,128)(2,1)S(1)}, bf16[256,384]{1,0:T(8,128)(2,1)S(1)}, u32[]{:S(2)}, u32[]{:S(2)}) collective-permute-start(bf16[256,384]{1,0:T(8,128)(2,1)S(1)} %collective-permute-done.refs_0_), channel_id=1, source_target_pairs={{0,2},{2,0},{1,3},{3,1},{4,6},{6,4},{5,7},{7,5},{8,10},{10,8},{9,1... | collective-permute-start | bytes 589832 | tf_op jit(solution)/shard_map/ppermute | solution.py:23
  20.6 0.8 %collective-permute-done.8.refs_10_ = bf16[160,384]{1,0:T(8,128)(2,1)S(1)} collective-permute-done((bf16[160,384]{1,0:T(8,128)(2,1)S(1)}, bf16[160,384]{1,0:T(8,128)(2,1)S(1)}, u32[]{:S(2)}, u32[]{:S(2)}) %collective-permute-start.8) | collective-permute-done | bytes 122912 | tf_op jit(solution)/shard_map/ppermute | solution.py:23
  21.4 1.3 %own_features.1 = (bf16[512,512]{1,0:T(8,128)(2,1)S(1)}, bf16[320,1536]{1,0:T(8,128)(2,1)S(1)}, bf16[128,768]{1,0:T(8,128)(2,1)S(1)}, f32[512,1]{1,0:T(8,128)S(1...) custom-call(bf16[128,128]{1,0:T(8,128)(2,1)S(1)} %get-tuple-element.49.refs_0_, ...), custom_call_target="tpu_custom_call" | custom-call | flops 654311424 | bytes 6494208 | tf_op jit(solution)/shard_map/own_features/pallas_call | solution.py:44
  22.8 0.8 %other_features.1 = (bf16[128,384]{1,0:T(8,128)(2,1)S(1)}, f32[512,1]{1,0:T(8,128)S(1)}, f32[512,320]{1,0:T(8,128)S(1)}, f32[128,512]{1,0:T(8,128)S(1)}) custom-call(bf16[256,384]{1,0:T(8,128)(2,1)S(1)} %collective-permute-done.9.refs_0_, bf16[256,384]{1,0:T(8,128)(2,1)S(1)} %collective-permute-done.10.refs_1_, ...), custom_call_target="tpu_custom_call" | custom-call | flops 327155712 | bytes 6330368 | tf_op jit(solution)/shard_map/other_features/pallas_call | solution.py:44
  23.5 0.9 %copy-done = bf16[768,1536]{1,0:T(8,128)(2,1)S(1)} copy-done((bf16[768,1536]{1,0:T(8,128)(2,1)S(1)}, bf16[768,1536]{1,0:T(8,128)(2,1)}, u32[]{:S(2)}) %copy-start) | copy-done | bytes 2359320
  24.4 2.1 %attend.1 = (bf16[128,768]{1,0:T(8,128)(2,1)S(1)}, bf16[128,768]{1,0:T(8,128)(2,1)S(1)}, bf16[128,1536]{1,0:T(8,128)(2,1)S(1)}) custom-call(bf16[256,384]{1,0:T(8,128)(2,1)S(1)} %collective-permute-done.refs_0_, bf16[256,384]{1,0:T(8,128)(2,1)S(1)} %collective-permute-done.1.refs_1_, bf16[512,512]{1,0:T(8,128)(2,1)S(1)} %get-tuple-element.59.refs_2_, ...), custom_call_target="tpu_custom_call" | custom-call | flops 528482304 | bytes 10524672 | tf_op jit(solution)/shard_map/attend/pallas_call | solution.py:44
  26.5 1.7 %collective-permute-start.12 = (bf16[128,768]{1,0:T(8,128)(2,1)S(1)}, bf16[128,768]{1,0:T(8,128)(2,1)S(1)}, u32[]{:S(2)}, u32[]{:S(2)}) collective-permute-start(bf16[128,768]{1,0:T(8,128)(2,1)S(1)} %get-tuple-element.76.refs_0_), channel_id=1, source_target_pairs={{0,1},{1,0},{2,3},{3,2},{4,5},{5,4},{6,7},{7,6},{8,9},{9,8},{10,11... | collective-permute-start | bytes 589832 | tf_op jit(solution)/shard_map/ppermute | solution.py:23
  28.2 0.3 second_share.1.refs_0_
  28.5 0.5 %collective-permute-start.11 = (bf16[128,768]{1,0:T(8,128)(2,1)S(1)}, bf16[128,768]{1,0:T(8,128)(2,1)S(1)}, u32[]{:S(2)}, u32[]{:S(2)}) collective-permute-start(bf16[128,768]{1,0:T(8,128)(2,1)S(1)} %second_share.1.refs_0_), channel_id=1, source_target_pairs={{0,1},{1,0},{2,3},{3,2},{4,5},{5,4},{6,7},{7,6},{8,9},{9,8},{10,11... | collective-permute-start | bytes 589832 | tf_op jit(solution)/shard_map/ppermute | solution.py:23
  29.0 0.6 %copy.13 = bf16[1536,2,768]{2,0,1:T(8,128)(2,1)S(1)} copy(bf16[1536,2,768]{2,1,0:T(2,128)(2,1)S(1)} %bitcast.10) | data formatting | bytes 9437184 | tf_op jit(solution)/shard_map/optimization_barrier | solution.py:478
  29.6 4.7 %collective-permute-done.12.refs_1_ = bf16[128,768]{1,0:T(8,128)(2,1)S(1)} collective-permute-done((bf16[128,768]{1,0:T(8,128)(2,1)S(1)}, bf16[128,768]{1,0:T(8,128)(2,1)S(1)}, u32[]{:S(2)}, u32[]{:S(2)}) %collective-permute-start.12) | collective-permute-done | bytes 196640 | tf_op jit(solution)/shard_map/ppermute | solution.py:23
  34.3 0.5 %first_tracks.1 = (f32[128,1]{1,0:T(8,128)S(1)}, f32[128,768]{1,0:T(8,128)S(1)}, f32[128,768]{1,0:T(8,128)S(1)}) custom-call(bf16[128,768]{1,0:T(8,128)(2,1)S(1)} %get-tuple-element.76.refs_0_, bf16[128,768]{1,0:T(8,128)(2,1)S(1)} %collective-permute-done.12.refs_1_, bf16[128,1536]{1,0:T(8,128)(2,1)S(1)} %get-tuple-element.73.refs_2_, ...), custom_call_target="tpu_custom_call" | custom-call | flops 301989888 | bytes 6363136 | tf_op jit(solution)/shard_map/first_tracks/pallas_call | solution.py:44
  34.8 2.9 %collective-permute-done.11.refs_1_ = bf16[128,768]{1,0:T(8,128)(2,1)S(1)} collective-permute-done((bf16[128,768]{1,0:T(8,128)(2,1)S(1)}, bf16[128,768]{1,0:T(8,128)(2,1)S(1)}, u32[]{:S(2)}, u32[]{:S(2)}) %collective-permute-start.11) | collective-permute-done | bytes 196640 | tf_op jit(solution)/shard_map/ppermute | solution.py:23
  37.7 0.5 %sent_tracks.1 = (bf16[128,768]{1,0:T(8,128)(2,1)S(1)}, bf16[128,768]{1,0:T(8,128)(2,1)S(1)}, f32[128,1]{1,0:T(8,128)S(1)}) custom-call(bf16[128,768]{1,0:T(8,128)(2,1)S(1)} %second_share.1.refs_0_, bf16[128,768]{1,0:T(8,128)(2,1)S(1)} %collective-permute-done.11.refs_1_, bf16[128,1536]{1,0:T(8,128)(2,1)S(1)} %get-tuple-element.73.refs_2_, ...), custom_call_target="tpu_custom_call" | custom-call | flops 150994944 | bytes 6428672 | tf_op jit(solution)/shard_map/sent_tracks/pallas_call | solution.py:44
  38.2 0.1 collective-permute-start.13
  38.3 0.1 copy-done.1
  38.4 0.5 %kept_tracks.1.kept = bf16[128,768]{1,0:T(8,128)(2,1)S(1)} custom-call(bf16[128,768]{1,0:T(8,128)(2,1)S(1)} %get-tuple-element.79.gained, bf16[2,1536,768]{2,1,0:T(8,128)(2,1)S(1)} %bitcast.8, f32[128,768]{1,0:T(8,128)S(1)} %get-tuple-element.80.to_keep, f32[128,1]{1,0:T(8,128)S(1)} %get-tuple-element.81.scale), custom_call_target="tpu_custom_call" | custom-call | flops 150994944 | bytes 5570560 | tf_op jit(solution)/shard_map/kept_tracks/pallas_call | solution.py:44
  38.9 0.9 %collective-permute-done.13.received = bf16[128,768]{1,0:T(8,128)(2,1)S(1)} collective-permute-done((bf16[128,768]{1,0:T(8,128)(2,1)S(1)}, bf16[128,768]{1,0:T(8,128)(2,1)S(1)}, u32[]{:S(2)}, u32[]{:S(2)}) %collective-permute-start.13) | collective-permute-done | bytes 196640 | tf_op jit(solution)/shard_map/ppermute | solution.py:23
  39.7 1.0 %average.1 = f32[128,768]{1,0:T(8,128)} custom-call(bf16[128,768]{1,0:T(8,128)(2,1)S(1)} %kept_tracks.1.kept, bf16[128,768]{1,0:T(8,128)(2,1)S(1)} %collective-permute-done.13.received, s32[1,768]{1,0:T(1,128)S(1)} %reshape.7.pairs), custom_call_target="tpu_custom_call" | custom-call | bytes 789504 | tf_op jit(solution)/shard_map/average/pallas_call | solution.py:44
  (17 shorter events, 0.0 us)
Async XLA Ops:
  1.1 7.2 %collective-permute-start.2 = (bf16[160,384]{1,0:T(8,128)(2,1)S(1)}, bf16[160,384]{1,0:T(8,128)(2,1)S(1)}, u32[]{:S(2)}, u32[]{:S(2)}) collective-permute-start(bf16[160,384]{1,0:T(8,128)(2,1)S(1)} %get-tuple-element.45), channel_id=1, source_target_pairs={{0,1},{1,0},{2,3},{3,2},{4,5},{5,4},{6,7},{7,6},{8,9},{9,8},{10,11... | collective-permute-start | bytes 368648 | tf_op jit(solution)/shard_map/ppermute | solution.py:23
  4.1 13.8 %collective-permute-start.9 = (bf16[256,384]{1,0:T(8,128)(2,1)S(1)}, bf16[256,384]{1,0:T(8,128)(2,1)S(1)}, u32[]{:S(2)}, u32[]{:S(2)}) collective-permute-start(bf16[256,384]{1,0:T(8,128)(2,1)S(1)} %get-tuple-element.61), channel_id=1, source_target_pairs={{0,1},{1,0},{2,3},{3,2},{4,5},{5,4},{6,7},{7,6},{8,9},{9,8},{10,11... | collective-permute-start | bytes 589832 | tf_op jit(solution)/shard_map/ppermute | solution.py:23
  4.2 15.9 %collective-permute-start = (bf16[256,384]{1,0:T(8,128)(2,1)S(1)}, bf16[256,384]{1,0:T(8,128)(2,1)S(1)}, u32[]{:S(2)}, u32[]{:S(2)}) collective-permute-start(bf16[256,384]{1,0:T(8,128)(2,1)S(1)} %get-tuple-element.44), channel_id=1, source_target_pairs={{0,1},{1,0},{2,3},{3,2},{4,5},{5,4},{6,7},{7,6},{8,9},{9,8},{10,11... | collective-permute-start | bytes 589832 | tf_op jit(solution)/shard_map/ppermute | solution.py:23
  8.3 11.8 %collective-permute-start.3 = (bf16[160,384]{1,0:T(8,128)(2,1)S(1)}, bf16[160,384]{1,0:T(8,128)(2,1)S(1)}, u32[]{:S(2)}, u32[]{:S(2)}) collective-permute-start(bf16[160,384]{1,0:T(8,128)(2,1)S(1)} %collective-permute-done.2.refs_7_), channel_id=1, source_target_pairs={{0,16},{16,0},{1,17},{17,1},{2,18},{18,2},{3,19},{19,3},{4,20},{20... | collective-permute-start | bytes 368648 | tf_op jit(solution)/shard_map/ppermute | solution.py:23
  10.4 5.8 %collective-permute-start.4 = (bf16[128,128]{1,0:T(8,128)(2,1)S(1)}, bf16[128,128]{1,0:T(8,128)(2,1)S(1)}, u32[]{:S(2)}, u32[]{:S(2)}) collective-permute-start(bf16[128,128]{1,0:T(8,128)(2,1)S(1)} %get-tuple-element.49.refs_0_), channel_id=1, source_target_pairs={{0,4},{4,8},{8,12},{12,0},{1,5},{5,9},{9,13},{13,1},{2,6},{6,10},{... | collective-permute-start | bytes 98312 | tf_op jit(solution)/shard_map/ppermute | solution.py:23
  11.9 5.9 %collective-permute-start.5 = (bf16[128,128]{1,0:T(8,128)(2,1)S(1)}, bf16[128,128]{1,0:T(8,128)(2,1)S(1)}, u32[]{:S(2)}, u32[]{:S(2)}) collective-permute-start(bf16[128,128]{1,0:T(8,128)(2,1)S(1)} %get-tuple-element.49.refs_0_), channel_id=1, source_target_pairs={{0,8},{4,12},{8,0},{12,4},{1,9},{5,13},{9,1},{13,5},{2,10},{6,14},... | collective-permute-start | bytes 98312 | tf_op jit(solution)/shard_map/ppermute | solution.py:23
  16.2 3.9 %collective-permute-start.6 = (bf16[128,128]{1,0:T(8,128)(2,1)S(1)}, bf16[128,128]{1,0:T(8,128)(2,1)S(1)}, u32[]{:S(2)}, u32[]{:S(2)}) collective-permute-start(bf16[128,128]{1,0:T(8,128)(2,1)S(1)} %get-tuple-element.49.refs_0_), channel_id=1, source_target_pairs={{0,12},{4,0},{8,4},{12,8},{1,13},{5,1},{9,5},{13,9},{2,14},{6,2},{... | collective-permute-start | bytes 98312 | tf_op jit(solution)/shard_map/ppermute | solution.py:23
  17.9 4.8 %collective-permute-start.10 = (bf16[256,384]{1,0:T(8,128)(2,1)S(1)}, bf16[256,384]{1,0:T(8,128)(2,1)S(1)}, u32[]{:S(2)}, u32[]{:S(2)}) collective-permute-start(bf16[256,384]{1,0:T(8,128)(2,1)S(1)} %collective-permute-done.9.refs_0_), channel_id=1, source_target_pairs={{0,2},{2,0},{1,3},{3,1},{4,6},{6,4},{5,7},{7,5},{8,10},{10,8},{9,1... | collective-permute-start | bytes 589832 | tf_op jit(solution)/shard_map/ppermute | solution.py:23
  17.9 2.7 %collective-permute-start.7 = (bf16[160,384]{1,0:T(8,128)(2,1)S(1)}, bf16[160,384]{1,0:T(8,128)(2,1)S(1)}, u32[]{:S(2)}, u32[]{:S(2)}) collective-permute-start(bf16[160,384]{1,0:T(8,128)(2,1)S(1)} %collective-permute-done.2.refs_7_), channel_id=1, source_target_pairs={{0,2},{2,0},{1,3},{3,1},{4,6},{6,4},{5,7},{7,5},{8,10},{10,8},{9,1... | collective-permute-start | bytes 368648 | tf_op jit(solution)/shard_map/ppermute | solution.py:23
  20.1 1.3 %collective-permute-start.8 = (bf16[160,384]{1,0:T(8,128)(2,1)S(1)}, bf16[160,384]{1,0:T(8,128)(2,1)S(1)}, u32[]{:S(2)}, u32[]{:S(2)}) collective-permute-start(bf16[160,384]{1,0:T(8,128)(2,1)S(1)} %collective-permute-done.3.refs_9_), channel_id=1, source_target_pairs={{0,2},{2,0},{1,3},{3,1},{4,6},{6,4},{5,7},{7,5},{8,10},{10,8},{9,1... | collective-permute-start | bytes 368648 | tf_op jit(solution)/shard_map/ppermute | solution.py:23
  20.1 3.4 %collective-permute-start.1 = (bf16[256,384]{1,0:T(8,128)(2,1)S(1)}, bf16[256,384]{1,0:T(8,128)(2,1)S(1)}, u32[]{:S(2)}, u32[]{:S(2)}) collective-permute-start(bf16[256,384]{1,0:T(8,128)(2,1)S(1)} %collective-permute-done.refs_0_), channel_id=1, source_target_pairs={{0,2},{2,0},{1,3},{3,1},{4,6},{6,4},{5,7},{7,5},{8,10},{10,8},{9,1... | collective-permute-start | bytes 589832 | tf_op jit(solution)/shard_map/ppermute | solution.py:23
  22.7 1.7 %copy-start = (bf16[768,1536]{1,0:T(8,128)(2,1)S(1)}, bf16[768,1536]{1,0:T(8,128)(2,1)}, u32[]{:S(2)}) copy-start(bf16[768,1536]{1,0:T(8,128)(2,1)} %w_out.1) | copy-start | bytes 7077892
  23.5 5.5 %slice-start = ((s8[4718592]{0:T(1024)(128)(4,1)}), s8[4194304]{0:T(1024)(128)(4,1)S(1)}, s32[]{:S(2)}) async-start(s8[4718592]{0:T(1024)(128)(4,1)} %bitcast.9), calls=%async_computation | async-start | bytes 8388608
  24.4 4.6 %slice-start.1 = ((s8[4718592]{0:T(1024)(128)(4,1)}), s8[524288]{0:T(1024)(128)(4,1)S(1)}, s32[]{:S(2)}) async-start(s8[4718592]{0:T(1024)(128)(4,1)} %bitcast.9), calls=%async_computation.1 | async-start | bytes 1048576
  26.5 7.8 %collective-permute-start.12 = (bf16[128,768]{1,0:T(8,128)(2,1)S(1)}, bf16[128,768]{1,0:T(8,128)(2,1)S(1)}, u32[]{:S(2)}, u32[]{:S(2)}) collective-permute-start(bf16[128,768]{1,0:T(8,128)(2,1)S(1)} %get-tuple-element.76.refs_0_), channel_id=1, source_target_pairs={{0,1},{1,0},{2,3},{3,2},{4,5},{5,4},{6,7},{7,6},{8,9},{9,8},{10,11... | collective-permute-start | bytes 589832 | tf_op jit(solution)/shard_map/ppermute | solution.py:23
  28.5 9.2 %collective-permute-start.11 = (bf16[128,768]{1,0:T(8,128)(2,1)S(1)}, bf16[128,768]{1,0:T(8,128)(2,1)S(1)}, u32[]{:S(2)}, u32[]{:S(2)}) collective-permute-start(bf16[128,768]{1,0:T(8,128)(2,1)S(1)} %second_share.1.refs_0_), channel_id=1, source_target_pairs={{0,1},{1,0},{2,3},{3,2},{4,5},{5,4},{6,7},{7,6},{8,9},{9,8},{10,11... | collective-permute-start | bytes 589832 | tf_op jit(solution)/shard_map/ppermute | solution.py:23
  37.7 0.7 %copy-start.1 = (s32[768]{0:T(1024)S(1)}, s32[768]{0:T(1024)}, u32[]{:S(2)}) copy-start(s32[768]{0:T(1024)} %param.19) | copy-start | bytes 9220
  38.2 1.5 %collective-permute-start.13 = (bf16[128,768]{1,0:T(8,128)(2,1)S(1)}, bf16[128,768]{1,0:T(8,128)(2,1)S(1)}, u32[]{:S(2)}, u32[]{:S(2)}) collective-permute-start(bf16[128,768]{1,0:T(8,128)(2,1)S(1)} %get-tuple-element.82), channel_id=1, source_target_pairs={{0,2},{2,0},{1,3},{3,1},{4,6},{6,4},{5,7},{7,5},{8,10},{10,8},{9,1... | collective-permute-start | bytes 589832 | tf_op jit(solution)/shard_map/ppermute | solution.py:23

commit v4 on v3

--- a/solution.py
+++ b/solution.py
@@ -71,8 +71,9 @@
         lax.fori_loop(0, total // block, one, 0)
 
 
-def stage_kernel(chunks, embed, key_t, value_t, *refs):
-    part_kv, pieces, sems = refs[0], refs[1 : 1 + chunks], refs[1 + chunks]
+def stage_kernel(chunks, embed, key_t, value_t, codes, *refs):
+    part_kv, pieces = refs[0], refs[1 : 1 + chunks]
+    codes_out, raw_codes, sems = refs[1 + chunks :]
     strand = lax.axis_index("strand")
     part = strand * lax.axis_size("groups") + lax.axis_index("groups")
     key_cols, value_cols = key_t.shape[0], value_t.shape[0]
@@ -87,18 +88,21 @@
     for i in range(chunks):
         source = embed.at[rows, pl.ds(i * width, width)]
         copies.append(pltpu.make_async_copy(source, pieces[i], sems.at[2 + i]))
+    copies.append(pltpu.make_async_copy(codes, raw_codes, sems.at[2 + chunks]))
     for copy in copies:
         copy.start()
-    for copy in copies:
+    copies[-1].wait()
+    codes_out[...] = raw_codes[...].astype(F32).astype(BF16)
+    for copy in copies[:-1]:
         copy.wait()
 
 
-def prepare_kernel(embed, key_t, value_t, w_query, gain, last_gain, codes, *refs):
-    table, key_out, value_out, query_out, gain_out, last_out, cosine, sine, codes_out = refs[:9]
-    raw_gain, raw_last, raw_codes, sems = refs[9:]
+def prepare_kernel(rows, embed, key_t, value_t, w_query, gain, last_gain, *refs):
+    table, key_out, value_out, query_out, gain_out, last_out, cosine, sine = refs[:8]
+    raw_gain, raw_last, sems = refs[8:]
     strand, pos = lax.axis_index("strand"), lax.axis_index("pos")
     half = embed.shape[0] // 2
-    pairs = [(codes, raw_codes), (gain, raw_gain), (last_gain, raw_last)]
+    pairs = [(gain, raw_gain), (last_gain, raw_last)]
     for i in range(2):
         part = strand if i == 0 else 1 - strand
         source = embed.at[pl.ds(pl.multiple_of(part * half, half), half)]
@@ -108,15 +112,13 @@
     for copy in copies:
         copy.start()
     total = cosine.shape[0]
-    rows = codes.shape[0]
     blocks = total // rows
     lane = lax.broadcasted_iota(jnp.int32, (1, KDIM), 1)
     inverse = jnp.exp((lane % (KDIM // 2)).astype(F32) * (-math.log(10000.0) / (KDIM // 2)))
     sign = jnp.where(lane < KDIM // 2, -1.0, 1.0)
     offset = lax.broadcasted_iota(jnp.int32, (rows, KDIM), 0)
-    for copy in copies[:3]:
+    for copy in copies[:2]:
         copy.wait()
-    codes_out[...] = raw_codes[...].astype(F32).astype(BF16)
     gain_out[...] = raw_gain[...].reshape(gain_out.shape)
     last_out[...] = raw_last[...].reshape(last_out.shape)
 
@@ -131,7 +133,19 @@
             step(i * rows)
     else:
         over_blocks(total, rows, step)
-    for copy in copies[3:]:
+    for copy in copies[2:]:
+        copy.wait()
+
+
+def fetch_kernel(w_out, first_out, second_out, sems):
+    out_half = first_out.shape[1]
+    copies = [
+        pltpu.make_async_copy(w_out.at[:, pl.ds(0, out_half)], first_out, sems.at[0]),
+        pltpu.make_async_copy(w_out.at[:, pl.ds(out_half, out_half)], second_out, sems.at[1]),
+    ]
+    for copy in copies:
+        copy.start()
+    for copy in copies:
         copy.wait()
 
 
@@ -166,7 +180,8 @@
     return found
 
 
-def own_kernel(blocks, kv_steps, *refs):
+def own_kernel(code_steps, kv_steps, *refs):
+    blocks = len(code_steps)
     codes = refs[:blocks]
     table, key_t, value_t = refs[blocks : blocks + 3]
     parts = refs[blocks + 3 : blocks + 3 + len(kv_steps)]
@@ -178,8 +193,9 @@
     half = entries // 2
     rows = codes[0].shape[0]
     total = blocks * rows
-    for i in range(blocks):
-        all_codes[i * rows : (i + 1) * rows, :] = codes[i][...]
+    for piece, (forward, reverse) in zip(codes, code_steps):
+        spot = jnp.where(strand == 0, forward, reverse) * rows
+        all_codes[pl.ds(pl.multiple_of(spot, rows), rows), :] = piece[...]
 
     def kv_rows(owner):
         key_rows = pl.ds(pl.multiple_of(owner * key_cols, 16), key_cols)
@@ -246,9 +262,10 @@
 
 def attend_kernel(steps, chunks, *refs):
     mine, theirs, onehot, kv_t, w_query, gain, square, kv_sum, q_sum = refs[:9]
-    own, cosine, sine, w_out = refs[9:13]
+    own, cosine, sine, first_out = refs[9:13]
     founds = refs[13 : 13 + len(steps) - 1]
-    share, merged, inputs, table, squares, sums, queries, keys, values = refs[12 + len(steps) :]
+    share, merged, inputs = refs[12 + len(steps) : 15 + len(steps)]
+    table, squares, sums, queries, keys, values = refs[15 + len(steps) :]
     half, width = mine.shape
     rows, own_width = own.shape
     features = inputs.shape[1]
@@ -281,12 +298,11 @@
         weight_sum = jnp.sum(weights, axis=1, keepdims=True)
         found = (matmul(weights.astype(BF16), values[...]) / weight_sum).astype(BF16)
         merged[:, head * VDIM : (head + 1) * VDIM] = found
-    share[...] = matmul(merged[...], w_out[:, : w_out.shape[1] // 2]).astype(BF16)
-
-
-def second_kernel(merged, w_out, share):
-    half = w_out.shape[1] // 2
-    share[...] = matmul(merged[...], w_out[:, half:]).astype(BF16)
+    share[...] = matmul(merged[...], first_out[...]).astype(BF16)
+
+
+def second_kernel(merged, second_out, share):
+    share[...] = matmul(merged[...], second_out[...]).astype(BF16)
 
 
 def gather_hidden(shares, inputs, gain, chunk):
@@ -374,16 +390,18 @@
     wide = width // chunks
 
     hbm = pltpu.HBM
-    part_kv, *own_pieces = call(
+    part_kv, *own_pieces, own_codes = call(
         functools.partial(stage_kernel, chunks),
-        [shape((kv_cols, features // (2 * groups)), BF16)] + [shape((half, wide), BF16)] * chunks,
-        [embed_table, key_t, value_t],
+        [shape((kv_cols, features // (2 * groups)), BF16)]
+        + [shape((half, wide), BF16)] * chunks
+        + [shape((rows, BIN), BF16)],
+        [embed_table, key_t, value_t, base_codes.reshape(rows, BIN)],
         "stage",
-        scratch=[pltpu.SemaphoreType.DMA((2 + chunks,))],
-        spaces=[hbm] * 3,
-    )
-    table, key_own, value_own, query_own, gain, last_gain, cosine, sine, own_codes = call(
-        prepare_kernel,
+        scratch=[pltpu.VMEM((rows, BIN), jnp.int32), pltpu.SemaphoreType.DMA((3 + chunks,))],
+        spaces=[hbm] * 4,
+    )
+    table, key_own, value_own, query_own, gain, last_gain, cosine, sine = call(
+        functools.partial(prepare_kernel, rows),
         [
             shape((entries, width), BF16),
             shape(key_t.shape, BF16),
@@ -393,29 +411,50 @@
             shape((1, features), F32),
             shape((total, KDIM), F32),
             shape((total, KDIM), F32),
-            shape((rows, BIN), BF16),
         ],
-        [embed_table, key_t, value_t, w_query, attn_gain, head_gain, base_codes.reshape(rows, BIN)],
+        [embed_table, key_t, value_t, w_query, attn_gain, head_gain],
         "prepare",
         scratch=[
             pltpu.VMEM((features,), F32),
             pltpu.VMEM((features,), F32),
-            pltpu.VMEM((rows, BIN), jnp.int32),
-            pltpu.SemaphoreType.DMA((8,)),
+            pltpu.SemaphoreType.DMA((7,)),
         ],
-        spaces=[hbm] * 7,
+        spaces=[hbm] * 6,
     )
     kv_parts, kv_steps, pieces, steps = [], [], [], []
     from_heads = [shifted(part_kv, "heads", step) for step in range(1, size)]
     if from_heads:
-        from_heads[0], own_codes = lax.optimization_barrier((from_heads[0], own_codes))
-    codes = [own_codes] + [shifted(own_codes, "pos", k) for k in range(1, blocks)]
+        from_heads[0], table = lax.optimization_barrier((from_heads[0], table))
+    to_core = [shifted(here, "strand", 1) for here in from_heads]
+    out_in = w_out
+    if to_core:
+        out_in = w_out
+    first_out, second_out = call(
+        fetch_kernel,
+        [shape((w_out.shape[0], features // 2), BF16)] * 2,
+        [out_in],
+        "fetch_out",
+        scratch=[pltpu.SemaphoreType.DMA((2,))],
+        spaces=[hbm],
+    )
+    raw, raw_steps = [], []
+    for k in range(1, blocks, 2):
+        if k + 1 < blocks:
+            pairs = [((p, s), ((p + k + s) % blocks, s)) for p in range(blocks) for s in range(2)]
+            pairs = [(2 * p + s, 2 * q + t) for (p, s), (q, t) in pairs]
+            raw.append(lax.ppermute(own_codes, ("pos", "strand"), pairs))
+            raw_steps.append((k, k + 1))
+        else:
+            raw.append(shifted(own_codes, "pos", k))
+            raw_steps.append((k, k))
+    if raw:
+        raw[0], first_out = lax.optimization_barrier((raw[0], first_out))
     for step in range(1, size):
         for k in range(groups):
             here = from_heads[step - 1] if k == 0 else shifted(from_heads[step - 1], "groups", k)
-            if step == 1 and k == groups - 1:
-                here, *codes = lax.optimization_barrier((here, *codes))
-            kv_parts += [here, shifted(here, "strand", 1)]
+            if step == 1 and k == groups - 1 and blocks > 1:
+                here, *raw = lax.optimization_barrier((here, *raw))
+            kv_parts += [here, to_core[step - 1] if k == 0 else shifted(here, "strand", 1)]
             kv_steps += [(step, k, 0), (step, k, 1)]
     for step in range(1, size):
         for i in range(chunks):
@@ -423,9 +462,16 @@
             pieces.append((here, shifted(here, "strand", 1)))
             steps.append((step, i))
 
+    codes, code_steps = [own_codes], [(0, 0)]
+    for here, (mine, other) in zip(raw, raw_steps):
+        codes.append(here)
+        code_steps.append((mine, other))
+        if mine != other:
+            codes.append(shifted(here, "strand", 1))
+            code_steps.append((other, mine))
     sums = [shape((total, 1), F32), shape((total, kv_all), F32), shape((rows, q_cols), F32)]
     onehot, kv_t, own, *state = call(
-        functools.partial(own_kernel, blocks, kv_steps),
+        functools.partial(own_kernel, code_steps, kv_steps),
         [shape((total, entries), BF16), shape((kv_all, features), BF16), shape((rows, width), BF16)] + sums,
         codes + [table, key_own, value_own] + kv_parts + [query_own, gain],
         "own_features",
@@ -453,7 +499,7 @@
             shape((rows, o_cols), BF16),
             shape((rows, features), BF16),
         ],
-        list(pieces[-1]) + [onehot, kv_t, query_own, gain] + state + [own, cosine, sine, w_out] + founds,
+        list(pieces[-1]) + [onehot, kv_t, query_own, gain] + state + [own, cosine, sine, first_out] + founds,
         "attend",
         scratch=[
             pltpu.VMEM((entries, wide), BF16),
@@ -469,7 +515,7 @@
     (share_two,) = call(
         second_kernel,
         [shape((rows, features // 2), BF16)],
-        [merged, w_out],
+        [merged, second_out],
         "second_share",
         flops=rows * o_cols * features,
     )

time: 41 us -> 37 us (0.902)
  waiting for transfers between devices: 12.9 us -> 10.1 us
  starting transfers between devices: 16.2 us -> 14.2 us
  Pallas kernels: 9.95 us -> 11.6 us
  local copies, waits for them, and re-layouts: 1.6 us -> 0.73 us
    ppermute x14 -> x13, starting transfers between devices: 16.2 us -> 12.6 us  [shifted(): lax.ppermute(value, axis, [(i, (i + distance) % size) for i in range(size)])]
    ppermute x14 -> x13, waiting for transfers between devices: 12.9 us -> 9.79 us  [shifted(): lax.ppermute(value, axis, [(i, (i + distance) % size) for i in range(size)])]
    pallas_call x10 -> x11, Pallas kernels: 9.95 us -> 11.6 us  [call(): pl.pallas_call(kernel, out_shape=list(outs), in_specs=specs, out_specs=[v...]
    ppermute x0 -> x1, starting transfers between devices: none -> 1.58 us  [body(): raw.append(lax.ppermute(own_codes, ('pos', 'strand'), pairs))]
    unnamed x8 -> x6, local copies, waits for them, and re-layouts: 1 us -> 0.13 us
  transfers between devices with their start and end apart: 14 -> 14, of which waited for: 7 -> 7; matrix products, arithmetic and copies ran while one was open for 1% -> 2% of each run, Pallas kernels for 13% -> 19%
where the time goes in v4:
time: 37 us; the launch traced here: 36.8 us
  starting transfers between devices  14.2 us (38%)
  Pallas kernels  11.6 us (31%)
  waiting for transfers between devices  10.1 us (27%)
  local copies, waits for them, and re-layouts  0.73 us (2%)
    ppermute x13, starting transfers between devices, shifted(): lax.ppermute(value, axis, [(i, (i + distance) % size) for i in range(size)])  12.6 us
    pallas_call x11, Pallas kernels, call(): pl.pallas_call(kernel, out_shape=list(outs), in_specs=specs, out_specs=[v...  11.6 us
    ppermute x13, waiting for transfers between devices, shifted(): lax.ppermute(value, axis, [(i, (i + distance) % size) for i in range(size)])  9.79 us
    ppermute x1, starting transfers between devices, body(): raw.append(lax.ppermute(own_codes, ('pos', 'strand'), pairs))  1.58 us
  transfers between devices with their start and end apart: 14, of which 7 were waited for; matrix products, arithmetic and copies ran while one was open for 2% of the time, Pallas kernels for 19%

profile of v4, /device:TPU:0, one launch (start us, length us, event | category | flops | bytes accessed | tf_op | source)
XLA Modules:
  0.0 36.8 jit_solution(4819058296365936602)
XLA Ops:
  0.0 1.1 %stage.1 = (bf16[160,384]{1,0:T(8,128)(2,1)S(1)}, bf16[256,384]{1,0:T(8,128)(2,1)S(1)}, bf16[256,384]{1,0:T(8,128)(2,1)S(1)}, bf16[128,128]{1,0:T(8,128)(2,1)S(1)}) custom-call(bf16[512,768]{1,0:T(8,128)(2,1)} %embed.3, bf16[64,1536]{1,0:T(8,128)(2,1)} %bitcast.13, bf16[96,1536]{1,0:T(8,128)(2,1)} %bitcast.11, s32[128,128]{1,0:T(8,128)} %bitcast.15), custom_call_target="tpu_custom_call" | custom-call | bytes 614400 | tf_op jit(solution)/shard_map/stage/pallas_call | solution.py:44
  1.2 3.0 %collective-permute-start.2 = (bf16[160,384]{1,0:T(8,128)(2,1)S(1)}, bf16[160,384]{1,0:T(8,128)(2,1)S(1)}, u32[]{:S(2)}, u32[]{:S(2)}) collective-permute-start(bf16[160,384]{1,0:T(8,128)(2,1)S(1)} %get-tuple-element.48), channel_id=1, source_target_pairs={{0,1},{1,0},{2,3},{3,2},{4,5},{5,4},{6,7},{7,6},{8,9},{9,8},{10,11... | collective-permute-start | bytes 368648 | tf_op jit(solution)/shard_map/ppermute | solution.py:23
  4.2 0.1 collective-permute-start.9
  4.2 1.9 %collective-permute-start = (bf16[256,384]{1,0:T(8,128)(2,1)S(1)}, bf16[256,384]{1,0:T(8,128)(2,1)S(1)}, u32[]{:S(2)}, u32[]{:S(2)}) collective-permute-start(bf16[256,384]{1,0:T(8,128)(2,1)S(1)} %get-tuple-element.46), channel_id=1, source_target_pairs={{0,1},{1,0},{2,3},{3,2},{4,5},{5,4},{6,7},{7,6},{8,9},{9,8},{10,11... | collective-permute-start | bytes 589832 | tf_op jit(solution)/shard_map/ppermute | solution.py:23
  6.2 1.9 %prepare.1 = (bf16[512,768]{1,0:T(8,128)(2,1)S(1)}, bf16[64,1536]{1,0:T(8,128)(2,1)S(1)}, bf16[96,1536]{1,0:T(8,128)(2,1)S(1)}, bf16[1536,512]{1,0:T(8,128)(2,1)...) custom-call(bf16[512,768]{1,0:T(8,128)(2,1)} %embed.3, ...), custom_call_target="tpu_custom_call" | custom-call | bytes 3399680 | tf_op jit(solution)/shard_map/prepare/pallas_call | solution.py:44
  8.1 0.2 collective-permute-done.2.refs_7_
  8.3 2.1 %collective-permute-start.3 = (bf16[160,384]{1,0:T(8,128)(2,1)S(1)}, bf16[160,384]{1,0:T(8,128)(2,1)S(1)}, u32[]{:S(2)}, u32[]{:S(2)}) collective-permute-start(bf16[160,384]{1,0:T(8,128)(2,1)S(1)} %collective-permute-done.2.refs_7_), channel_id=1, source_target_pairs={{0,16},{16,0},{1,17},{17,1},{2,18},{18,2},{3,19},{19,3},{4,20},{20... | collective-permute-start | bytes 368648 | tf_op jit(solution)/shard_map/ppermute | solution.py:23
  10.4 1.6 %collective-permute-start.4 = (bf16[128,128]{1,0:T(8,128)(2,1)S(1)}, bf16[128,128]{1,0:T(8,128)(2,1)S(1)}, u32[]{:S(2)}, u32[]{:S(2)}) collective-permute-start(bf16[128,128]{1,0:T(8,128)(2,1)S(1)} %get-tuple-element.47.refs_0_), channel_id=1, source_target_pairs={{0,4},{2,10},{4,8},{6,14},{8,12},{10,2},{12,0},{14,6},{1,5},{3,11}... | collective-permute-start | bytes 98312 | tf_op jit(solution)/shard_map/ppermute | solution.py:445
  12.0 2.2 %collective-permute-start.5 = (bf16[128,128]{1,0:T(8,128)(2,1)S(1)}, bf16[128,128]{1,0:T(8,128)(2,1)S(1)}, u32[]{:S(2)}, u32[]{:S(2)}) collective-permute-start(bf16[128,128]{1,0:T(8,128)(2,1)S(1)} %get-tuple-element.47.refs_0_), channel_id=1, source_target_pairs={{0,12},{4,0},{8,4},{12,8},{1,13},{5,1},{9,5},{13,9},{2,14},{6,2},{... | collective-permute-start | bytes 98312 | tf_op jit(solution)/shard_map/ppermute | solution.py:23
  14.2 1.6 %fetch_out.1 = (bf16[768,768]{1,0:T(8,128)(2,1)S(1)}, bf16[768,768]{1,0:T(8,128)(2,1)S(1)}) custom-call(bf16[768,1536]{1,0:T(8,128)(2,1)} %w_out.1), custom_call_target="tpu_custom_call" | custom-call | bytes 2359296 | tf_op jit(solution)/shard_map/fetch_out/pallas_call | solution.py:44
  15.9 0.3 collective-permute-done.4.refs_1_
  16.2 0.2 collective-permute-start.7
  16.5 0.3 collective-permute-start.8
  16.7 0.2 collective-permute-start.1
  17.0 0.3 collective-permute-start.6
  17.3 0.3 collective-permute-done.7.refs_8_
  17.6 0.7 %collective-permute-done.6.refs_2_ = bf16[128,128]{1,0:T(8,128)(2,1)S(1)} collective-permute-done((bf16[128,128]{1,0:T(8,128)(2,1)S(1)}, bf16[128,128]{1,0:T(8,128)(2,1)S(1)}, u32[]{:S(2)}, u32[]{:S(2)}) %collective-permute-start.6) | collective-permute-done | bytes 32800 | tf_op jit(solution)/shard_map/ppermute | solution.py:23
  18.2 1.3 %own_features.1 = (bf16[512,512]{1,0:T(8,128)(2,1)S(1)}, bf16[320,1536]{1,0:T(8,128)(2,1)S(1)}, bf16[128,768]{1,0:T(8,128)(2,1)S(1)}, f32[512,1]{1,0:T(8,128)S(1...) custom-call(bf16[128,128]{1,0:T(8,128)(2,1)S(1)} %get-tuple-element.47.refs_0_, ...), custom_call_target="tpu_custom_call" | custom-call | flops 654311424 | bytes 6494208 | tf_op jit(solution)/shard_map/own_features/pallas_call | solution.py:44
  19.5 0.8 %other_features.1 = (bf16[128,384]{1,0:T(8,128)(2,1)S(1)}, f32[512,1]{1,0:T(8,128)S(1)}, f32[512,320]{1,0:T(8,128)S(1)}, f32[128,512]{1,0:T(8,128)S(1)}) custom-call(bf16[256,384]{1,0:T(8,128)(2,1)S(1)} %collective-permute-done.9.refs_0_, bf16[256,384]{1,0:T(8,128)(2,1)S(1)} %collective-permute-done.10.refs_1_, ...), custom_call_target="tpu_custom_call" | custom-call | flops 327155712 | bytes 6330368 | tf_op jit(solution)/shard_map/other_features/pallas_call | solution.py:44
  20.3 2.1 %attend.1 = (bf16[128,768]{1,0:T(8,128)(2,1)S(1)}, bf16[128,768]{1,0:T(8,128)(2,1)S(1)}, bf16[128,1536]{1,0:T(8,128)(2,1)S(1)}) custom-call(bf16[256,384]{1,0:T(8,128)(2,1)S(1)} %collective-permute-done.refs_0_, bf16[256,384]{1,0:T(8,128)(2,1)S(1)} %collective-permute-done.1.refs_1_, bf16[512,512]{1,0:T(8,128)(2,1)S(1)} %get-tuple-element.61.refs_2_, ...), custom_call_target="tpu_custom_call" | custom-call | flops 528482304 | bytes 9345024 | tf_op jit(solution)/shard_map/attend/pallas_call | solution.py:44
  22.4 1.6 %collective-permute-start.12 = (bf16[128,768]{1,0:T(8,128)(2,1)S(1)}, bf16[128,768]{1,0:T(8,128)(2,1)S(1)}, u32[]{:S(2)}, u32[]{:S(2)}) collective-permute-start(bf16[128,768]{1,0:T(8,128)(2,1)S(1)} %get-tuple-element.80.refs_0_), channel_id=1, source_target_pairs={{0,1},{1,0},{2,3},{3,2},{4,5},{5,4},{6,7},{7,6},{8,9},{9,8},{10,11... | collective-permute-start | bytes 589832 | tf_op jit(solution)/shard_map/ppermute | solution.py:23
  24.0 0.3 second_share.1.refs_0_
  24.3 0.6 %collective-permute-start.11 = (bf16[128,768]{1,0:T(8,128)(2,1)S(1)}, bf16[128,768]{1,0:T(8,128)(2,1)S(1)}, u32[]{:S(2)}, u32[]{:S(2)}) collective-permute-start(bf16[128,768]{1,0:T(8,128)(2,1)S(1)} %second_share.1.refs_0_), channel_id=1, source_target_pairs={{0,1},{1,0},{2,3},{3,2},{4,5},{5,4},{6,7},{7,6},{8,9},{9,8},{10,11... | collective-permute-start | bytes 589832 | tf_op jit(solution)/shard_map/ppermute | solution.py:23
  24.9 0.6 %copy.13 = bf16[1536,2,768]{2,0,1:T(8,128)(2,1)S(1)} copy(bf16[1536,2,768]{2,1,0:T(2,128)(2,1)S(1)} %bitcast.10) | data formatting | bytes 9437184 | tf_op jit(solution)/shard_map/optimization_barrier | solution.py:524
  25.5 4.7 %collective-permute-done.12.refs_1_ = bf16[128,768]{1,0:T(8,128)(2,1)S(1)} collective-permute-done((bf16[128,768]{1,0:T(8,128)(2,1)S(1)}, bf16[128,768]{1,0:T(8,128)(2,1)S(1)}, u32[]{:S(2)}, u32[]{:S(2)}) %collective-permute-start.12) | collective-permute-done | bytes 196640 | tf_op jit(solution)/shard_map/ppermute | solution.py:23
  30.2 0.5 %first_tracks.1 = (f32[128,1]{1,0:T(8,128)S(1)}, f32[128,768]{1,0:T(8,128)S(1)}, f32[128,768]{1,0:T(8,128)S(1)}) custom-call(bf16[128,768]{1,0:T(8,128)(2,1)S(1)} %get-tuple-element.80.refs_0_, bf16[128,768]{1,0:T(8,128)(2,1)S(1)} %collective-permute-done.12.refs_1_, bf16[128,1536]{1,0:T(8,128)(2,1)S(1)} %get-tuple-element.77.refs_2_, ...), custom_call_target="tpu_custom_call" | custom-call | flops 301989888 | bytes 6363136 | tf_op jit(solution)/shard_map/first_tracks/pallas_call | solution.py:44
  30.7 3.0 %collective-permute-done.11.refs_1_ = bf16[128,768]{1,0:T(8,128)(2,1)S(1)} collective-permute-done((bf16[128,768]{1,0:T(8,128)(2,1)S(1)}, bf16[128,768]{1,0:T(8,128)(2,1)S(1)}, u32[]{:S(2)}, u32[]{:S(2)}) %collective-permute-start.11) | collective-permute-done | bytes 196640 | tf_op jit(solution)/shard_map/ppermute | solution.py:23
  33.8 0.5 %sent_tracks.1 = (bf16[128,768]{1,0:T(8,128)(2,1)S(1)}, bf16[128,768]{1,0:T(8,128)(2,1)S(1)}, f32[128,1]{1,0:T(8,128)S(1)}) custom-call(bf16[128,768]{1,0:T(8,128)(2,1)S(1)} %second_share.1.refs_0_, bf16[128,768]{1,0:T(8,128)(2,1)S(1)} %collective-permute-done.11.refs_1_, bf16[128,1536]{1,0:T(8,128)(2,1)S(1)} %get-tuple-element.77.refs_2_, ...), custom_call_target="tpu_custom_call" | custom-call | flops 150994944 | bytes 6428672 | tf_op jit(solution)/shard_map/sent_tracks/pallas_call | solution.py:44
  34.3 0.1 copy-done
  34.4 0.5 %kept_tracks.1.kept = bf16[128,768]{1,0:T(8,128)(2,1)S(1)} custom-call(bf16[128,768]{1,0:T(8,128)(2,1)S(1)} %get-tuple-element.83.gained, bf16[2,1536,768]{2,1,0:T(8,128)(2,1)S(1)} %bitcast.8, f32[128,768]{1,0:T(8,128)S(1)} %get-tuple-element.84.to_keep, f32[128,1]{1,0:T(8,128)S(1)} %get-tuple-element.85.scale), custom_call_target="tpu_custom_call" | custom-call | flops 150994944 | bytes 5570560 | tf_op jit(solution)/shard_map/kept_tracks/pallas_call | solution.py:44
  34.9 0.9 %collective-permute-done.13.received = bf16[128,768]{1,0:T(8,128)(2,1)S(1)} collective-permute-done((bf16[128,768]{1,0:T(8,128)(2,1)S(1)}, bf16[128,768]{1,0:T(8,128)(2,1)S(1)}, u32[]{:S(2)}, u32[]{:S(2)}) %collective-permute-start.13) | collective-permute-done | bytes 196640 | tf_op jit(solution)/shard_map/ppermute | solution.py:23
  35.8 1.0 %average.1 = f32[128,768]{1,0:T(8,128)} custom-call(bf16[128,768]{1,0:T(8,128)(2,1)S(1)} %kept_tracks.1.kept, bf16[128,768]{1,0:T(8,128)(2,1)S(1)} %collective-permute-done.13.received, s32[1,768]{1,0:T(1,128)S(1)} %reshape.7.pairs), custom_call_target="tpu_custom_call" | custom-call | bytes 789504 | tf_op jit(solution)/shard_map/average/pallas_call | solution.py:44
  (16 shorter events, 0.1 us)
Async XLA Ops:
  1.2 7.2 %collective-permute-start.2 = (bf16[160,384]{1,0:T(8,128)(2,1)S(1)}, bf16[160,384]{1,0:T(8,128)(2,1)S(1)}, u32[]{:S(2)}, u32[]{:S(2)}) collective-permute-start(bf16[160,384]{1,0:T(8,128)(2,1)S(1)} %get-tuple-element.48), channel_id=1, source_target_pairs={{0,1},{1,0},{2,3},{3,2},{4,5},{5,4},{6,7},{7,6},{8,9},{9,8},{10,11... | collective-permute-start | bytes 368648 | tf_op jit(solution)/shard_map/ppermute | solution.py:23
  4.2 10.1 %collective-permute-start.9 = (bf16[256,384]{1,0:T(8,128)(2,1)S(1)}, bf16[256,384]{1,0:T(8,128)(2,1)S(1)}, u32[]{:S(2)}, u32[]{:S(2)}) collective-permute-start(bf16[256,384]{1,0:T(8,128)(2,1)S(1)} %get-tuple-element.63), channel_id=1, source_target_pairs={{0,1},{1,0},{2,3},{3,2},{4,5},{5,4},{6,7},{7,6},{8,9},{9,8},{10,11... | collective-permute-start | bytes 589832 | tf_op jit(solution)/shard_map/ppermute | solution.py:23
  4.2 12.5 %collective-permute-start = (bf16[256,384]{1,0:T(8,128)(2,1)S(1)}, bf16[256,384]{1,0:T(8,128)(2,1)S(1)}, u32[]{:S(2)}, u32[]{:S(2)}) collective-permute-start(bf16[256,384]{1,0:T(8,128)(2,1)S(1)} %get-tuple-element.46), channel_id=1, source_target_pairs={{0,1},{1,0},{2,3},{3,2},{4,5},{5,4},{6,7},{7,6},{8,9},{9,8},{10,11... | collective-permute-start | bytes 589832 | tf_op jit(solution)/shard_map/ppermute | solution.py:23
  8.3 8.2 %collective-permute-start.3 = (bf16[160,384]{1,0:T(8,128)(2,1)S(1)}, bf16[160,384]{1,0:T(8,128)(2,1)S(1)}, u32[]{:S(2)}, u32[]{:S(2)}) collective-permute-start(bf16[160,384]{1,0:T(8,128)(2,1)S(1)} %collective-permute-done.2.refs_7_), channel_id=1, source_target_pairs={{0,16},{16,0},{1,17},{17,1},{2,18},{18,2},{3,19},{19,3},{4,20},{20... | collective-permute-start | bytes 368648 | tf_op jit(solution)/shard_map/ppermute | solution.py:23
  10.4 5.8 %collective-permute-start.4 = (bf16[128,128]{1,0:T(8,128)(2,1)S(1)}, bf16[128,128]{1,0:T(8,128)(2,1)S(1)}, u32[]{:S(2)}, u32[]{:S(2)}) collective-permute-start(bf16[128,128]{1,0:T(8,128)(2,1)S(1)} %get-tuple-element.47.refs_0_), channel_id=1, source_target_pairs={{0,4},{2,10},{4,8},{6,14},{8,12},{10,2},{12,0},{14,6},{1,5},{3,11}... | collective-permute-start | bytes 98312 | tf_op jit(solution)/shard_map/ppermute | solution.py:445
  12.0 4.5 %collective-permute-start.5 = (bf16[128,128]{1,0:T(8,128)(2,1)S(1)}, bf16[128,128]{1,0:T(8,128)(2,1)S(1)}, u32[]{:S(2)}, u32[]{:S(2)}) collective-permute-start(bf16[128,128]{1,0:T(8,128)(2,1)S(1)} %get-tuple-element.47.refs_0_), channel_id=1, source_target_pairs={{0,12},{4,0},{8,4},{12,8},{1,13},{5,1},{9,5},{13,9},{2,14},{6,2},{... | collective-permute-start | bytes 98312 | tf_op jit(solution)/shard_map/ppermute | solution.py:23
  14.2 5.3 %collective-permute-start.10 = (bf16[256,384]{1,0:T(8,128)(2,1)S(1)}, bf16[256,384]{1,0:T(8,128)(2,1)S(1)}, u32[]{:S(2)}, u32[]{:S(2)}) collective-permute-start(bf16[256,384]{1,0:T(8,128)(2,1)S(1)} %collective-permute-done.9.refs_0_), channel_id=1, source_target_pairs={{0,2},{2,0},{1,3},{3,1},{4,6},{6,4},{5,7},{7,5},{8,10},{10,8},{9,1... | collective-permute-start | bytes 589832 | tf_op jit(solution)/shard_map/ppermute | solution.py:23
  16.2 1.3 %collective-permute-start.7 = (bf16[160,384]{1,0:T(8,128)(2,1)S(1)}, bf16[160,384]{1,0:T(8,128)(2,1)S(1)}, u32[]{:S(2)}, u32[]{:S(2)}) collective-permute-start(bf16[160,384]{1,0:T(8,128)(2,1)S(1)} %collective-permute-done.2.refs_7_), channel_id=1, source_target_pairs={{0,2},{2,0},{1,3},{3,1},{4,6},{6,4},{5,7},{7,5},{8,10},{10,8},{9,1... | collective-permute-start | bytes 368648 | tf_op jit(solution)/shard_map/ppermute | solution.py:23
  16.5 1.8 %collective-permute-start.8 = (bf16[160,384]{1,0:T(8,128)(2,1)S(1)}, bf16[160,384]{1,0:T(8,128)(2,1)S(1)}, u32[]{:S(2)}, u32[]{:S(2)}) collective-permute-start(bf16[160,384]{1,0:T(8,128)(2,1)S(1)} %collective-permute-done.3.refs_9_), channel_id=1, source_target_pairs={{0,2},{2,0},{1,3},{3,1},{4,6},{6,4},{5,7},{7,5},{8,10},{10,8},{9,1... | collective-permute-start | bytes 368648 | tf_op jit(solution)/shard_map/ppermute | solution.py:23
  16.7 3.6 %collective-permute-start.1 = (bf16[256,384]{1,0:T(8,128)(2,1)S(1)}, bf16[256,384]{1,0:T(8,128)(2,1)S(1)}, u32[]{:S(2)}, u32[]{:S(2)}) collective-permute-start(bf16[256,384]{1,0:T(8,128)(2,1)S(1)} %collective-permute-done.refs_0_), channel_id=1, source_target_pairs={{0,2},{2,0},{1,3},{3,1},{4,6},{6,4},{5,7},{7,5},{8,10},{10,8},{9,1... | collective-permute-start | bytes 589832 | tf_op jit(solution)/shard_map/ppermute | solution.py:23
  17.0 1.2 %collective-permute-start.6 = (bf16[128,128]{1,0:T(8,128)(2,1)S(1)}, bf16[128,128]{1,0:T(8,128)(2,1)S(1)}, u32[]{:S(2)}, u32[]{:S(2)}) collective-permute-start(bf16[128,128]{1,0:T(8,128)(2,1)S(1)} %collective-permute-done.4.refs_1_), channel_id=1, source_target_pairs={{0,2},{2,0},{1,3},{3,1},{4,6},{6,4},{5,7},{7,5},{8,10},{10,8},{9,1... | collective-permute-start | bytes 98312 | tf_op jit(solution)/shard_map/ppermute | solution.py:23
  19.5 5.4 %slice-start = ((s8[4718592]{0:T(1024)(128)(4,1)}), s8[4194304]{0:T(1024)(128)(4,1)S(1)}, s32[]{:S(2)}) async-start(s8[4718592]{0:T(1024)(128)(4,1)} %bitcast.9), calls=%async_computation | async-start | bytes 8388608
  20.3 4.6 %slice-start.1 = ((s8[4718592]{0:T(1024)(128)(4,1)}), s8[524288]{0:T(1024)(128)(4,1)S(1)}, s32[]{:S(2)}) async-start(s8[4718592]{0:T(1024)(128)(4,1)} %bitcast.9), calls=%async_computation.1 | async-start | bytes 1048576
  22.4 7.8 %collective-permute-start.12 = (bf16[128,768]{1,0:T(8,128)(2,1)S(1)}, bf16[128,768]{1,0:T(8,128)(2,1)S(1)}, u32[]{:S(2)}, u32[]{:S(2)}) collective-permute-start(bf16[128,768]{1,0:T(8,128)(2,1)S(1)} %get-tuple-element.80.refs_0_), channel_id=1, source_target_pairs={{0,1},{1,0},{2,3},{3,2},{4,5},{5,4},{6,7},{7,6},{8,9},{9,8},{10,11... | collective-permute-start | bytes 589832 | tf_op jit(solution)/shard_map/ppermute | solution.py:23
  24.3 9.4 %collective-permute-start.11 = (bf16[128,768]{1,0:T(8,128)(2,1)S(1)}, bf16[128,768]{1,0:T(8,128)(2,1)S(1)}, u32[]{:S(2)}, u32[]{:S(2)}) collective-permute-start(bf16[128,768]{1,0:T(8,128)(2,1)S(1)} %second_share.1.refs_0_), channel_id=1, source_target_pairs={{0,1},{1,0},{2,3},{3,2},{4,5},{5,4},{6,7},{7,6},{8,9},{9,8},{10,11... | collective-permute-start | bytes 589832 | tf_op jit(solution)/shard_map/ppermute | solution.py:23
  33.8 0.7 %copy-start = (s32[768]{0:T(1024)S(1)}, s32[768]{0:T(1024)}, u32[]{:S(2)}) copy-start(s32[768]{0:T(1024)} %param.19) | copy-start | bytes 9220
  34.2 1.5 %collective-permute-start.13 = (bf16[128,768]{1,0:T(8,128)(2,1)S(1)}, bf16[128,768]{1,0:T(8,128)(2,1)S(1)}, u32[]{:S(2)}, u32[]{:S(2)}) collective-permute-start(bf16[128,768]{1,0:T(8,128)(2,1)S(1)} %get-tuple-element.86), channel_id=1, source_target_pairs={{0,2},{2,0},{1,3},{3,1},{4,6},{6,4},{5,7},{7,5},{8,10},{10,8},{9,1... | collective-permute-start | bytes 589832 | tf_op jit(solution)/shard_map/ppermute | solution.py:23

commit v5 on v4

--- a/solution.py
+++ b/solution.py
@@ -97,7 +97,7 @@
         copy.wait()
 
 
-def prepare_kernel(rows, embed, key_t, value_t, w_query, gain, last_gain, *refs):
+def prepare_kernel(rows, slots, embed, key_t, value_t, w_query, gain, last_gain, *refs):
     table, key_out, value_out, query_out, gain_out, last_out, cosine, sine = refs[:8]
     raw_gain, raw_last, sems = refs[8:]
     strand, pos = lax.axis_index("strand"), lax.axis_index("pos")
@@ -122,17 +122,12 @@
     gain_out[...] = raw_gain[...].reshape(gain_out.shape)
     last_out[...] = raw_last[...].reshape(last_out.shape)
 
-    def step(begin):
-        place = lax.rem(pos + blocks - begin // rows, blocks) * rows + offset
+    for i, (forward, reverse) in enumerate(slots):
+        behind = jnp.where(strand == 0, forward, reverse)
+        place = lax.rem(pos + blocks - behind, blocks) * rows + offset
         angle = jnp.where(strand == 0, place, total - 1 - place).astype(F32) * inverse
-        cosine[pl.ds(begin, rows), :] = jnp.cos(angle)
-        sine[pl.ds(begin, rows), :] = jnp.sin(angle) * sign
-
-    if blocks <= 4:
-        for i in range(blocks):
-            step(i * rows)
-    else:
-        over_blocks(total, rows, step)
+        cosine[i * rows : (i + 1) * rows, :] = jnp.cos(angle)
+        sine[i * rows : (i + 1) * rows, :] = jnp.sin(angle) * sign
     for copy in copies[2:]:
         copy.wait()
 
@@ -149,10 +144,36 @@
         copy.wait()
 
 
-def absorb(onehot, table, rows, start, width, weights, before, after):
+def block_of(count, rows):
+    if count <= 4 * rows:
+        return count
+    return 4 * rows if count % (4 * rows) == 0 else rows
+
+
+def mark(onehot, codes, first, entries, rows):
+    strand = lax.axis_index("strand")
+    half = entries // 2
+    count = codes.shape[0]
+    spot = lax.broadcasted_iota(jnp.int32, (BIN, entries), 1)
+    owner = jnp.where(spot < half, strand, 1 - strand)
+    entry = owner * half + spot % half
+    entry = jnp.where(strand == 0, entry, entries - 1 - entry)
+    place = lax.broadcasted_iota(jnp.int32, (BIN, entries), 0)
+    spread = jnp.where(place == entry // BASES, 1.0, 0.0).astype(BF16)
+    wanted = (entry[:1] % BASES).astype(F32)
+    block = block_of(count, rows)
+
+    def step(begin):
+        found = matmul(codes[pl.ds(begin, block), :], spread) == wanted
+        onehot[pl.ds(first + begin, block), :] = jnp.where(found, 1.0, 0.0).astype(BF16)
+
+    over_blocks(count, block, step)
+
+
+def absorb(onehot, span, table, rows, start, width, weights, before, after):
     kv_t, w_query, gain = weights
-    total = onehot.shape[0]
-    block = min(total, 4 * rows)
+    first, count = span
+    block = block_of(count, rows)
     cols = pl.ds(pl.multiple_of(start, LANES), width)
 
     def some(here):
@@ -161,7 +182,7 @@
         return found, floats, (floats * gain[:, cols]).astype(BF16)
 
     def step(begin):
-        here = pl.ds(begin, block)
+        here = pl.ds(first + begin, block)
         found, floats, gained = some(here)
         square = jnp.sum(floats * floats, axis=1, keepdims=True)
         kv = matmul_t(gained, kv_t[:, cols])
@@ -169,19 +190,20 @@
         after[1][here, :] = kv if before is None else before[1][here, :] + kv
         return found, gained
 
-    if total == block:
+    if count == block:
         found, gained = step(0)
         found, gained = found[:rows], gained[:rows]
     else:
-        over_blocks(total, block, lambda begin: step(begin) and None)
+        over_blocks(count, block, lambda begin: step(begin) and None)
         found, _, gained = some(pl.ds(0, rows))
+    if first:
+        return None
     query = matmul(gained, w_query[cols, :])
     after[2][...] = query if before is None else before[2][...] + query
     return found
 
 
-def own_kernel(code_steps, kv_steps, *refs):
-    blocks = len(code_steps)
+def own_kernel(blocks, kv_steps, *refs):
     codes = refs[:blocks]
     table, key_t, value_t = refs[blocks : blocks + 3]
     parts = refs[blocks + 3 : blocks + 3 + len(kv_steps)]
@@ -190,12 +212,9 @@
     size, groups = lax.axis_size("heads"), lax.axis_size("groups")
     key_cols, value_cols = key_t.shape[0], value_t.shape[0]
     entries, width = table.shape
-    half = entries // 2
     rows = codes[0].shape[0]
-    total = blocks * rows
-    for piece, (forward, reverse) in zip(codes, code_steps):
-        spot = jnp.where(strand == 0, forward, reverse) * rows
-        all_codes[pl.ds(pl.multiple_of(spot, rows), rows), :] = piece[...]
+    for i in range(blocks):
+        all_codes[i * rows : (i + 1) * rows, :] = codes[i][...]
 
     def kv_rows(owner):
         key_rows = pl.ds(pl.multiple_of(owner * key_cols, 16), key_cols)
@@ -211,30 +230,41 @@
         cols = pl.ds(pl.multiple_of(part * piece.shape[1], LANES), piece.shape[1])
         kv_t[key_rows, cols] = piece[:key_cols, :]
         kv_t[value_rows, cols] = piece[key_cols:, :]
-    spot = lax.broadcasted_iota(jnp.int32, (BIN, entries), 1)
-    owner = jnp.where(spot < half, strand, 1 - strand)
-    entry = owner * half + spot % half
-    entry = jnp.where(strand == 0, entry, entries - 1 - entry)
-    place = lax.broadcasted_iota(jnp.int32, (BIN, entries), 0)
-    spread = jnp.where(place == entry // BASES, 1.0, 0.0).astype(BF16)
-    wanted = (entry[:1] % BASES).astype(F32)
-    block = min(total, 4 * rows)
-
-    def mark(begin):
-        here = pl.ds(begin, block)
-        found = matmul(all_codes[here, :], spread) == wanted
-        onehot[here, :] = jnp.where(found, 1.0, 0.0).astype(BF16)
-
-    over_blocks(total, block, mark)
-    own[...] = absorb(
-        onehot, table, rows, mine * width, width, (kv_t, w_query, gain), None, (square, kv_sum, q_sum)
-    )
+    mark(onehot, all_codes, 0, entries, rows)
+    weights = (kv_t, w_query, gain)
+    span = (0, blocks * rows)
+    own[...] = absorb(onehot, span, table, rows, mine * width, width, weights, None, (square, kv_sum, q_sum))
 
 
 def chunk_start(step, index, chunks, width):
     size = lax.axis_size("heads")
     owner = lax.rem(lax.axis_index("heads") + size - step, size)
     return (owner * chunks + index) * width
+
+
+def join_kernel(step, index, chunks, rows, late, *refs):
+    mine, theirs, onehot_in, kv_t, w_query, gain, square_in, kv_in, q_in, own_table = refs[:10]
+    codes = refs[10 : 10 + late]
+    onehot, found, square, kv_sum, q_sum, table, all_codes = refs[10 + late :]
+    half, width = mine.shape
+    own_width = own_table.shape[1]
+    early = onehot_in.shape[0]
+    weights = (kv_t, w_query, gain)
+    for i in range(late):
+        all_codes[i * rows : (i + 1) * rows, :] = codes[i][...]
+    mark(onehot, all_codes, early, own_table.shape[0], rows)
+    onehot[:early, :] = onehot_in[...]
+    square[:early, :] = square_in[...]
+    kv_sum[:early, :] = kv_in[...]
+    span = (early, late * rows)
+    begin = lax.axis_index("heads") * own_width
+    absorb(onehot, span, own_table, rows, begin, own_width, weights, None, (square, kv_sum, None))
+    table[:half, :] = mine[...]
+    table[half:, :] = theirs[...]
+    begin = chunk_start(step, index, chunks, width)
+    span = (0, early + late * rows)
+    sums = (square, kv_sum, q_sum)
+    found[...] = absorb(onehot, span, table, rows, begin, width, weights, (square, kv_sum, q_in), sums)
 
 
 def chunk_kernel(step, index, chunks, rows, *refs):
@@ -245,6 +275,7 @@
     table[half:, :] = theirs[...]
     found[...] = absorb(
         onehot,
+        (0, onehot.shape[0]),
         table,
         rows,
         chunk_start(step, index, chunks, width),
@@ -270,13 +301,13 @@
     rows, own_width = own.shape
     features = inputs.shape[1]
     total = onehot.shape[0]
-    block = min(total, 4 * rows)
+    block = block_of(total, rows)
     table[:half, :] = mine[...]
     table[half:, :] = theirs[...]
     start = chunk_start(*steps[-1], chunks, width)
-    last = absorb(
-        onehot, table, rows, start, width, (kv_t, w_query, gain), (square, kv_sum, q_sum), (squares, sums, queries)
-    )
+    span, weights = (0, total), (kv_t, w_query, gain)
+    before, after = (square, kv_sum, q_sum), (squares, sums, queries)
+    last = absorb(onehot, span, table, rows, start, width, weights, before, after)
     inputs[:, pl.ds(pl.multiple_of(start, LANES), width)] = last
     for found, spot in zip(founds, steps):
         inputs[:, pl.ds(pl.multiple_of(chunk_start(*spot, chunks, width), LANES), width)] = found[...]
@@ -389,6 +420,12 @@
     chunks = 2 if width % (2 * LANES) == 0 else 1
     wide = width // chunks
 
+    early, late = [(0, 0)], []
+    for k in range(1, blocks, 2):
+        early.append((k, min(k + 1, blocks - 1)))
+        if k + 1 < blocks:
+            late.append((k + 1, k))
+
     hbm = pltpu.HBM
     part_kv, *own_pieces, own_codes = call(
         functools.partial(stage_kernel, chunks),
@@ -401,7 +438,7 @@
         spaces=[hbm] * 4,
     )
     table, key_own, value_own, query_own, gain, last_gain, cosine, sine = call(
-        functools.partial(prepare_kernel, rows),
+        functools.partial(prepare_kernel, rows, early + late),
         [
             shape((entries, width), BF16),
             shape(key_t.shape, BF16),
@@ -437,59 +474,75 @@
         scratch=[pltpu.SemaphoreType.DMA((2,))],
         spaces=[hbm],
     )
-    raw, raw_steps = [], []
-    for k in range(1, blocks, 2):
-        if k + 1 < blocks:
+    raw = []
+    for k, other in early[1:]:
+        if k != other:
             pairs = [((p, s), ((p + k + s) % blocks, s)) for p in range(blocks) for s in range(2)]
             pairs = [(2 * p + s, 2 * q + t) for (p, s), (q, t) in pairs]
             raw.append(lax.ppermute(own_codes, ("pos", "strand"), pairs))
-            raw_steps.append((k, k + 1))
         else:
+            if to_core:
+                own_codes, to_core[0] = lax.optimization_barrier((own_codes, to_core[0]))
             raw.append(shifted(own_codes, "pos", k))
-            raw_steps.append((k, k))
     if raw:
         raw[0], first_out = lax.optimization_barrier((raw[0], first_out))
     for step in range(1, size):
         for k in range(groups):
             here = from_heads[step - 1] if k == 0 else shifted(from_heads[step - 1], "groups", k)
-            if step == 1 and k == groups - 1 and blocks > 1:
-                here, *raw = lax.optimization_barrier((here, *raw))
             kv_parts += [here, to_core[step - 1] if k == 0 else shifted(here, "strand", 1)]
             kv_steps += [(step, k, 0), (step, k, 1)]
     for step in range(1, size):
         for i in range(chunks):
             here = shifted(own_pieces[i], "heads", step)
+            if step == 1 and i == chunks - 1 and raw:
+                here, *raw = lax.optimization_barrier((here, *raw))
             pieces.append((here, shifted(here, "strand", 1)))
             steps.append((step, i))
 
-    codes, code_steps = [own_codes], [(0, 0)]
-    for here, (mine, other) in zip(raw, raw_steps):
-        codes.append(here)
-        code_steps.append((mine, other))
-        if mine != other:
-            codes.append(shifted(here, "strand", 1))
-            code_steps.append((other, mine))
-    sums = [shape((total, 1), F32), shape((total, kv_all), F32), shape((rows, q_cols), F32)]
+    swapped = [shifted(raw[i], "strand", 1) for i in range(len(late))]
+    codes = [own_codes] + raw
+    if len(steps) < 2:
+        codes, swapped = codes + swapped, []
+
+    def sums_of(count):
+        return [shape((count, 1), F32), shape((count, kv_all), F32), shape((rows, q_cols), F32)]
+
+    count = rows * len(codes)
     onehot, kv_t, own, *state = call(
-        functools.partial(own_kernel, code_steps, kv_steps),
-        [shape((total, entries), BF16), shape((kv_all, features), BF16), shape((rows, width), BF16)] + sums,
+        functools.partial(own_kernel, len(codes), kv_steps),
+        [shape((count, entries), BF16), shape((kv_all, features), BF16), shape((rows, width), BF16)]
+        + sums_of(count),
         codes + [table, key_own, value_own] + kv_parts + [query_own, gain],
         "own_features",
-        scratch=[pltpu.VMEM((total, BIN), BF16)],
-        flops=2 * total * width * (entries + kv_all),
+        scratch=[pltpu.VMEM((count, BIN), BF16)],
+        flops=2 * count * width * (entries + kv_all),
         spare=8 * total * entries,
     )
     founds = []
     for (step, i), pair in zip(steps[:-1], pieces[:-1]):
-        found, *state = call(
-            functools.partial(chunk_kernel, step, i, chunks, rows),
-            [shape((rows, wide), BF16)] + sums,
-            list(pair) + [onehot, kv_t, query_own, gain] + state,
+        operands = list(pair) + [onehot, kv_t, query_own, gain] + state
+        outs = [shape((rows, wide), BF16)] + sums_of(total)
+        scratch = [pltpu.VMEM((entries, wide), BF16)]
+        if swapped:
+            kernel = functools.partial(join_kernel, step, i, chunks, rows, len(swapped))
+            operands += [table] + swapped
+            outs = [shape((total, entries), BF16)] + outs
+            scratch.append(pltpu.VMEM((rows * len(swapped), BIN), BF16))
+        else:
+            kernel = functools.partial(chunk_kernel, step, i, chunks, rows)
+        results = call(
+            kernel,
+            outs,
+            operands,
             "other_features",
-            scratch=[pltpu.VMEM((entries, wide), BF16)],
+            scratch=scratch,
             flops=2 * total * wide * (entries + kv_all),
             spare=8 * total * entries,
         )
+        if swapped:
+            onehot, *results = results
+            swapped = []
+        found, *state = results
         founds.append(found)
     o_cols = q_cols // KDIM * VDIM
     share_one, merged, inputs = call(

time: 37 us -> 36 us (0.973)
  waiting for transfers between devices: 10.1 us -> 9.01 us
    ppermute x13, waiting for transfers between devices: 9.79 us -> 9.01 us  [shifted(): lax.ppermute(value, axis, [(i, (i + distance) % size) for i in range(size)])]
  transfers between devices with their start and end apart: 14 -> 14, of which waited for: 7 -> 6; matrix products, arithmetic and copies ran while one was open for 2% -> 2% of each run, Pallas kernels for 19% -> 20%
where the time goes in v5:
time: 36 us; the launch traced here: 35.8 us
  starting transfers between devices  14 us (39%)
  Pallas kernels  11.9 us (33%)
  waiting for transfers between devices  9.01 us (25%)
  local copies, waits for them, and re-layouts  0.73 us (2%)
    ppermute x13, starting transfers between devices, shifted(): lax.ppermute(value, axis, [(i, (i + distance) % size) for i in range(size)])  12.5 us
    pallas_call x11, Pallas kernels, call(): pl.pallas_call(kernel, out_shape=list(outs), in_specs=specs, out_specs=[v...  11.9 us
    ppermute x13, waiting for transfers between devices, shifted(): lax.ppermute(value, axis, [(i, (i + distance) % size) for i in range(size)])  9.01 us
    ppermute x1, starting transfers between devices, body(): raw.append(lax.ppermute(own_codes, ('pos', 'strand'), pairs))  1.58 us
  transfers between devices with their start and end apart: 14, of which 6 were waited for; matrix products, arithmetic and copies ran while one was open for 2% of the time, Pallas kernels for 20%

profile of v5, /device:TPU:0, one launch (start us, length us, event | category | flops | bytes accessed | tf_op | source)
XLA Modules:
  0.0 35.8 jit_solution(9084881355766277268)
XLA Ops:
  0.0 1.1 %stage.1 = (bf16[160,384]{1,0:T(8,128)(2,1)S(1)}, bf16[256,384]{1,0:T(8,128)(2,1)S(1)}, bf16[256,384]{1,0:T(8,128)(2,1)S(1)}, bf16[128,128]{1,0:T(8,128)(2,1)S(1)}) custom-call(bf16[512,768]{1,0:T(8,128)(2,1)} %embed.3, bf16[64,1536]{1,0:T(8,128)(2,1)} %bitcast.13, bf16[96,1536]{1,0:T(8,128)(2,1)} %bitcast.11, s32[128,128]{1,0:T(8,128)} %bitcast.15), custom_call_target="tpu_custom_call" | custom-call | bytes 614400 | tf_op jit(solution)/shard_map/stage/pallas_call | solution.py:44
  1.2 3.0 %collective-permute-start.2 = (bf16[160,384]{1,0:T(8,128)(2,1)S(1)}, bf16[160,384]{1,0:T(8,128)(2,1)S(1)}, u32[]{:S(2)}, u32[]{:S(2)}) collective-permute-start(bf16[160,384]{1,0:T(8,128)(2,1)S(1)} %get-tuple-element.53), channel_id=1, source_target_pairs={{0,1},{1,0},{2,3},{3,2},{4,5},{5,4},{6,7},{7,6},{8,9},{9,8},{10,11... | collective-permute-start | bytes 368648 | tf_op jit(solution)/shard_map/ppermute | solution.py:23
  4.2 0.1 collective-permute-start.6
  4.2 1.9 %collective-permute-start = (bf16[256,384]{1,0:T(8,128)(2,1)S(1)}, bf16[256,384]{1,0:T(8,128)(2,1)S(1)}, u32[]{:S(2)}, u32[]{:S(2)}) collective-permute-start(bf16[256,384]{1,0:T(8,128)(2,1)S(1)} %get-tuple-element.49), channel_id=1, source_target_pairs={{0,1},{1,0},{2,3},{3,2},{4,5},{5,4},{6,7},{7,6},{8,9},{9,8},{10,11... | collective-permute-start | bytes 589832 | tf_op jit(solution)/shard_map/ppermute | solution.py:23
  6.2 1.9 %prepare.1 = (bf16[512,768]{1,0:T(8,128)(2,1)S(1)}, bf16[64,1536]{1,0:T(8,128)(2,1)S(1)}, bf16[96,1536]{1,0:T(8,128)(2,1)S(1)}, bf16[1536,512]{1,0:T(8,128)(2,1)...) custom-call(bf16[512,768]{1,0:T(8,128)(2,1)} %embed.3, ...), custom_call_target="tpu_custom_call" | custom-call | bytes 3399680 | tf_op jit(solution)/shard_map/prepare/pallas_call | solution.py:44
  8.1 0.2 collective-permute-done.2.refs_6_
  8.3 2.1 %collective-permute-start.8 = (bf16[160,384]{1,0:T(8,128)(2,1)S(1)}, bf16[160,384]{1,0:T(8,128)(2,1)S(1)}, u32[]{:S(2)}, u32[]{:S(2)}) collective-permute-start(bf16[160,384]{1,0:T(8,128)(2,1)S(1)} %collective-permute-done.2.refs_6_), channel_id=1, source_target_pairs={{0,16},{16,0},{1,17},{17,1},{2,18},{18,2},{3,19},{19,3},{4,20},{20... | collective-permute-start | bytes 368648 | tf_op jit(solution)/shard_map/ppermute | solution.py:23
  10.4 1.6 %collective-permute-start.1 = (bf16[128,128]{1,0:T(8,128)(2,1)S(1)}, bf16[128,128]{1,0:T(8,128)(2,1)S(1)}, u32[]{:S(2)}, u32[]{:S(2)}) collective-permute-start(bf16[128,128]{1,0:T(8,128)(2,1)S(1)} %get-tuple-element.56.refs_0_), channel_id=1, source_target_pairs={{0,4},{2,10},{4,8},{6,14},{8,12},{10,2},{12,0},{14,6},{1,5},{3,11}... | collective-permute-start | bytes 98312 | tf_op jit(solution)/shard_map/ppermute | solution.py:482
  12.0 2.2 %collective-permute-start.4 = (bf16[128,128]{1,0:T(8,128)(2,1)S(1)}, bf16[128,128]{1,0:T(8,128)(2,1)S(1)}, u32[]{:S(2)}, u32[]{:S(2)}) collective-permute-start(bf16[128,128]{1,0:T(8,128)(2,1)S(1)} %get-tuple-element.56.refs_0_), channel_id=1, source_target_pairs={{0,12},{4,0},{8,4},{12,8},{1,13},{5,1},{9,5},{13,9},{2,14},{6,2},{... | collective-permute-start | bytes 98312 | tf_op jit(solution)/shard_map/ppermute | solution.py:23
  14.2 0.2 collective-permute-done.8.refs_8_
  14.4 0.4 collective-permute-start.9
  14.7 1.6 %fetch_out.1 = (bf16[768,768]{1,0:T(8,128)(2,1)S(1)}, bf16[768,768]{1,0:T(8,128)(2,1)S(1)}) custom-call(bf16[768,1536]{1,0:T(8,128)(2,1)} %w_out.1), custom_call_target="tpu_custom_call" | custom-call | bytes 2359296 | tf_op jit(solution)/shard_map/fetch_out/pallas_call | solution.py:44
  16.4 0.2 collective-permute-done.4.refs_2_
  16.6 0.1 collective-permute-start.5
  16.7 0.4 %collective-permute-start.10 = (bf16[128,128]{1,0:T(8,128)(2,1)S(1)}, bf16[128,128]{1,0:T(8,128)(2,1)S(1)}, u32[]{:S(2)}, u32[]{:S(2)}) collective-permute-start(bf16[128,128]{1,0:T(8,128)(2,1)S(1)} %collective-permute-done.1.refs_1_), channel_id=1, source_target_pairs={{0,2},{2,0},{1,3},{3,1},{4,6},{6,4},{5,7},{7,5},{8,10},{10,8},{9,1... | collective-permute-start | bytes 98312 | tf_op jit(solution)/shard_map/ppermute | solution.py:23
  17.1 1.1 %own_features.1 = (bf16[384,512]{1,0:T(8,128)(2,1)S(1)}, bf16[320,1536]{1,0:T(8,128)(2,1)S(1)}, bf16[128,768]{1,0:T(8,128)(2,1)S(1)}, f32[384,1]{1,0:T(8,128)S(1...) custom-call(bf16[128,128]{1,0:T(8,128)(2,1)S(1)} %get-tuple-element.56.refs_0_, ...), custom_call_target="tpu_custom_call" | custom-call | flops 490733568 | bytes 6068224 | tf_op jit(solution)/shard_map/own_features/pallas_call | solution.py:44
  18.2 1.3 %other_features.1 = (bf16[512,512]{1,0:T(8,128)(2,1)S(1)}, bf16[128,384]{1,0:T(8,128)(2,1)S(1)}, f32[512,1]{1,0:T(8,128)S(1)}, f32[512,320]{1,0:T(8,128)S(1)}, f32[128,512]{1,0:T(8,128)S(1)}) custom-call(bf16[256,384]{1,0:T(8,128)(2,1)S(1)} %collective-permute-done.6.refs_0_, bf16[256,384]{1,0:T(8,128)(2,1)S(1)} %collective-permute-done.7.refs_1_, ...), custom_call_target="tpu_custom_call" | custom-call | flops 327155712 | bytes 7346176 | tf_op jit(solution)/shard_map/other_features/pallas_call | solution.py:44
  19.5 0.0 slice-start.1
  19.5 2.1 %attend.1 = (bf16[128,768]{1,0:T(8,128)(2,1)S(1)}, bf16[128,768]{1,0:T(8,128)(2,1)S(1)}, bf16[128,1536]{1,0:T(8,128)(2,1)S(1)}) custom-call(bf16[256,384]{1,0:T(8,128)(2,1)S(1)} %collective-permute-done.refs_0_, bf16[256,384]{1,0:T(8,128)(2,1)S(1)} %collective-permute-done.5.refs_1_, bf16[512,512]{1,0:T(8,128)(2,1)S(1)} %get-tuple-element.72.refs_2_, ...), custom_call_target="tpu_custom_call" | custom-call | flops 528482304 | bytes 9345024 | tf_op jit(solution)/shard_map/attend/pallas_call | solution.py:44
  21.6 1.6 %collective-permute-start.12 = (bf16[128,768]{1,0:T(8,128)(2,1)S(1)}, bf16[128,768]{1,0:T(8,128)(2,1)S(1)}, u32[]{:S(2)}, u32[]{:S(2)}) collective-permute-start(bf16[128,768]{1,0:T(8,128)(2,1)S(1)} %get-tuple-element.86.refs_0_), channel_id=1, source_target_pairs={{0,1},{1,0},{2,3},{3,2},{4,5},{5,4},{6,7},{7,6},{8,9},{9,8},{10,11... | collective-permute-start | bytes 589832 | tf_op jit(solution)/shard_map/ppermute | solution.py:23
  23.1 0.3 second_share.1.refs_0_
  23.5 0.6 %collective-permute-start.11 = (bf16[128,768]{1,0:T(8,128)(2,1)S(1)}, bf16[128,768]{1,0:T(8,128)(2,1)S(1)}, u32[]{:S(2)}, u32[]{:S(2)}) collective-permute-start(bf16[128,768]{1,0:T(8,128)(2,1)S(1)} %second_share.1.refs_0_), channel_id=1, source_target_pairs={{0,1},{1,0},{2,3},{3,2},{4,5},{5,4},{6,7},{7,6},{8,9},{9,8},{10,11... | collective-permute-start | bytes 589832 | tf_op jit(solution)/shard_map/ppermute | solution.py:23
  24.1 0.6 %copy.13 = bf16[1536,2,768]{2,0,1:T(8,128)(2,1)S(1)} copy(bf16[1536,2,768]{2,1,0:T(2,128)(2,1)S(1)} %bitcast.10) | data formatting | bytes 9437184 | tf_op jit(solution)/shard_map/optimization_barrier | solution.py:577
  24.7 4.7 %collective-permute-done.12.refs_1_ = bf16[128,768]{1,0:T(8,128)(2,1)S(1)} collective-permute-done((bf16[128,768]{1,0:T(8,128)(2,1)S(1)}, bf16[128,768]{1,0:T(8,128)(2,1)S(1)}, u32[]{:S(2)}, u32[]{:S(2)}) %collective-permute-start.12) | collective-permute-done | bytes 196640 | tf_op jit(solution)/shard_map/ppermute | solution.py:23
  29.4 0.5 %first_tracks.1 = (f32[128,1]{1,0:T(8,128)S(1)}, f32[128,768]{1,0:T(8,128)S(1)}, f32[128,768]{1,0:T(8,128)S(1)}) custom-call(bf16[128,768]{1,0:T(8,128)(2,1)S(1)} %get-tuple-element.86.refs_0_, bf16[128,768]{1,0:T(8,128)(2,1)S(1)} %collective-permute-done.12.refs_1_, bf16[128,1536]{1,0:T(8,128)(2,1)S(1)} %get-tuple-element.83.refs_2_, ...), custom_call_target="tpu_custom_call" | custom-call | flops 301989888 | bytes 6363136 | tf_op jit(solution)/shard_map/first_tracks/pallas_call | solution.py:44
  29.9 2.9 %collective-permute-done.11.refs_1_ = bf16[128,768]{1,0:T(8,128)(2,1)S(1)} collective-permute-done((bf16[128,768]{1,0:T(8,128)(2,1)S(1)}, bf16[128,768]{1,0:T(8,128)(2,1)S(1)}, u32[]{:S(2)}, u32[]{:S(2)}) %collective-permute-start.11) | collective-permute-done | bytes 196640 | tf_op jit(solution)/shard_map/ppermute | solution.py:23
  32.8 0.5 %sent_tracks.1 = (bf16[128,768]{1,0:T(8,128)(2,1)S(1)}, bf16[128,768]{1,0:T(8,128)(2,1)S(1)}, f32[128,1]{1,0:T(8,128)S(1)}) custom-call(bf16[128,768]{1,0:T(8,128)(2,1)S(1)} %second_share.1.refs_0_, bf16[128,768]{1,0:T(8,128)(2,1)S(1)} %collective-permute-done.11.refs_1_, bf16[128,1536]{1,0:T(8,128)(2,1)S(1)} %get-tuple-element.83.refs_2_, ...), custom_call_target="tpu_custom_call" | custom-call | flops 150994944 | bytes 6428672 | tf_op jit(solution)/shard_map/sent_tracks/pallas_call | solution.py:44
  33.3 0.1 collective-permute-start.13
  33.4 0.1 copy-done
  33.5 0.5 %kept_tracks.1.kept = bf16[128,768]{1,0:T(8,128)(2,1)S(1)} custom-call(bf16[128,768]{1,0:T(8,128)(2,1)S(1)} %get-tuple-element.89.gained, bf16[2,1536,768]{2,1,0:T(8,128)(2,1)S(1)} %bitcast.8, f32[128,768]{1,0:T(8,128)S(1)} %get-tuple-element.90.to_keep, f32[128,1]{1,0:T(8,128)S(1)} %get-tuple-element.91.scale), custom_call_target="tpu_custom_call" | custom-call | flops 150994944 | bytes 5570560 | tf_op jit(solution)/shard_map/kept_tracks/pallas_call | solution.py:44
  33.9 0.9 %collective-permute-done.13.received = bf16[128,768]{1,0:T(8,128)(2,1)S(1)} collective-permute-done((bf16[128,768]{1,0:T(8,128)(2,1)S(1)}, bf16[128,768]{1,0:T(8,128)(2,1)S(1)}, u32[]{:S(2)}, u32[]{:S(2)}) %collective-permute-start.13) | collective-permute-done | bytes 196640 | tf_op jit(solution)/shard_map/ppermute | solution.py:23
  34.8 1.0 %average.1 = f32[128,768]{1,0:T(8,128)} custom-call(bf16[128,768]{1,0:T(8,128)(2,1)S(1)} %kept_tracks.1.kept, bf16[128,768]{1,0:T(8,128)(2,1)S(1)} %collective-permute-done.13.received, s32[1,768]{1,0:T(1,128)S(1)} %reshape.7.pairs), custom_call_target="tpu_custom_call" | custom-call | bytes 789504 | tf_op jit(solution)/shard_map/average/pallas_call | solution.py:44
  (16 shorter events, 0.0 us)
Async XLA Ops:
  1.2 7.2 %collective-permute-start.2 = (bf16[160,384]{1,0:T(8,128)(2,1)S(1)}, bf16[160,384]{1,0:T(8,128)(2,1)S(1)}, u32[]{:S(2)}, u32[]{:S(2)}) collective-permute-start(bf16[160,384]{1,0:T(8,128)(2,1)S(1)} %get-tuple-element.53), channel_id=1, source_target_pairs={{0,1},{1,0},{2,3},{3,2},{4,5},{5,4},{6,7},{7,6},{8,9},{9,8},{10,11... | collective-permute-start | bytes 368648 | tf_op jit(solution)/shard_map/ppermute | solution.py:23
  4.2 10.1 %collective-permute-start.6 = (bf16[256,384]{1,0:T(8,128)(2,1)S(1)}, bf16[256,384]{1,0:T(8,128)(2,1)S(1)}, u32[]{:S(2)}, u32[]{:S(2)}) collective-permute-start(bf16[256,384]{1,0:T(8,128)(2,1)S(1)} %get-tuple-element.58), channel_id=1, source_target_pairs={{0,1},{1,0},{2,3},{3,2},{4,5},{5,4},{6,7},{7,6},{8,9},{9,8},{10,11... | collective-permute-start | bytes 589832 | tf_op jit(solution)/shard_map/ppermute | solution.py:23
  4.2 12.2 %collective-permute-start = (bf16[256,384]{1,0:T(8,128)(2,1)S(1)}, bf16[256,384]{1,0:T(8,128)(2,1)S(1)}, u32[]{:S(2)}, u32[]{:S(2)}) collective-permute-start(bf16[256,384]{1,0:T(8,128)(2,1)S(1)} %get-tuple-element.49), channel_id=1, source_target_pairs={{0,1},{1,0},{2,3},{3,2},{4,5},{5,4},{6,7},{7,6},{8,9},{9,8},{10,11... | collective-permute-start | bytes 589832 | tf_op jit(solution)/shard_map/ppermute | solution.py:23
  8.3 3.7 %collective-permute-start.3 = (bf16[160,384]{1,0:T(8,128)(2,1)S(1)}, bf16[160,384]{1,0:T(8,128)(2,1)S(1)}, u32[]{:S(2)}, u32[]{:S(2)}) collective-permute-start(bf16[160,384]{1,0:T(8,128)(2,1)S(1)} %collective-permute-done.2.refs_6_), channel_id=1, source_target_pairs={{0,2},{2,0},{1,3},{3,1},{4,6},{6,4},{5,7},{7,5},{8,10},{10,8},{9,1... | collective-permute-start | bytes 368648 | tf_op jit(solution)/shard_map/ppermute | solution.py:23
  8.3 6.1 %collective-permute-start.8 = (bf16[160,384]{1,0:T(8,128)(2,1)S(1)}, bf16[160,384]{1,0:T(8,128)(2,1)S(1)}, u32[]{:S(2)}, u32[]{:S(2)}) collective-permute-start(bf16[160,384]{1,0:T(8,128)(2,1)S(1)} %collective-permute-done.2.refs_6_), channel_id=1, source_target_pairs={{0,16},{16,0},{1,17},{17,1},{2,18},{18,2},{3,19},{19,3},{4,20},{20... | collective-permute-start | bytes 368648 | tf_op jit(solution)/shard_map/ppermute | solution.py:23
  10.4 6.0 %collective-permute-start.1 = (bf16[128,128]{1,0:T(8,128)(2,1)S(1)}, bf16[128,128]{1,0:T(8,128)(2,1)S(1)}, u32[]{:S(2)}, u32[]{:S(2)}) collective-permute-start(bf16[128,128]{1,0:T(8,128)(2,1)S(1)} %get-tuple-element.56.refs_0_), channel_id=1, source_target_pairs={{0,4},{2,10},{4,8},{6,14},{8,12},{10,2},{12,0},{14,6},{1,5},{3,11}... | collective-permute-start | bytes 98312 | tf_op jit(solution)/shard_map/ppermute | solution.py:482
  12.0 4.6 %collective-permute-start.4 = (bf16[128,128]{1,0:T(8,128)(2,1)S(1)}, bf16[128,128]{1,0:T(8,128)(2,1)S(1)}, u32[]{:S(2)}, u32[]{:S(2)}) collective-permute-start(bf16[128,128]{1,0:T(8,128)(2,1)S(1)} %get-tuple-element.56.refs_0_), channel_id=1, source_target_pairs={{0,12},{4,0},{8,4},{12,8},{1,13},{5,1},{9,5},{13,9},{2,14},{6,2},{... | collective-permute-start | bytes 98312 | tf_op jit(solution)/shard_map/ppermute | solution.py:23
  14.2 3.9 %collective-permute-start.7 = (bf16[256,384]{1,0:T(8,128)(2,1)S(1)}, bf16[256,384]{1,0:T(8,128)(2,1)S(1)}, u32[]{:S(2)}, u32[]{:S(2)}) collective-permute-start(bf16[256,384]{1,0:T(8,128)(2,1)S(1)} %collective-permute-done.6.refs_0_), channel_id=1, source_target_pairs={{0,2},{2,0},{1,3},{3,1},{4,6},{6,4},{5,7},{7,5},{8,10},{10,8},{9,1... | collective-permute-start | bytes 589832 | tf_op jit(solution)/shard_map/ppermute | solution.py:23
  14.4 2.7 %collective-permute-start.9 = (bf16[160,384]{1,0:T(8,128)(2,1)S(1)}, bf16[160,384]{1,0:T(8,128)(2,1)S(1)}, u32[]{:S(2)}, u32[]{:S(2)}) collective-permute-start(bf16[160,384]{1,0:T(8,128)(2,1)S(1)} %collective-permute-done.8.refs_8_), channel_id=1, source_target_pairs={{0,2},{2,0},{1,3},{3,1},{4,6},{6,4},{5,7},{7,5},{8,10},{10,8},{9,1... | collective-permute-start | bytes 368648 | tf_op jit(solution)/shard_map/ppermute | solution.py:23
  16.6 2.9 %collective-permute-start.5 = (bf16[256,384]{1,0:T(8,128)(2,1)S(1)}, bf16[256,384]{1,0:T(8,128)(2,1)S(1)}, u32[]{:S(2)}, u32[]{:S(2)}) collective-permute-start(bf16[256,384]{1,0:T(8,128)(2,1)S(1)} %collective-permute-done.refs_0_), channel_id=1, source_target_pairs={{0,2},{2,0},{1,3},{3,1},{4,6},{6,4},{5,7},{7,5},{8,10},{10,8},{9,1... | collective-permute-start | bytes 589832 | tf_op jit(solution)/shard_map/ppermute | solution.py:23
  16.7 1.5 %collective-permute-start.10 = (bf16[128,128]{1,0:T(8,128)(2,1)S(1)}, bf16[128,128]{1,0:T(8,128)(2,1)S(1)}, u32[]{:S(2)}, u32[]{:S(2)}) collective-permute-start(bf16[128,128]{1,0:T(8,128)(2,1)S(1)} %collective-permute-done.1.refs_1_), channel_id=1, source_target_pairs={{0,2},{2,0},{1,3},{3,1},{4,6},{6,4},{5,7},{7,5},{8,10},{10,8},{9,1... | collective-permute-start | bytes 98312 | tf_op jit(solution)/shard_map/ppermute | solution.py:23
  18.2 5.9 %slice-start = ((s8[4718592]{0:T(1024)(128)(4,1)}), s8[4194304]{0:T(1024)(128)(4,1)S(1)}, s32[]{:S(2)}) async-start(s8[4718592]{0:T(1024)(128)(4,1)} %bitcast.9), calls=%async_computation | async-start | bytes 8388608
  19.5 4.6 %slice-start.1 = ((s8[4718592]{0:T(1024)(128)(4,1)}), s8[524288]{0:T(1024)(128)(4,1)S(1)}, s32[]{:S(2)}) async-start(s8[4718592]{0:T(1024)(128)(4,1)} %bitcast.9), calls=%async_computation.1 | async-start | bytes 1048576
  21.6 7.8 %collective-permute-start.12 = (bf16[128,768]{1,0:T(8,128)(2,1)S(1)}, bf16[128,768]{1,0:T(8,128)(2,1)S(1)}, u32[]{:S(2)}, u32[]{:S(2)}) collective-permute-start(bf16[128,768]{1,0:T(8,128)(2,1)S(1)} %get-tuple-element.86.refs_0_), channel_id=1, source_target_pairs={{0,1},{1,0},{2,3},{3,2},{4,5},{5,4},{6,7},{7,6},{8,9},{9,8},{10,11... | collective-permute-start | bytes 589832 | tf_op jit(solution)/shard_map/ppermute | solution.py:23
  23.5 9.3 %collective-permute-start.11 = (bf16[128,768]{1,0:T(8,128)(2,1)S(1)}, bf16[128,768]{1,0:T(8,128)(2,1)S(1)}, u32[]{:S(2)}, u32[]{:S(2)}) collective-permute-start(bf16[128,768]{1,0:T(8,128)(2,1)S(1)} %second_share.1.refs_0_), channel_id=1, source_target_pairs={{0,1},{1,0},{2,3},{3,2},{4,5},{5,4},{6,7},{7,6},{8,9},{9,8},{10,11... | collective-permute-start | bytes 589832 | tf_op jit(solution)/shard_map/ppermute | solution.py:23
  32.8 0.7 %copy-start = (s32[768]{0:T(1024)S(1)}, s32[768]{0:T(1024)}, u32[]{:S(2)}) copy-start(s32[768]{0:T(1024)} %param.19) | copy-start | bytes 9220
  33.3 1.5 %collective-permute-start.13 = (bf16[128,768]{1,0:T(8,128)(2,1)S(1)}, bf16[128,768]{1,0:T(8,128)(2,1)S(1)}, u32[]{:S(2)}, u32[]{:S(2)}) collective-permute-start(bf16[128,768]{1,0:T(8,128)(2,1)S(1)} %get-tuple-element.92), channel_id=1, source_target_pairs={{0,2},{2,0},{1,3},{3,1},{4,6},{6,4},{5,7},{7,5},{8,10},{10,8},{9,1... | collective-permute-start | bytes 589832 | tf_op jit(solution)/shard_map/ppermute | solution.py:23

commit v6 on v5

--- a/solution.py
+++ b/solution.py
@@ -31,7 +31,7 @@
     return lax.dot_general(a, b, (((1,), (1,)), ((), ())), preferred_element_type=F32)
 
 
-def call(kernel, outs, operands, name, scratch=(), spaces=None, flops=0, spare=0):
+def call(kernel, outs, operands, name, scratch=(), spaces=None, flops=0, spare=0, out_space=None):
     vmem = pl.BlockSpec(memory_space=pltpu.VMEM)
     spaces = spaces or [None] * len(operands)
     operands = [
@@ -45,7 +45,7 @@
         kernel,
         out_shape=list(outs),
         in_specs=specs,
-        out_specs=[vmem] * len(outs),
+        out_specs=[pl.BlockSpec(memory_space=out_space or pltpu.VMEM)] * len(outs),
         scratch_shapes=list(scratch),
         compiler_params=pltpu.CompilerParams(
             vmem_limit_bytes=min(VMEM_LIMIT, moved + moved // 4 + 6 * 2**20 + spare)
@@ -380,17 +380,25 @@
     kept[...] = soft(logits * scale[...]).astype(BF16)
 
 
-def average_kernel(kept, received, pairs, out):
+def average_kernel(parts, kept, received, pairs, out, stage, sems):
     strand = lax.axis_index("strand")
     count = kept.shape[1]
-    mine, theirs = kept[...].astype(F32), received[...].astype(F32)
-    forward = jnp.where(strand == 0, mine, theirs)
-    reverse = jnp.where(strand == 0, theirs, mine)
+    rows = kept.shape[0] // parts
     index = lax.broadcasted_iota(jnp.int32, (1, count), 1)
     even = index % 2 == 0
     swapped = (pairs[...] % 2 == 0) != even
-    partner = jnp.where(even, pltpu.roll(reverse, count - 1, 1), pltpu.roll(reverse, 1, 1))
-    out[...] = 0.5 * (forward + jnp.where(swapped, partner, reverse))
+    copies = []
+    for i in range(parts):
+        here = slice(i * rows, (i + 1) * rows)
+        mine, theirs = kept[here, :].astype(F32), received[here, :].astype(F32)
+        forward = jnp.where(strand == 0, mine, theirs)
+        reverse = jnp.where(strand == 0, theirs, mine)
+        partner = jnp.where(even, pltpu.roll(reverse, count - 1, 1), pltpu.roll(reverse, 1, 1))
+        stage[here, :] = 0.5 * (forward + jnp.where(swapped, partner, reverse))
+        copies.append(pltpu.make_async_copy(stage.at[here], out.at[here], sems.at[i]))
+        copies[-1].start()
+    for copy in copies:
+        copy.wait()
 
 
 def body(
@@ -607,10 +615,12 @@
         flops=rows * features * tracks_half,
     )
     (out,) = call(
-        average_kernel,
+        functools.partial(average_kernel, 4),
         [shape((rows, tracks_half), F32)],
         [kept, received, track_pairs.reshape(1, tracks_half)],
         "average",
+        scratch=[pltpu.VMEM((rows, tracks_half), F32), pltpu.SemaphoreType.DMA((4,))],
+        out_space=hbm,
     )
     return out
 

time: 36 us -> 35.9 us (level)
  no operation moved by 1% of the time
where the time goes in v6:
time: 35.9 us; the launch traced here: 35.7 us
  starting transfers between devices  14 us (39%)
  Pallas kernels  11.8 us (33%)
  waiting for transfers between devices  9.01 us (25%)
  local copies, waits for them, and re-layouts  0.73 us (2%)
    ppermute x13, starting transfers between devices, shifted(): lax.ppermute(value, axis, [(i, (i + distance) % size) for i in range(size)])  12.5 us
    pallas_call x11, Pallas kernels, call(): pl.pallas_call(kernel, out_shape=list(outs), in_specs=specs, out_specs=[p...  11.8 us
    ppermute x13, waiting for transfers between devices, shifted(): lax.ppermute(value, axis, [(i, (i + distance) % size) for i in range(size)])  9.01 us
    ppermute x1, starting transfers between devices, body(): raw.append(lax.ppermute(own_codes, ('pos', 'strand'), pairs))  1.58 us
  transfers between devices with their start and end apart: 14, of which 6 were waited for; matrix products, arithmetic and copies ran while one was open for 2% of the time, Pallas kernels for 20%

profile of v6, /device:TPU:0, one launch (start us, length us, event | category | flops | bytes accessed | tf_op | source)
XLA Modules:
  0.0 35.7 jit_solution(2695660372064757644)
XLA Ops:
  0.0 1.1 %stage.1 = (bf16[160,384]{1,0:T(8,128)(2,1)S(1)}, bf16[256,384]{1,0:T(8,128)(2,1)S(1)}, bf16[256,384]{1,0:T(8,128)(2,1)S(1)}, bf16[128,128]{1,0:T(8,128)(2,1)S(1)}) custom-call(bf16[512,768]{1,0:T(8,128)(2,1)} %embed.3, bf16[64,1536]{1,0:T(8,128)(2,1)} %bitcast.13, bf16[96,1536]{1,0:T(8,128)(2,1)} %bitcast.11, s32[128,128]{1,0:T(8,128)} %bitcast.15), custom_call_target="tpu_custom_call" | custom-call | bytes 614400 | tf_op jit(solution)/shard_map/stage/pallas_call | solution.py:44
  1.2 3.0 %collective-permute-start.2 = (bf16[160,384]{1,0:T(8,128)(2,1)S(1)}, bf16[160,384]{1,0:T(8,128)(2,1)S(1)}, u32[]{:S(2)}, u32[]{:S(2)}) collective-permute-start(bf16[160,384]{1,0:T(8,128)(2,1)S(1)} %get-tuple-element.53), channel_id=1, source_target_pairs={{0,1},{1,0},{2,3},{3,2},{4,5},{5,4},{6,7},{7,6},{8,9},{9,8},{10,11... | collective-permute-start | bytes 368648 | tf_op jit(solution)/shard_map/ppermute | solution.py:23
  4.2 0.1 collective-permute-start.6
  4.2 1.9 %collective-permute-start = (bf16[256,384]{1,0:T(8,128)(2,1)S(1)}, bf16[256,384]{1,0:T(8,128)(2,1)S(1)}, u32[]{:S(2)}, u32[]{:S(2)}) collective-permute-start(bf16[256,384]{1,0:T(8,128)(2,1)S(1)} %get-tuple-element.49), channel_id=1, source_target_pairs={{0,1},{1,0},{2,3},{3,2},{4,5},{5,4},{6,7},{7,6},{8,9},{9,8},{10,11... | collective-permute-start | bytes 589832 | tf_op jit(solution)/shard_map/ppermute | solution.py:23
  6.2 1.9 %prepare.1 = (bf16[512,768]{1,0:T(8,128)(2,1)S(1)}, bf16[64,1536]{1,0:T(8,128)(2,1)S(1)}, bf16[96,1536]{1,0:T(8,128)(2,1)S(1)}, bf16[1536,512]{1,0:T(8,128)(2,1)...) custom-call(bf16[512,768]{1,0:T(8,128)(2,1)} %embed.3, ...), custom_call_target="tpu_custom_call" | custom-call | bytes 3399680 | tf_op jit(solution)/shard_map/prepare/pallas_call | solution.py:44
  8.1 0.2 collective-permute-done.2.refs_6_
  8.3 2.1 %collective-permute-start.8 = (bf16[160,384]{1,0:T(8,128)(2,1)S(1)}, bf16[160,384]{1,0:T(8,128)(2,1)S(1)}, u32[]{:S(2)}, u32[]{:S(2)}) collective-permute-start(bf16[160,384]{1,0:T(8,128)(2,1)S(1)} %collective-permute-done.2.refs_6_), channel_id=1, source_target_pairs={{0,16},{16,0},{1,17},{17,1},{2,18},{18,2},{3,19},{19,3},{4,20},{20... | collective-permute-start | bytes 368648 | tf_op jit(solution)/shard_map/ppermute | solution.py:23
  10.4 1.6 %collective-permute-start.1 = (bf16[128,128]{1,0:T(8,128)(2,1)S(1)}, bf16[128,128]{1,0:T(8,128)(2,1)S(1)}, u32[]{:S(2)}, u32[]{:S(2)}) collective-permute-start(bf16[128,128]{1,0:T(8,128)(2,1)S(1)} %get-tuple-element.56.refs_0_), channel_id=1, source_target_pairs={{0,4},{2,10},{4,8},{6,14},{8,12},{10,2},{12,0},{14,6},{1,5},{3,11}... | collective-permute-start | bytes 98312 | tf_op jit(solution)/shard_map/ppermute | solution.py:490
  12.0 2.2 %collective-permute-start.4 = (bf16[128,128]{1,0:T(8,128)(2,1)S(1)}, bf16[128,128]{1,0:T(8,128)(2,1)S(1)}, u32[]{:S(2)}, u32[]{:S(2)}) collective-permute-start(bf16[128,128]{1,0:T(8,128)(2,1)S(1)} %get-tuple-element.56.refs_0_), channel_id=1, source_target_pairs={{0,12},{4,0},{8,4},{12,8},{1,13},{5,1},{9,5},{13,9},{2,14},{6,2},{... | collective-permute-start | bytes 98312 | tf_op jit(solution)/shard_map/ppermute | solution.py:23
  14.2 0.2 collective-permute-done.8.refs_8_
  14.4 0.4 collective-permute-start.9
  14.7 1.6 %fetch_out.1 = (bf16[768,768]{1,0:T(8,128)(2,1)S(1)}, bf16[768,768]{1,0:T(8,128)(2,1)S(1)}) custom-call(bf16[768,1536]{1,0:T(8,128)(2,1)} %w_out.1), custom_call_target="tpu_custom_call" | custom-call | bytes 2359296 | tf_op jit(solution)/shard_map/fetch_out/pallas_call | solution.py:44
  16.4 0.2 collective-permute-done.4.refs_2_
  16.6 0.1 collective-permute-start.5
  16.7 0.4 %collective-permute-start.10 = (bf16[128,128]{1,0:T(8,128)(2,1)S(1)}, bf16[128,128]{1,0:T(8,128)(2,1)S(1)}, u32[]{:S(2)}, u32[]{:S(2)}) collective-permute-start(bf16[128,128]{1,0:T(8,128)(2,1)S(1)} %collective-permute-done.1.refs_1_), channel_id=1, source_target_pairs={{0,2},{2,0},{1,3},{3,1},{4,6},{6,4},{5,7},{7,5},{8,10},{10,8},{9,1... | collective-permute-start | bytes 98312 | tf_op jit(solution)/shard_map/ppermute | solution.py:23
  17.1 1.1 %own_features.1 = (bf16[384,512]{1,0:T(8,128)(2,1)S(1)}, bf16[320,1536]{1,0:T(8,128)(2,1)S(1)}, bf16[128,768]{1,0:T(8,128)(2,1)S(1)}, f32[384,1]{1,0:T(8,128)S(1...) custom-call(bf16[128,128]{1,0:T(8,128)(2,1)S(1)} %get-tuple-element.56.refs_0_, ...), custom_call_target="tpu_custom_call" | custom-call | flops 490733568 | bytes 6068224 | tf_op jit(solution)/shard_map/own_features/pallas_call | solution.py:44
  18.2 1.3 %other_features.1 = (bf16[512,512]{1,0:T(8,128)(2,1)S(1)}, bf16[128,384]{1,0:T(8,128)(2,1)S(1)}, f32[512,1]{1,0:T(8,128)S(1)}, f32[512,320]{1,0:T(8,128)S(1)}, f32[128,512]{1,0:T(8,128)S(1)}) custom-call(bf16[256,384]{1,0:T(8,128)(2,1)S(1)} %collective-permute-done.6.refs_0_, bf16[256,384]{1,0:T(8,128)(2,1)S(1)} %collective-permute-done.7.refs_1_, ...), custom_call_target="tpu_custom_call" | custom-call | flops 327155712 | bytes 7346176 | tf_op jit(solution)/shard_map/other_features/pallas_call | solution.py:44
  19.5 0.0 slice-start.1
  19.5 2.1 %attend.1 = (bf16[128,768]{1,0:T(8,128)(2,1)S(1)}, bf16[128,768]{1,0:T(8,128)(2,1)S(1)}, bf16[128,1536]{1,0:T(8,128)(2,1)S(1)}) custom-call(bf16[256,384]{1,0:T(8,128)(2,1)S(1)} %collective-permute-done.refs_0_, bf16[256,384]{1,0:T(8,128)(2,1)S(1)} %collective-permute-done.5.refs_1_, bf16[512,512]{1,0:T(8,128)(2,1)S(1)} %get-tuple-element.72.refs_2_, ...), custom_call_target="tpu_custom_call" | custom-call | flops 528482304 | bytes 9345024 | tf_op jit(solution)/shard_map/attend/pallas_call | solution.py:44
  21.6 1.6 %collective-permute-start.12 = (bf16[128,768]{1,0:T(8,128)(2,1)S(1)}, bf16[128,768]{1,0:T(8,128)(2,1)S(1)}, u32[]{:S(2)}, u32[]{:S(2)}) collective-permute-start(bf16[128,768]{1,0:T(8,128)(2,1)S(1)} %get-tuple-element.86.refs_0_), channel_id=1, source_target_pairs={{0,1},{1,0},{2,3},{3,2},{4,5},{5,4},{6,7},{7,6},{8,9},{9,8},{10,11... | collective-permute-start | bytes 589832 | tf_op jit(solution)/shard_map/ppermute | solution.py:23
  23.1 0.3 second_share.1.refs_0_
  23.5 0.6 %collective-permute-start.11 = (bf16[128,768]{1,0:T(8,128)(2,1)S(1)}, bf16[128,768]{1,0:T(8,128)(2,1)S(1)}, u32[]{:S(2)}, u32[]{:S(2)}) collective-permute-start(bf16[128,768]{1,0:T(8,128)(2,1)S(1)} %second_share.1.refs_0_), channel_id=1, source_target_pairs={{0,1},{1,0},{2,3},{3,2},{4,5},{5,4},{6,7},{7,6},{8,9},{9,8},{10,11... | collective-permute-start | bytes 589832 | tf_op jit(solution)/shard_map/ppermute | solution.py:23
  24.1 0.6 %copy.13 = bf16[1536,2,768]{2,0,1:T(8,128)(2,1)S(1)} copy(bf16[1536,2,768]{2,1,0:T(2,128)(2,1)S(1)} %bitcast.10) | data formatting | bytes 9437184 | tf_op jit(solution)/shard_map/optimization_barrier | solution.py:585
  24.7 4.7 %collective-permute-done.12.refs_1_ = bf16[128,768]{1,0:T(8,128)(2,1)S(1)} collective-permute-done((bf16[128,768]{1,0:T(8,128)(2,1)S(1)}, bf16[128,768]{1,0:T(8,128)(2,1)S(1)}, u32[]{:S(2)}, u32[]{:S(2)}) %collective-permute-start.12) | collective-permute-done | bytes 196640 | tf_op jit(solution)/shard_map/ppermute | solution.py:23
  29.4 0.5 %first_tracks.1 = (f32[128,1]{1,0:T(8,128)S(1)}, f32[128,768]{1,0:T(8,128)S(1)}, f32[128,768]{1,0:T(8,128)S(1)}) custom-call(bf16[128,768]{1,0:T(8,128)(2,1)S(1)} %get-tuple-element.86.refs_0_, bf16[128,768]{1,0:T(8,128)(2,1)S(1)} %collective-permute-done.12.refs_1_, bf16[128,1536]{1,0:T(8,128)(2,1)S(1)} %get-tuple-element.83.refs_2_, ...), custom_call_target="tpu_custom_call" | custom-call | flops 301989888 | bytes 6363136 | tf_op jit(solution)/shard_map/first_tracks/pallas_call | solution.py:44
  29.9 2.9 %collective-permute-done.11.refs_1_ = bf16[128,768]{1,0:T(8,128)(2,1)S(1)} collective-permute-done((bf16[128,768]{1,0:T(8,128)(2,1)S(1)}, bf16[128,768]{1,0:T(8,128)(2,1)S(1)}, u32[]{:S(2)}, u32[]{:S(2)}) %collective-permute-start.11) | collective-permute-done | bytes 196640 | tf_op jit(solution)/shard_map/ppermute | solution.py:23
  32.8 0.5 %sent_tracks.1 = (bf16[128,768]{1,0:T(8,128)(2,1)S(1)}, bf16[128,768]{1,0:T(8,128)(2,1)S(1)}, f32[128,1]{1,0:T(8,128)S(1)}) custom-call(bf16[128,768]{1,0:T(8,128)(2,1)S(1)} %second_share.1.refs_0_, bf16[128,768]{1,0:T(8,128)(2,1)S(1)} %collective-permute-done.11.refs_1_, bf16[128,1536]{1,0:T(8,128)(2,1)S(1)} %get-tuple-element.83.refs_2_, ...), custom_call_target="tpu_custom_call" | custom-call | flops 150994944 | bytes 6428672 | tf_op jit(solution)/shard_map/sent_tracks/pallas_call | solution.py:44
  33.3 0.1 collective-permute-start.13
  33.4 0.1 copy-done
  33.5 0.5 %kept_tracks.1.kept = bf16[128,768]{1,0:T(8,128)(2,1)S(1)} custom-call(bf16[128,768]{1,0:T(8,128)(2,1)S(1)} %get-tuple-element.89.gained, bf16[2,1536,768]{2,1,0:T(8,128)(2,1)S(1)} %bitcast.8, f32[128,768]{1,0:T(8,128)S(1)} %get-tuple-element.90.to_keep, f32[128,1]{1,0:T(8,128)S(1)} %get-tuple-element.91.scale), custom_call_target="tpu_custom_call" | custom-call | flops 150994944 | bytes 5570560 | tf_op jit(solution)/shard_map/kept_tracks/pallas_call | solution.py:44
  33.9 0.9 %collective-permute-done.13.received = bf16[128,768]{1,0:T(8,128)(2,1)S(1)} collective-permute-done((bf16[128,768]{1,0:T(8,128)(2,1)S(1)}, bf16[128,768]{1,0:T(8,128)(2,1)S(1)}, u32[]{:S(2)}, u32[]{:S(2)}) %collective-permute-start.13) | collective-permute-done | bytes 196640 | tf_op jit(solution)/shard_map/ppermute | solution.py:23
  34.8 0.9 %average.1 = f32[128,768]{1,0:T(8,128)} custom-call(bf16[128,768]{1,0:T(8,128)(2,1)S(1)} %kept_tracks.1.kept, bf16[128,768]{1,0:T(8,128)(2,1)S(1)} %collective-permute-done.13.received, s32[1,768]{1,0:T(1,128)S(1)} %reshape.7.pairs), custom_call_target="tpu_custom_call" | custom-call | bytes 1182720 | tf_op jit(solution)/shard_map/average/pallas_call | solution.py:44
  (16 shorter events, 0.0 us)
Async XLA Ops:
  1.2 7.2 %collective-permute-start.2 = (bf16[160,384]{1,0:T(8,128)(2,1)S(1)}, bf16[160,384]{1,0:T(8,128)(2,1)S(1)}, u32[]{:S(2)}, u32[]{:S(2)}) collective-permute-start(bf16[160,384]{1,0:T(8,128)(2,1)S(1)} %get-tuple-element.53), channel_id=1, source_target_pairs={{0,1},{1,0},{2,3},{3,2},{4,5},{5,4},{6,7},{7,6},{8,9},{9,8},{10,11... | collective-permute-start | bytes 368648 | tf_op jit(solution)/shard_map/ppermute | solution.py:23
  4.2 10.1 %collective-permute-start.6 = (bf16[256,384]{1,0:T(8,128)(2,1)S(1)}, bf16[256,384]{1,0:T(8,128)(2,1)S(1)}, u32[]{:S(2)}, u32[]{:S(2)}) collective-permute-start(bf16[256,384]{1,0:T(8,128)(2,1)S(1)} %get-tuple-element.58), channel_id=1, source_target_pairs={{0,1},{1,0},{2,3},{3,2},{4,5},{5,4},{6,7},{7,6},{8,9},{9,8},{10,11... | collective-permute-start | bytes 589832 | tf_op jit(solution)/shard_map/ppermute | solution.py:23
  4.2 12.2 %collective-permute-start = (bf16[256,384]{1,0:T(8,128)(2,1)S(1)}, bf16[256,384]{1,0:T(8,128)(2,1)S(1)}, u32[]{:S(2)}, u32[]{:S(2)}) collective-permute-start(bf16[256,384]{1,0:T(8,128)(2,1)S(1)} %get-tuple-element.49), channel_id=1, source_target_pairs={{0,1},{1,0},{2,3},{3,2},{4,5},{5,4},{6,7},{7,6},{8,9},{9,8},{10,11... | collective-permute-start | bytes 589832 | tf_op jit(solution)/shard_map/ppermute | solution.py:23
  8.3 3.7 %collective-permute-start.3 = (bf16[160,384]{1,0:T(8,128)(2,1)S(1)}, bf16[160,384]{1,0:T(8,128)(2,1)S(1)}, u32[]{:S(2)}, u32[]{:S(2)}) collective-permute-start(bf16[160,384]{1,0:T(8,128)(2,1)S(1)} %collective-permute-done.2.refs_6_), channel_id=1, source_target_pairs={{0,2},{2,0},{1,3},{3,1},{4,6},{6,4},{5,7},{7,5},{8,10},{10,8},{9,1... | collective-permute-start | bytes 368648 | tf_op jit(solution)/shard_map/ppermute | solution.py:23
  8.3 6.1 %collective-permute-start.8 = (bf16[160,384]{1,0:T(8,128)(2,1)S(1)}, bf16[160,384]{1,0:T(8,128)(2,1)S(1)}, u32[]{:S(2)}, u32[]{:S(2)}) collective-permute-start(bf16[160,384]{1,0:T(8,128)(2,1)S(1)} %collective-permute-done.2.refs_6_), channel_id=1, source_target_pairs={{0,16},{16,0},{1,17},{17,1},{2,18},{18,2},{3,19},{19,3},{4,20},{20... | collective-permute-start | bytes 368648 | tf_op jit(solution)/shard_map/ppermute | solution.py:23
  10.4 6.0 %collective-permute-start.1 = (bf16[128,128]{1,0:T(8,128)(2,1)S(1)}, bf16[128,128]{1,0:T(8,128)(2,1)S(1)}, u32[]{:S(2)}, u32[]{:S(2)}) collective-permute-start(bf16[128,128]{1,0:T(8,128)(2,1)S(1)} %get-tuple-element.56.refs_0_), channel_id=1, source_target_pairs={{0,4},{2,10},{4,8},{6,14},{8,12},{10,2},{12,0},{14,6},{1,5},{3,11}... | collective-permute-start | bytes 98312 | tf_op jit(solution)/shard_map/ppermute | solution.py:490
  12.0 4.6 %collective-permute-start.4 = (bf16[128,128]{1,0:T(8,128)(2,1)S(1)}, bf16[128,128]{1,0:T(8,128)(2,1)S(1)}, u32[]{:S(2)}, u32[]{:S(2)}) collective-permute-start(bf16[128,128]{1,0:T(8,128)(2,1)S(1)} %get-tuple-element.56.refs_0_), channel_id=1, source_target_pairs={{0,12},{4,0},{8,4},{12,8},{1,13},{5,1},{9,5},{13,9},{2,14},{6,2},{... | collective-permute-start | bytes 98312 | tf_op jit(solution)/shard_map/ppermute | solution.py:23
  14.2 3.9 %collective-permute-start.7 = (bf16[256,384]{1,0:T(8,128)(2,1)S(1)}, bf16[256,384]{1,0:T(8,128)(2,1)S(1)}, u32[]{:S(2)}, u32[]{:S(2)}) collective-permute-start(bf16[256,384]{1,0:T(8,128)(2,1)S(1)} %collective-permute-done.6.refs_0_), channel_id=1, source_target_pairs={{0,2},{2,0},{1,3},{3,1},{4,6},{6,4},{5,7},{7,5},{8,10},{10,8},{9,1... | collective-permute-start | bytes 589832 | tf_op jit(solution)/shard_map/ppermute | solution.py:23
  14.4 2.7 %collective-permute-start.9 = (bf16[160,384]{1,0:T(8,128)(2,1)S(1)}, bf16[160,384]{1,0:T(8,128)(2,1)S(1)}, u32[]{:S(2)}, u32[]{:S(2)}) collective-permute-start(bf16[160,384]{1,0:T(8,128)(2,1)S(1)} %collective-permute-done.8.refs_8_), channel_id=1, source_target_pairs={{0,2},{2,0},{1,3},{3,1},{4,6},{6,4},{5,7},{7,5},{8,10},{10,8},{9,1... | collective-permute-start | bytes 368648 | tf_op jit(solution)/shard_map/ppermute | solution.py:23
  16.6 2.9 %collective-permute-start.5 = (bf16[256,384]{1,0:T(8,128)(2,1)S(1)}, bf16[256,384]{1,0:T(8,128)(2,1)S(1)}, u32[]{:S(2)}, u32[]{:S(2)}) collective-permute-start(bf16[256,384]{1,0:T(8,128)(2,1)S(1)} %collective-permute-done.refs_0_), channel_id=1, source_target_pairs={{0,2},{2,0},{1,3},{3,1},{4,6},{6,4},{5,7},{7,5},{8,10},{10,8},{9,1... | collective-permute-start | bytes 589832 | tf_op jit(solution)/shard_map/ppermute | solution.py:23
  16.7 1.5 %collective-permute-start.10 = (bf16[128,128]{1,0:T(8,128)(2,1)S(1)}, bf16[128,128]{1,0:T(8,128)(2,1)S(1)}, u32[]{:S(2)}, u32[]{:S(2)}) collective-permute-start(bf16[128,128]{1,0:T(8,128)(2,1)S(1)} %collective-permute-done.1.refs_1_), channel_id=1, source_target_pairs={{0,2},{2,0},{1,3},{3,1},{4,6},{6,4},{5,7},{7,5},{8,10},{10,8},{9,1... | collective-permute-start | bytes 98312 | tf_op jit(solution)/shard_map/ppermute | solution.py:23
  18.2 5.9 %slice-start = ((s8[4718592]{0:T(1024)(128)(4,1)}), s8[4194304]{0:T(1024)(128)(4,1)S(1)}, s32[]{:S(2)}) async-start(s8[4718592]{0:T(1024)(128)(4,1)} %bitcast.9), calls=%async_computation | async-start | bytes 8388608
  19.5 4.6 %slice-start.1 = ((s8[4718592]{0:T(1024)(128)(4,1)}), s8[524288]{0:T(1024)(128)(4,1)S(1)}, s32[]{:S(2)}) async-start(s8[4718592]{0:T(1024)(128)(4,1)} %bitcast.9), calls=%async_computation.1 | async-start | bytes 1048576
  21.6 7.8 %collective-permute-start.12 = (bf16[128,768]{1,0:T(8,128)(2,1)S(1)}, bf16[128,768]{1,0:T(8,128)(2,1)S(1)}, u32[]{:S(2)}, u32[]{:S(2)}) collective-permute-start(bf16[128,768]{1,0:T(8,128)(2,1)S(1)} %get-tuple-element.86.refs_0_), channel_id=1, source_target_pairs={{0,1},{1,0},{2,3},{3,2},{4,5},{5,4},{6,7},{7,6},{8,9},{9,8},{10,11... | collective-permute-start | bytes 589832 | tf_op jit(solution)/shard_map/ppermute | solution.py:23
  23.5 9.3 %collective-permute-start.11 = (bf16[128,768]{1,0:T(8,128)(2,1)S(1)}, bf16[128,768]{1,0:T(8,128)(2,1)S(1)}, u32[]{:S(2)}, u32[]{:S(2)}) collective-permute-start(bf16[128,768]{1,0:T(8,128)(2,1)S(1)} %second_share.1.refs_0_), channel_id=1, source_target_pairs={{0,1},{1,0},{2,3},{3,2},{4,5},{5,4},{6,7},{7,6},{8,9},{9,8},{10,11... | collective-permute-start | bytes 589832 | tf_op jit(solution)/shard_map/ppermute | solution.py:23
  32.8 0.7 %copy-start = (s32[768]{0:T(1024)S(1)}, s32[768]{0:T(1024)}, u32[]{:S(2)}) copy-start(s32[768]{0:T(1024)} %param.19) | copy-start | bytes 9220
  33.3 1.5 %collective-permute-start.13 = (bf16[128,768]{1,0:T(8,128)(2,1)S(1)}, bf16[128,768]{1,0:T(8,128)(2,1)S(1)}, u32[]{:S(2)}, u32[]{:S(2)}) collective-permute-start(bf16[128,768]{1,0:T(8,128)(2,1)S(1)} %get-tuple-element.92), channel_id=1, source_target_pairs={{0,2},{2,0},{1,3},{3,1},{4,6},{6,4},{5,7},{7,5},{8,10},{10,8},{9,1... | collective-permute-start | bytes 589832 | tf_op jit(solution)/shard_map/ppermute | solution.py:23

commit v7 on v6

--- a/solution.py
+++ b/solution.py
@@ -132,12 +132,14 @@
         copy.wait()
 
 
-def fetch_kernel(w_out, first_out, second_out, sems):
-    out_half = first_out.shape[1]
-    copies = [
-        pltpu.make_async_copy(w_out.at[:, pl.ds(0, out_half)], first_out, sems.at[0]),
-        pltpu.make_async_copy(w_out.at[:, pl.ds(out_half, out_half)], second_out, sems.at[1]),
-    ]
+def fetch_kernel(w_out, out, sems):
+    heads = w_out.shape[0] // VDIM
+    rest = VDIM - LANES
+    copies = []
+    for head in range(heads):
+        for begin, count, spot in ((0, LANES, head * LANES), (LANES, rest, heads * LANES + head * rest)):
+            source = w_out.at[pl.ds(head * VDIM + begin, count)]
+            copies.append(pltpu.make_async_copy(source, out.at[pl.ds(spot, count)], sems.at[len(copies)]))
     for copy in copies:
         copy.start()
     for copy in copies:
@@ -293,7 +295,7 @@
 
 def attend_kernel(steps, chunks, *refs):
     mine, theirs, onehot, kv_t, w_query, gain, square, kv_sum, q_sum = refs[:9]
-    own, cosine, sine, first_out = refs[9:13]
+    own, cosine, sine, out = refs[9:13]
     founds = refs[13 : 13 + len(steps) - 1]
     share, merged, inputs = refs[12 + len(steps) : 15 + len(steps)]
     table, squares, sums, queries, keys, values = refs[15 + len(steps) :]
@@ -322,18 +324,21 @@
 
     over_blocks(total, block, finish)
     scaled = queries[...] * lax.rsqrt(squares[:rows, :] / features + 1e-06)
-    for head in range(queries.shape[1] // KDIM):
+    heads = queries.shape[1] // KDIM
+    for head in range(heads):
         query = turn(scaled[:, head * KDIM : (head + 1) * KDIM], cosine[:rows, :], sine[:rows, :])
         scores = matmul_t(query, keys[...]) * KDIM ** (-0.5)
         weights = jnp.exp(scores - jnp.max(scores, axis=1, keepdims=True))
         weight_sum = jnp.sum(weights, axis=1, keepdims=True)
         found = (matmul(weights.astype(BF16), values[...]) / weight_sum).astype(BF16)
-        merged[:, head * VDIM : (head + 1) * VDIM] = found
-    share[...] = matmul(merged[...], first_out[...]).astype(BF16)
-
-
-def second_kernel(merged, second_out, share):
-    share[...] = matmul(merged[...], second_out[...]).astype(BF16)
+        merged[:, head * LANES : (head + 1) * LANES] = found[:, :LANES]
+        spot = heads * LANES + head * (VDIM - LANES)
+        merged[:, spot : spot + VDIM - LANES] = found[:, LANES:]
+    share[...] = matmul(merged[...], out[:, : share.shape[1]]).astype(BF16)
+
+
+def second_kernel(merged, out, share):
+    share[...] = matmul(merged[...], out[:, share.shape[1] :]).astype(BF16)
 
 
 def gather_hidden(shares, inputs, gain, chunk):
@@ -373,28 +378,34 @@
     scale_out[...] = scale
 
 
-def keep_kernel(gained, tracks, to_keep, scale, kept):
+def swap_pairs(values, pairs):
+    even = lax.broadcasted_iota(jnp.int32, (1, LANES), 1) % 2 == 0
+    parts = []
+    for begin in range(0, values.shape[1], LANES):
+        part = values[:, begin : begin + LANES]
+        swapped = (pairs[:, begin : begin + LANES] % 2 == 0) != even
+        partner = jnp.where(even, pltpu.roll(part, LANES - 1, 1), pltpu.roll(part, 1, 1))
+        parts.append(jnp.where(swapped, partner, part))
+    return jnp.concatenate(parts, axis=1)
+
+
+def keep_kernel(gained, tracks, to_keep, scale, pairs, kept):
     strand = lax.axis_index("strand")
     width = gained.shape[1]
     logits = to_keep[...] + matmul(gained[...], tracks[strand, width:, :])
-    kept[...] = soft(logits * scale[...]).astype(BF16)
+    found = soft(logits * scale[...]).astype(BF16).astype(F32)
+    kept[...] = jnp.where(strand == 0, found, swap_pairs(found, pairs)).astype(BF16)
 
 
 def average_kernel(parts, kept, received, pairs, out, stage, sems):
     strand = lax.axis_index("strand")
-    count = kept.shape[1]
     rows = kept.shape[0] // parts
-    index = lax.broadcasted_iota(jnp.int32, (1, count), 1)
-    even = index % 2 == 0
-    swapped = (pairs[...] % 2 == 0) != even
     copies = []
     for i in range(parts):
         here = slice(i * rows, (i + 1) * rows)
-        mine, theirs = kept[here, :].astype(F32), received[here, :].astype(F32)
-        forward = jnp.where(strand == 0, mine, theirs)
-        reverse = jnp.where(strand == 0, theirs, mine)
-        partner = jnp.where(even, pltpu.roll(reverse, count - 1, 1), pltpu.roll(reverse, 1, 1))
-        stage[here, :] = 0.5 * (forward + jnp.where(swapped, partner, reverse))
+        theirs = received[here, :].astype(F32)
+        theirs = jnp.where(strand == 0, swap_pairs(theirs, pairs), theirs)
+        stage[here, :] = 0.5 * (kept[here, :].astype(F32) + theirs)
         copies.append(pltpu.make_async_copy(stage.at[here], out.at[here], sems.at[i]))
         copies[-1].start()
     for copy in copies:
@@ -471,15 +482,12 @@
     if from_heads:
         from_heads[0], table = lax.optimization_barrier((from_heads[0], table))
     to_core = [shifted(here, "strand", 1) for here in from_heads]
-    out_in = w_out
-    if to_core:
-        out_in = w_out
-    first_out, second_out = call(
+    (out_here,) = call(
         fetch_kernel,
-        [shape((w_out.shape[0], features // 2), BF16)] * 2,
-        [out_in],
+        [shape(w_out.shape, BF16)],
+        [w_out],
         "fetch_out",
-        scratch=[pltpu.SemaphoreType.DMA((2,))],
+        scratch=[pltpu.SemaphoreType.DMA((2 * (q_cols // KDIM),))],
         spaces=[hbm],
     )
     raw = []
@@ -493,7 +501,7 @@
                 own_codes, to_core[0] = lax.optimization_barrier((own_codes, to_core[0]))
             raw.append(shifted(own_codes, "pos", k))
     if raw:
-        raw[0], first_out = lax.optimization_barrier((raw[0], first_out))
+        raw[0], out_here = lax.optimization_barrier((raw[0], out_here))
     for step in range(1, size):
         for k in range(groups):
             here = from_heads[step - 1] if k == 0 else shifted(from_heads[step - 1], "groups", k)
@@ -560,7 +568,7 @@
             shape((rows, o_cols), BF16),
             shape((rows, features), BF16),
         ],
-        list(pieces[-1]) + [onehot, kv_t, query_own, gain] + state + [own, cosine, sine, first_out] + founds,
+        list(pieces[-1]) + [onehot, kv_t, query_own, gain] + state + [own, cosine, sine, out_here] + founds,
         "attend",
         scratch=[
             pltpu.VMEM((entries, wide), BF16),
@@ -576,7 +584,7 @@
     (share_two,) = call(
         second_kernel,
         [shape((rows, features // 2), BF16)],
-        [merged, second_out],
+        [merged, out_here],
         "second_share",
         flops=rows * o_cols * features,
     )
@@ -607,17 +615,18 @@
         flops=rows * features * tracks_half,
     )
     received = shifted(sent, "strand", 1)
+    pairs = track_pairs.reshape(1, tracks_half)
     (kept,) = call(
         keep_kernel,
         [shape((rows, tracks_half), BF16)],
-        [gained, tracks, to_keep, scale],
+        [gained, tracks, to_keep, scale, pairs],
         "kept_tracks",
         flops=rows * features * tracks_half,
     )
     (out,) = call(
         functools.partial(average_kernel, 4),
         [shape((rows, tracks_half), F32)],
-        [kept, received, track_pairs.reshape(1, tracks_half)],
+        [kept, received, pairs],
         "average",
         scratch=[pltpu.VMEM((rows, tracks_half), F32), pltpu.SemaphoreType.DMA((4,))],
         out_space=hbm,

time: 35.9 us -> 35.9 us (level)
  transfers between devices with their start and end apart: 14 -> 14, of which waited for: 6 -> 6; matrix products, arithmetic and copies ran while one was open for 2% -> 2% of each run, Pallas kernels for 20% -> 21%
where the time goes in v7:
time: 35.9 us; the launch traced here: 35.6 us
  starting transfers between devices  14 us (39%)
  Pallas kernels  11.9 us (33%)
  waiting for transfers between devices  8.85 us (25%)
  local copies, waits for them, and re-layouts  0.73 us (2%)
    ppermute x13, starting transfers between devices, shifted(): lax.ppermute(value, axis, [(i, (i + distance) % size) for i in range(size)])  12.5 us
    pallas_call x11, Pallas kernels, call(): pl.pallas_call(kernel, out_shape=list(outs), in_specs=specs, out_specs=[p...  11.9 us
    ppermute x13, waiting for transfers between devices, shifted(): lax.ppermute(value, axis, [(i, (i + distance) % size) for i in range(size)])  8.85 us
    ppermute x1, starting transfers between devices, body(): raw.append(lax.ppermute(own_codes, ('pos', 'strand'), pairs))  1.58 us
  transfers between devices with their start and end apart: 14, of which 6 were waited for; matrix products, arithmetic and copies ran while one was open for 2% of the time, Pallas kernels for 21%

profile of v7, /device:TPU:0, one launch (start us, length us, event | category | flops | bytes accessed | tf_op | source)
XLA Modules:
  0.0 35.6 jit_solution(17712011712750494544)
XLA Ops:
  0.0 1.1 %stage.1 = (bf16[160,384]{1,0:T(8,128)(2,1)S(1)}, bf16[256,384]{1,0:T(8,128)(2,1)S(1)}, bf16[256,384]{1,0:T(8,128)(2,1)S(1)}, bf16[128,128]{1,0:T(8,128)(2,1)S(1)}) custom-call(bf16[512,768]{1,0:T(8,128)(2,1)} %embed.3, bf16[64,1536]{1,0:T(8,128)(2,1)} %bitcast.13, bf16[96,1536]{1,0:T(8,128)(2,1)} %bitcast.11, s32[128,128]{1,0:T(8,128)} %bitcast.15), custom_call_target="tpu_custom_call" | custom-call | bytes 614400 | tf_op jit(solution)/shard_map/stage/pallas_call | solution.py:44
  1.2 3.0 %collective-permute-start.2 = (bf16[160,384]{1,0:T(8,128)(2,1)S(1)}, bf16[160,384]{1,0:T(8,128)(2,1)S(1)}, u32[]{:S(2)}, u32[]{:S(2)}) collective-permute-start(bf16[160,384]{1,0:T(8,128)(2,1)S(1)} %get-tuple-element.50), channel_id=1, source_target_pairs={{0,1},{1,0},{2,3},{3,2},{4,5},{5,4},{6,7},{7,6},{8,9},{9,8},{10,11... | collective-permute-start | bytes 368648 | tf_op jit(solution)/shard_map/ppermute | solution.py:23
  4.2 0.1 collective-permute-start.6
  4.2 1.9 %collective-permute-start = (bf16[256,384]{1,0:T(8,128)(2,1)S(1)}, bf16[256,384]{1,0:T(8,128)(2,1)S(1)}, u32[]{:S(2)}, u32[]{:S(2)}) collective-permute-start(bf16[256,384]{1,0:T(8,128)(2,1)S(1)} %get-tuple-element.47), channel_id=1, source_target_pairs={{0,1},{1,0},{2,3},{3,2},{4,5},{5,4},{6,7},{7,6},{8,9},{9,8},{10,11... | collective-permute-start | bytes 589832 | tf_op jit(solution)/shard_map/ppermute | solution.py:23
  6.2 1.9 %prepare.1 = (bf16[512,768]{1,0:T(8,128)(2,1)S(1)}, bf16[64,1536]{1,0:T(8,128)(2,1)S(1)}, bf16[96,1536]{1,0:T(8,128)(2,1)S(1)}, bf16[1536,512]{1,0:T(8,128)(2,1)...) custom-call(bf16[512,768]{1,0:T(8,128)(2,1)} %embed.3, ...), custom_call_target="tpu_custom_call" | custom-call | bytes 3399680 | tf_op jit(solution)/shard_map/prepare/pallas_call | solution.py:44
  8.1 0.2 collective-permute-done.2.refs_6_
  8.3 2.1 %collective-permute-start.8 = (bf16[160,384]{1,0:T(8,128)(2,1)S(1)}, bf16[160,384]{1,0:T(8,128)(2,1)S(1)}, u32[]{:S(2)}, u32[]{:S(2)}) collective-permute-start(bf16[160,384]{1,0:T(8,128)(2,1)S(1)} %collective-permute-done.2.refs_6_), channel_id=1, source_target_pairs={{0,16},{16,0},{1,17},{17,1},{2,18},{18,2},{3,19},{19,3},{4,20},{20... | collective-permute-start | bytes 368648 | tf_op jit(solution)/shard_map/ppermute | solution.py:23
  10.4 1.6 %collective-permute-start.1 = (bf16[128,128]{1,0:T(8,128)(2,1)S(1)}, bf16[128,128]{1,0:T(8,128)(2,1)S(1)}, u32[]{:S(2)}, u32[]{:S(2)}) collective-permute-start(bf16[128,128]{1,0:T(8,128)(2,1)S(1)} %get-tuple-element.53.refs_0_), channel_id=1, source_target_pairs={{0,4},{2,10},{4,8},{6,14},{8,12},{10,2},{12,0},{14,6},{1,5},{3,11}... | collective-permute-start | bytes 98312 | tf_op jit(solution)/shard_map/ppermute | solution.py:498
  12.0 2.2 %collective-permute-start.4 = (bf16[128,128]{1,0:T(8,128)(2,1)S(1)}, bf16[128,128]{1,0:T(8,128)(2,1)S(1)}, u32[]{:S(2)}, u32[]{:S(2)}) collective-permute-start(bf16[128,128]{1,0:T(8,128)(2,1)S(1)} %get-tuple-element.53.refs_0_), channel_id=1, source_target_pairs={{0,12},{4,0},{8,4},{12,8},{1,13},{5,1},{9,5},{13,9},{2,14},{6,2},{... | collective-permute-start | bytes 98312 | tf_op jit(solution)/shard_map/ppermute | solution.py:23
  14.2 0.2 collective-permute-done.8.refs_8_
  14.4 0.4 collective-permute-start.9
  14.7 1.7 %fetch_out.1.refs_12_.out = bf16[768,1536]{1,0:T(8,128)(2,1)S(1)} custom-call(bf16[768,1536]{1,0:T(8,128)(2,1)} %w_out.1), custom_call_target="tpu_custom_call" | custom-call | bytes 2359296 | tf_op jit(solution)/shard_map/fetch_out/pallas_call | solution.py:44
  16.5 0.1 collective-permute-done.4.refs_2_
  16.6 0.1 collective-permute-start.5
  16.7 0.4 %collective-permute-start.10 = (bf16[128,128]{1,0:T(8,128)(2,1)S(1)}, bf16[128,128]{1,0:T(8,128)(2,1)S(1)}, u32[]{:S(2)}, u32[]{:S(2)}) collective-permute-start(bf16[128,128]{1,0:T(8,128)(2,1)S(1)} %collective-permute-done.1.refs_1_), channel_id=1, source_target_pairs={{0,2},{2,0},{1,3},{3,1},{4,6},{6,4},{5,7},{7,5},{8,10},{10,8},{9,1... | collective-permute-start | bytes 98312 | tf_op jit(solution)/shard_map/ppermute | solution.py:23
  17.1 1.1 %own_features.1 = (bf16[384,512]{1,0:T(8,128)(2,1)S(1)}, bf16[320,1536]{1,0:T(8,128)(2,1)S(1)}, bf16[128,768]{1,0:T(8,128)(2,1)S(1)}, f32[384,1]{1,0:T(8,128)S(1...) custom-call(bf16[128,128]{1,0:T(8,128)(2,1)S(1)} %get-tuple-element.53.refs_0_, ...), custom_call_target="tpu_custom_call" | custom-call | flops 490733568 | bytes 6068224 | tf_op jit(solution)/shard_map/own_features/pallas_call | solution.py:44
  18.2 1.3 %other_features.1 = (bf16[512,512]{1,0:T(8,128)(2,1)S(1)}, bf16[128,384]{1,0:T(8,128)(2,1)S(1)}, f32[512,1]{1,0:T(8,128)S(1)}, f32[512,320]{1,0:T(8,128)S(1)}, f32[128,512]{1,0:T(8,128)S(1)}) custom-call(bf16[256,384]{1,0:T(8,128)(2,1)S(1)} %collective-permute-done.6.refs_0_, bf16[256,384]{1,0:T(8,128)(2,1)S(1)} %collective-permute-done.7.refs_1_, ...), custom_call_target="tpu_custom_call" | custom-call | flops 327155712 | bytes 7346176 | tf_op jit(solution)/shard_map/other_features/pallas_call | solution.py:44
  19.5 0.0 slice-start
  19.5 2.0 %attend.1 = (bf16[128,768]{1,0:T(8,128)(2,1)S(1)}, bf16[128,768]{1,0:T(8,128)(2,1)S(1)}, bf16[128,1536]{1,0:T(8,128)(2,1)S(1)}) custom-call(bf16[256,384]{1,0:T(8,128)(2,1)S(1)} %collective-permute-done.refs_0_, bf16[256,384]{1,0:T(8,128)(2,1)S(1)} %collective-permute-done.5.refs_1_, bf16[512,512]{1,0:T(8,128)(2,1)S(1)} %get-tuple-element.69.refs_2_, ...), custom_call_target="tpu_custom_call" | custom-call | flops 528482304 | bytes 10524672 | tf_op jit(solution)/shard_map/attend/pallas_call | solution.py:44
  21.5 1.6 %collective-permute-start.12 = (bf16[128,768]{1,0:T(8,128)(2,1)S(1)}, bf16[128,768]{1,0:T(8,128)(2,1)S(1)}, u32[]{:S(2)}, u32[]{:S(2)}) collective-permute-start(bf16[128,768]{1,0:T(8,128)(2,1)S(1)} %get-tuple-element.82.refs_0_), channel_id=1, source_target_pairs={{0,1},{1,0},{2,3},{3,2},{4,5},{5,4},{6,7},{7,6},{8,9},{9,8},{10,11... | collective-permute-start | bytes 589832 | tf_op jit(solution)/shard_map/ppermute | solution.py:23
  23.1 0.3 second_share.1.refs_0_
  23.4 0.6 %collective-permute-start.11 = (bf16[128,768]{1,0:T(8,128)(2,1)S(1)}, bf16[128,768]{1,0:T(8,128)(2,1)S(1)}, u32[]{:S(2)}, u32[]{:S(2)}) collective-permute-start(bf16[128,768]{1,0:T(8,128)(2,1)S(1)} %second_share.1.refs_0_), channel_id=1, source_target_pairs={{0,1},{1,0},{2,3},{3,2},{4,5},{5,4},{6,7},{7,6},{8,9},{9,8},{10,11... | collective-permute-start | bytes 589832 | tf_op jit(solution)/shard_map/ppermute | solution.py:23
  24.0 0.6 %copy.13 = bf16[1536,2,768]{2,0,1:T(8,128)(2,1)S(1)} copy(bf16[1536,2,768]{2,1,0:T(2,128)(2,1)S(1)} %bitcast.10) | data formatting | bytes 9437184 | tf_op jit(solution)/shard_map/optimization_barrier | solution.py:593
  24.6 4.7 %collective-permute-done.12.refs_1_ = bf16[128,768]{1,0:T(8,128)(2,1)S(1)} collective-permute-done((bf16[128,768]{1,0:T(8,128)(2,1)S(1)}, bf16[128,768]{1,0:T(8,128)(2,1)S(1)}, u32[]{:S(2)}, u32[]{:S(2)}) %collective-permute-start.12) | collective-permute-done | bytes 196640 | tf_op jit(solution)/shard_map/ppermute | solution.py:23
  29.4 0.5 %first_tracks.1 = (f32[128,1]{1,0:T(8,128)S(1)}, f32[128,768]{1,0:T(8,128)S(1)}, f32[128,768]{1,0:T(8,128)S(1)}) custom-call(bf16[128,768]{1,0:T(8,128)(2,1)S(1)} %get-tuple-element.82.refs_0_, bf16[128,768]{1,0:T(8,128)(2,1)S(1)} %collective-permute-done.12.refs_1_, bf16[128,1536]{1,0:T(8,128)(2,1)S(1)} %get-tuple-element.79.refs_2_, ...), custom_call_target="tpu_custom_call" | custom-call | flops 301989888 | bytes 6363136 | tf_op jit(solution)/shard_map/first_tracks/pallas_call | solution.py:44
  29.8 2.9 %collective-permute-done.11.refs_1_ = bf16[128,768]{1,0:T(8,128)(2,1)S(1)} collective-permute-done((bf16[128,768]{1,0:T(8,128)(2,1)S(1)}, bf16[128,768]{1,0:T(8,128)(2,1)S(1)}, u32[]{:S(2)}, u32[]{:S(2)}) %collective-permute-start.11) | collective-permute-done | bytes 196640 | tf_op jit(solution)/shard_map/ppermute | solution.py:23
  32.7 0.5 %sent_tracks.1 = (bf16[128,768]{1,0:T(8,128)(2,1)S(1)}, bf16[128,768]{1,0:T(8,128)(2,1)S(1)}, f32[128,1]{1,0:T(8,128)S(1)}) custom-call(bf16[128,768]{1,0:T(8,128)(2,1)S(1)} %second_share.1.refs_0_, bf16[128,768]{1,0:T(8,128)(2,1)S(1)} %collective-permute-done.11.refs_1_, bf16[128,1536]{1,0:T(8,128)(2,1)S(1)} %get-tuple-element.79.refs_2_, ...), custom_call_target="tpu_custom_call" | custom-call | flops 150994944 | bytes 6428672 | tf_op jit(solution)/shard_map/sent_tracks/pallas_call | solution.py:44
  33.2 0.1 collective-permute-start.13
  33.3 0.1 copy-done
  33.4 0.6 %kept_tracks.1.kept = bf16[128,768]{1,0:T(8,128)(2,1)S(1)} custom-call(bf16[128,768]{1,0:T(8,128)(2,1)S(1)} %get-tuple-element.85.gained, bf16[2,1536,768]{2,1,0:T(8,128)(2,1)S(1)} %bitcast.8, f32[128,768]{1,0:T(8,128)S(1)} %get-tuple-element.86.to_keep, f32[128,1]{1,0:T(8,128)S(1)} %get-tuple-element.87.scale, s32[1,768]{1,0:T(1,128)S(1)} %reshape.7.pairs), custom_call_target="tpu_custom_call" | custom-call | flops 150994944 | bytes 5573632 | tf_op jit(solution)/shard_map/kept_tracks/pallas_call | solution.py:44
  34.0 0.7 %collective-permute-done.13.received = bf16[128,768]{1,0:T(8,128)(2,1)S(1)} collective-permute-done((bf16[128,768]{1,0:T(8,128)(2,1)S(1)}, bf16[128,768]{1,0:T(8,128)(2,1)S(1)}, u32[]{:S(2)}, u32[]{:S(2)}) %collective-permute-start.13) | collective-permute-done | bytes 196640 | tf_op jit(solution)/shard_map/ppermute | solution.py:23
  34.7 0.9 %average.1 = f32[128,768]{1,0:T(8,128)} custom-call(bf16[128,768]{1,0:T(8,128)(2,1)S(1)} %kept_tracks.1.kept, bf16[128,768]{1,0:T(8,128)(2,1)S(1)} %collective-permute-done.13.received, s32[1,768]{1,0:T(1,128)S(1)} %reshape.7.pairs), custom_call_target="tpu_custom_call" | custom-call | bytes 1182720 | tf_op jit(solution)/shard_map/average/pallas_call | solution.py:44
  (16 shorter events, 0.0 us)
Async XLA Ops:
  1.2 7.2 %collective-permute-start.2 = (bf16[160,384]{1,0:T(8,128)(2,1)S(1)}, bf16[160,384]{1,0:T(8,128)(2,1)S(1)}, u32[]{:S(2)}, u32[]{:S(2)}) collective-permute-start(bf16[160,384]{1,0:T(8,128)(2,1)S(1)} %get-tuple-element.50), channel_id=1, source_target_pairs={{0,1},{1,0},{2,3},{3,2},{4,5},{5,4},{6,7},{7,6},{8,9},{9,8},{10,11... | collective-permute-start | bytes 368648 | tf_op jit(solution)/shard_map/ppermute | solution.py:23
  4.2 10.1 %collective-permute-start.6 = (bf16[256,384]{1,0:T(8,128)(2,1)S(1)}, bf16[256,384]{1,0:T(8,128)(2,1)S(1)}, u32[]{:S(2)}, u32[]{:S(2)}) collective-permute-start(bf16[256,384]{1,0:T(8,128)(2,1)S(1)} %get-tuple-element.55), channel_id=1, source_target_pairs={{0,1},{1,0},{2,3},{3,2},{4,5},{5,4},{6,7},{7,6},{8,9},{9,8},{10,11... | collective-permute-start | bytes 589832 | tf_op jit(solution)/shard_map/ppermute | solution.py:23
  4.2 12.2 %collective-permute-start = (bf16[256,384]{1,0:T(8,128)(2,1)S(1)}, bf16[256,384]{1,0:T(8,128)(2,1)S(1)}, u32[]{:S(2)}, u32[]{:S(2)}) collective-permute-start(bf16[256,384]{1,0:T(8,128)(2,1)S(1)} %get-tuple-element.47), channel_id=1, source_target_pairs={{0,1},{1,0},{2,3},{3,2},{4,5},{5,4},{6,7},{7,6},{8,9},{9,8},{10,11... | collective-permute-start | bytes 589832 | tf_op jit(solution)/shard_map/ppermute | solution.py:23
  8.3 3.7 %collective-permute-start.3 = (bf16[160,384]{1,0:T(8,128)(2,1)S(1)}, bf16[160,384]{1,0:T(8,128)(2,1)S(1)}, u32[]{:S(2)}, u32[]{:S(2)}) collective-permute-start(bf16[160,384]{1,0:T(8,128)(2,1)S(1)} %collective-permute-done.2.refs_6_), channel_id=1, source_target_pairs={{0,2},{2,0},{1,3},{3,1},{4,6},{6,4},{5,7},{7,5},{8,10},{10,8},{9,1... | collective-permute-start | bytes 368648 | tf_op jit(solution)/shard_map/ppermute | solution.py:23
  8.3 6.1 %collective-permute-start.8 = (bf16[160,384]{1,0:T(8,128)(2,1)S(1)}, bf16[160,384]{1,0:T(8,128)(2,1)S(1)}, u32[]{:S(2)}, u32[]{:S(2)}) collective-permute-start(bf16[160,384]{1,0:T(8,128)(2,1)S(1)} %collective-permute-done.2.refs_6_), channel_id=1, source_target_pairs={{0,16},{16,0},{1,17},{17,1},{2,18},{18,2},{3,19},{19,3},{4,20},{20... | collective-permute-start | bytes 368648 | tf_op jit(solution)/shard_map/ppermute | solution.py:23
  10.4 6.0 %collective-permute-start.1 = (bf16[128,128]{1,0:T(8,128)(2,1)S(1)}, bf16[128,128]{1,0:T(8,128)(2,1)S(1)}, u32[]{:S(2)}, u32[]{:S(2)}) collective-permute-start(bf16[128,128]{1,0:T(8,128)(2,1)S(1)} %get-tuple-element.53.refs_0_), channel_id=1, source_target_pairs={{0,4},{2,10},{4,8},{6,14},{8,12},{10,2},{12,0},{14,6},{1,5},{3,11}... | collective-permute-start | bytes 98312 | tf_op jit(solution)/shard_map/ppermute | solution.py:498
  12.0 4.6 %collective-permute-start.4 = (bf16[128,128]{1,0:T(8,128)(2,1)S(1)}, bf16[128,128]{1,0:T(8,128)(2,1)S(1)}, u32[]{:S(2)}, u32[]{:S(2)}) collective-permute-start(bf16[128,128]{1,0:T(8,128)(2,1)S(1)} %get-tuple-element.53.refs_0_), channel_id=1, source_target_pairs={{0,12},{4,0},{8,4},{12,8},{1,13},{5,1},{9,5},{13,9},{2,14},{6,2},{... | collective-permute-start | bytes 98312 | tf_op jit(solution)/shard_map/ppermute | solution.py:23
  14.2 3.9 %collective-permute-start.7 = (bf16[256,384]{1,0:T(8,128)(2,1)S(1)}, bf16[256,384]{1,0:T(8,128)(2,1)S(1)}, u32[]{:S(2)}, u32[]{:S(2)}) collective-permute-start(bf16[256,384]{1,0:T(8,128)(2,1)S(1)} %collective-permute-done.6.refs_0_), channel_id=1, source_target_pairs={{0,2},{2,0},{1,3},{3,1},{4,6},{6,4},{5,7},{7,5},{8,10},{10,8},{9,1... | collective-permute-start | bytes 589832 | tf_op jit(solution)/shard_map/ppermute | solution.py:23
  14.4 2.7 %collective-permute-start.9 = (bf16[160,384]{1,0:T(8,128)(2,1)S(1)}, bf16[160,384]{1,0:T(8,128)(2,1)S(1)}, u32[]{:S(2)}, u32[]{:S(2)}) collective-permute-start(bf16[160,384]{1,0:T(8,128)(2,1)S(1)} %collective-permute-done.8.refs_8_), channel_id=1, source_target_pairs={{0,2},{2,0},{1,3},{3,1},{4,6},{6,4},{5,7},{7,5},{8,10},{10,8},{9,1... | collective-permute-start | bytes 368648 | tf_op jit(solution)/shard_map/ppermute | solution.py:23
  16.6 2.9 %collective-permute-start.5 = (bf16[256,384]{1,0:T(8,128)(2,1)S(1)}, bf16[256,384]{1,0:T(8,128)(2,1)S(1)}, u32[]{:S(2)}, u32[]{:S(2)}) collective-permute-start(bf16[256,384]{1,0:T(8,128)(2,1)S(1)} %collective-permute-done.refs_0_), channel_id=1, source_target_pairs={{0,2},{2,0},{1,3},{3,1},{4,6},{6,4},{5,7},{7,5},{8,10},{10,8},{9,1... | collective-permute-start | bytes 589832 | tf_op jit(solution)/shard_map/ppermute | solution.py:23
  16.7 1.5 %collective-permute-start.10 = (bf16[128,128]{1,0:T(8,128)(2,1)S(1)}, bf16[128,128]{1,0:T(8,128)(2,1)S(1)}, u32[]{:S(2)}, u32[]{:S(2)}) collective-permute-start(bf16[128,128]{1,0:T(8,128)(2,1)S(1)} %collective-permute-done.1.refs_1_), channel_id=1, source_target_pairs={{0,2},{2,0},{1,3},{3,1},{4,6},{6,4},{5,7},{7,5},{8,10},{10,8},{9,1... | collective-permute-start | bytes 98312 | tf_op jit(solution)/shard_map/ppermute | solution.py:23
  19.5 4.6 %slice-start = ((s8[4718592]{0:T(1024)(128)(4,1)}), s8[4194304]{0:T(1024)(128)(4,1)S(1)}, s32[]{:S(2)}) async-start(s8[4718592]{0:T(1024)(128)(4,1)} %bitcast.9), calls=%async_computation | async-start | bytes 8388608
  19.5 4.5 %slice-start.1 = ((s8[4718592]{0:T(1024)(128)(4,1)}), s8[524288]{0:T(1024)(128)(4,1)S(1)}, s32[]{:S(2)}) async-start(s8[4718592]{0:T(1024)(128)(4,1)} %bitcast.9), calls=%async_computation.1 | async-start | bytes 1048576
  21.5 7.8 %collective-permute-start.12 = (bf16[128,768]{1,0:T(8,128)(2,1)S(1)}, bf16[128,768]{1,0:T(8,128)(2,1)S(1)}, u32[]{:S(2)}, u32[]{:S(2)}) collective-permute-start(bf16[128,768]{1,0:T(8,128)(2,1)S(1)} %get-tuple-element.82.refs_0_), channel_id=1, source_target_pairs={{0,1},{1,0},{2,3},{3,2},{4,5},{5,4},{6,7},{7,6},{8,9},{9,8},{10,11... | collective-permute-start | bytes 589832 | tf_op jit(solution)/shard_map/ppermute | solution.py:23
  23.4 9.3 %collective-permute-start.11 = (bf16[128,768]{1,0:T(8,128)(2,1)S(1)}, bf16[128,768]{1,0:T(8,128)(2,1)S(1)}, u32[]{:S(2)}, u32[]{:S(2)}) collective-permute-start(bf16[128,768]{1,0:T(8,128)(2,1)S(1)} %second_share.1.refs_0_), channel_id=1, source_target_pairs={{0,1},{1,0},{2,3},{3,2},{4,5},{5,4},{6,7},{7,6},{8,9},{9,8},{10,11... | collective-permute-start | bytes 589832 | tf_op jit(solution)/shard_map/ppermute | solution.py:23
  32.7 0.7 %copy-start = (s32[768]{0:T(1024)S(1)}, s32[768]{0:T(1024)}, u32[]{:S(2)}) copy-start(s32[768]{0:T(1024)} %param.19) | copy-start | bytes 9220
  33.2 1.5 %collective-permute-start.13 = (bf16[128,768]{1,0:T(8,128)(2,1)S(1)}, bf16[128,768]{1,0:T(8,128)(2,1)S(1)}, u32[]{:S(2)}, u32[]{:S(2)}) collective-permute-start(bf16[128,768]{1,0:T(8,128)(2,1)S(1)} %get-tuple-element.88), channel_id=1, source_target_pairs={{0,2},{2,0},{1,3},{3,1},{4,6},{6,4},{5,7},{7,5},{8,10},{10,8},{9,1... | collective-permute-start | bytes 589832 | tf_op jit(solution)/shard_map/ppermute | solution.py:23

commit v8 on v7

--- a/solution.py
+++ b/solution.py
@@ -244,7 +244,7 @@
     return (owner * chunks + index) * width
 
 
-def join_kernel(step, index, chunks, rows, late, *refs):
+def join_kernel(step, index, chunks, carry, rows, late, *refs):
     mine, theirs, onehot_in, kv_t, w_query, gain, square_in, kv_in, q_in, own_table = refs[:10]
     codes = refs[10 : 10 + late]
     onehot, found, square, kv_sum, q_sum, table, all_codes = refs[10 + late :]
@@ -261,27 +261,29 @@
     span = (early, late * rows)
     begin = lax.axis_index("heads") * own_width
     absorb(onehot, span, own_table, rows, begin, own_width, weights, None, (square, kv_sum, None))
-    table[:half, :] = mine[...]
-    table[half:, :] = theirs[...]
+    taken = width - carry
+    table[:half, :] = mine[:, :taken]
+    table[half:, :] = theirs[:, :taken]
     begin = chunk_start(step, index, chunks, width)
     span = (0, early + late * rows)
     sums = (square, kv_sum, q_sum)
-    found[...] = absorb(onehot, span, table, rows, begin, width, weights, (square, kv_sum, q_in), sums)
-
-
-def chunk_kernel(step, index, chunks, rows, *refs):
+    found[...] = absorb(onehot, span, table, rows, begin, taken, weights, (square, kv_sum, q_in), sums)
+
+
+def chunk_kernel(step, index, chunks, carry, rows, *refs):
     mine, theirs, onehot, kv_t, w_query, gain, square, kv_sum, q_sum = refs[:9]
     found, square_out, kv_out, q_out, table = refs[9:]
     half, width = mine.shape
-    table[:half, :] = mine[...]
-    table[half:, :] = theirs[...]
+    taken = width - carry
+    table[:half, :] = mine[:, :taken]
+    table[half:, :] = theirs[:, :taken]
     found[...] = absorb(
         onehot,
         (0, onehot.shape[0]),
         table,
         rows,
         chunk_start(step, index, chunks, width),
-        width,
+        taken,
         (kv_t, w_query, gain),
         (square, kv_sum, q_sum),
         (square_out, kv_out, q_out),
@@ -293,7 +295,9 @@
     return (floats * cosine + pltpu.roll(floats, KDIM // 2, 1) * sine).astype(BF16)
 
 
-def attend_kernel(steps, chunks, *refs):
+def attend_kernel(steps, chunks, carry, *refs):
+    if carry:
+        earlier, refs = refs[:2], refs[2:]
     mine, theirs, onehot, kv_t, w_query, gain, square, kv_sum, q_sum = refs[:9]
     own, cosine, sine, out = refs[9:13]
     founds = refs[13 : 13 + len(steps) - 1]
@@ -304,15 +308,18 @@
     features = inputs.shape[1]
     total = onehot.shape[0]
     block = block_of(total, rows)
-    table[:half, :] = mine[...]
-    table[half:, :] = theirs[...]
-    start = chunk_start(*steps[-1], chunks, width)
+    if carry:
+        table[:half, :carry] = earlier[0][:, width - carry :]
+        table[half:, :carry] = earlier[1][:, width - carry :]
+    table[:half, carry:] = mine[...]
+    table[half:, carry:] = theirs[...]
+    start = chunk_start(*steps[-1], chunks, width) - carry
     span, weights = (0, total), (kv_t, w_query, gain)
     before, after = (square, kv_sum, q_sum), (squares, sums, queries)
-    last = absorb(onehot, span, table, rows, start, width, weights, before, after)
-    inputs[:, pl.ds(pl.multiple_of(start, LANES), width)] = last
+    last = absorb(onehot, span, table, rows, start, width + carry, weights, before, after)
+    inputs[:, pl.ds(pl.multiple_of(start, LANES), width + carry)] = last
     for found, spot in zip(founds, steps):
-        inputs[:, pl.ds(pl.multiple_of(chunk_start(*spot, chunks, width), LANES), width)] = found[...]
+        inputs[:, pl.ds(pl.multiple_of(chunk_start(*spot, chunks, width), LANES), found.shape[1])] = found[...]
     begin = pl.multiple_of(lax.axis_index("heads") * own_width, LANES)
     inputs[:, pl.ds(begin, own_width)] = own[...]
 
@@ -438,6 +445,7 @@
     tracks_half = w_tracks.shape[2]
     chunks = 2 if width % (2 * LANES) == 0 else 1
     wide = width // chunks
+    carry = LANES if chunks == 2 and wide % (2 * LANES) and wide > LANES else 0
 
     early, late = [(0, 0)], []
     for k in range(1, blocks, 2):
@@ -536,16 +544,17 @@
     )
     founds = []
     for (step, i), pair in zip(steps[:-1], pieces[:-1]):
+        left = carry if step == size - 1 else 0
         operands = list(pair) + [onehot, kv_t, query_own, gain] + state
-        outs = [shape((rows, wide), BF16)] + sums_of(total)
-        scratch = [pltpu.VMEM((entries, wide), BF16)]
+        outs = [shape((rows, wide - left), BF16)] + sums_of(total)
+        scratch = [pltpu.VMEM((entries, wide - left), BF16)]
         if swapped:
-            kernel = functools.partial(join_kernel, step, i, chunks, rows, len(swapped))
+            kernel = functools.partial(join_kernel, step, i, chunks, left, rows, len(swapped))
             operands += [table] + swapped
             outs = [shape((total, entries), BF16)] + outs
             scratch.append(pltpu.VMEM((rows * len(swapped), BIN), BF16))
         else:
-            kernel = functools.partial(chunk_kernel, step, i, chunks, rows)
+            kernel = functools.partial(chunk_kernel, step, i, chunks, left, rows)
         results = call(
             kernel,
             outs,
@@ -562,16 +571,20 @@
         founds.append(found)
     o_cols = q_cols // KDIM * VDIM
     share_one, merged, inputs = call(
-        functools.partial(attend_kernel, steps, chunks),
+        functools.partial(attend_kernel, steps, chunks, carry),
         [
             shape((rows, features // 2), BF16),
             shape((rows, o_cols), BF16),
             shape((rows, features), BF16),
         ],
-        list(pieces[-1]) + [onehot, kv_t, query_own, gain] + state + [own, cosine, sine, out_here] + founds,
+        (list(pieces[-2]) if carry else [])
+        + list(pieces[-1])
+        + [onehot, kv_t, query_own, gain]
+        + state
+        + [own, cosine, sine, out_here] + founds,
         "attend",
         scratch=[
-            pltpu.VMEM((entries, wide), BF16),
+            pltpu.VMEM((entries, wide + carry), BF16),
             pltpu.VMEM((total, 1), F32),
             pltpu.VMEM((total, kv_all), F32),
             pltpu.VMEM((rows, q_cols), F32),

time: 35.9 us -> 35.7 us (level)
  transfers between devices with their start and end apart: 14 -> 14, of which waited for: 6 -> 6; matrix products, arithmetic and copies ran while one was open for 2% -> 2% of each run, Pallas kernels for 21% -> 20%
where the time goes in v8:
time: 35.7 us; the launch traced here: 35.4 us
  starting transfers between devices  14 us (39%)
  Pallas kernels  11.7 us (33%)
  waiting for transfers between devices  8.85 us (25%)
  local copies, waits for them, and re-layouts  0.73 us (2%)
    ppermute x13, starting transfers between devices, shifted(): lax.ppermute(value, axis, [(i, (i + distance) % size) for i in range(size)])  12.5 us
    pallas_call x11, Pallas kernels, call(): pl.pallas_call(kernel, out_shape=list(outs), in_specs=specs, out_specs=[p...  11.7 us
    ppermute x13, waiting for transfers between devices, shifted(): lax.ppermute(value, axis, [(i, (i + distance) % size) for i in range(size)])  8.84 us
    ppermute x1, starting transfers between devices, body(): raw.append(lax.ppermute(own_codes, ('pos', 'strand'), pairs))  1.58 us
  transfers between devices with their start and end apart: 14, of which 6 were waited for; matrix products, arithmetic and copies ran while one was open for 2% of the time, Pallas kernels for 20%

profile of v8, /device:TPU:0, one launch (start us, length us, event | category | flops | bytes accessed | tf_op | source)
XLA Modules:
  0.0 35.4 jit_solution(8425416274456622495)
XLA Ops:
  0.0 1.1 %stage.1 = (bf16[160,384]{1,0:T(8,128)(2,1)S(1)}, bf16[256,384]{1,0:T(8,128)(2,1)S(1)}, bf16[256,384]{1,0:T(8,128)(2,1)S(1)}, bf16[128,128]{1,0:T(8,128)(2,1)S(1)}) custom-call(bf16[512,768]{1,0:T(8,128)(2,1)} %embed.3, bf16[64,1536]{1,0:T(8,128)(2,1)} %bitcast.13, bf16[96,1536]{1,0:T(8,128)(2,1)} %bitcast.11, s32[128,128]{1,0:T(8,128)} %bitcast.15), custom_call_target="tpu_custom_call" | custom-call | bytes 614400 | tf_op jit(solution)/shard_map/stage/pallas_call | solution.py:44
  1.2 3.0 %collective-permute-start.4 = (bf16[160,384]{1,0:T(8,128)(2,1)S(1)}, bf16[160,384]{1,0:T(8,128)(2,1)S(1)}, u32[]{:S(2)}, u32[]{:S(2)}) collective-permute-start(bf16[160,384]{1,0:T(8,128)(2,1)S(1)} %get-tuple-element.51), channel_id=1, source_target_pairs={{0,1},{1,0},{2,3},{3,2},{4,5},{5,4},{6,7},{7,6},{8,9},{9,8},{10,11... | collective-permute-start | bytes 368648 | tf_op jit(solution)/shard_map/ppermute | solution.py:23
  4.2 0.1 collective-permute-start
  4.2 1.9 %collective-permute-start.2 = (bf16[256,384]{1,0:T(8,128)(2,1)S(1)}, bf16[256,384]{1,0:T(8,128)(2,1)S(1)}, u32[]{:S(2)}, u32[]{:S(2)}) collective-permute-start(bf16[256,384]{1,0:T(8,128)(2,1)S(1)} %get-tuple-element.48), channel_id=1, source_target_pairs={{0,1},{1,0},{2,3},{3,2},{4,5},{5,4},{6,7},{7,6},{8,9},{9,8},{10,11... | collective-permute-start | bytes 589832 | tf_op jit(solution)/shard_map/ppermute | solution.py:23
  6.2 1.9 %prepare.1 = (bf16[512,768]{1,0:T(8,128)(2,1)S(1)}, bf16[64,1536]{1,0:T(8,128)(2,1)S(1)}, bf16[96,1536]{1,0:T(8,128)(2,1)S(1)}, bf16[1536,512]{1,0:T(8,128)(2,1)...) custom-call(bf16[512,768]{1,0:T(8,128)(2,1)} %embed.3, ...), custom_call_target="tpu_custom_call" | custom-call | bytes 3399680 | tf_op jit(solution)/shard_map/prepare/pallas_call | solution.py:44
  8.1 0.2 collective-permute-done.4.refs_6_
  8.3 2.1 %collective-permute-start.8 = (bf16[160,384]{1,0:T(8,128)(2,1)S(1)}, bf16[160,384]{1,0:T(8,128)(2,1)S(1)}, u32[]{:S(2)}, u32[]{:S(2)}) collective-permute-start(bf16[160,384]{1,0:T(8,128)(2,1)S(1)} %collective-permute-done.4.refs_6_), channel_id=1, source_target_pairs={{0,16},{16,0},{1,17},{17,1},{2,18},{18,2},{3,19},{19,3},{4,20},{20... | collective-permute-start | bytes 368648 | tf_op jit(solution)/shard_map/ppermute | solution.py:23
  10.4 1.6 %collective-permute-start.3 = (bf16[128,128]{1,0:T(8,128)(2,1)S(1)}, bf16[128,128]{1,0:T(8,128)(2,1)S(1)}, u32[]{:S(2)}, u32[]{:S(2)}) collective-permute-start(bf16[128,128]{1,0:T(8,128)(2,1)S(1)} %get-tuple-element.54.refs_0_), channel_id=1, source_target_pairs={{0,4},{2,10},{4,8},{6,14},{8,12},{10,2},{12,0},{14,6},{1,5},{3,11}... | collective-permute-start | bytes 98312 | tf_op jit(solution)/shard_map/ppermute | solution.py:506
  12.0 2.2 %collective-permute-start.6 = (bf16[128,128]{1,0:T(8,128)(2,1)S(1)}, bf16[128,128]{1,0:T(8,128)(2,1)S(1)}, u32[]{:S(2)}, u32[]{:S(2)}) collective-permute-start(bf16[128,128]{1,0:T(8,128)(2,1)S(1)} %get-tuple-element.54.refs_0_), channel_id=1, source_target_pairs={{0,12},{4,0},{8,4},{12,8},{1,13},{5,1},{9,5},{13,9},{2,14},{6,2},{... | collective-permute-start | bytes 98312 | tf_op jit(solution)/shard_map/ppermute | solution.py:23
  14.2 0.2 collective-permute-done.8.refs_8_
  14.4 0.4 %collective-permute-start.9 = (bf16[160,384]{1,0:T(8,128)(2,1)S(1)}, bf16[160,384]{1,0:T(8,128)(2,1)S(1)}, u32[]{:S(2)}, u32[]{:S(2)}) collective-permute-start(bf16[160,384]{1,0:T(8,128)(2,1)S(1)} %collective-permute-done.8.refs_8_), channel_id=1, source_target_pairs={{0,2},{2,0},{1,3},{3,1},{4,6},{6,4},{5,7},{7,5},{8,10},{10,8},{9,1... | collective-permute-start | bytes 368648 | tf_op jit(solution)/shard_map/ppermute | solution.py:23
  14.7 1.7 %fetch_out.1.refs_14_.out = bf16[768,1536]{1,0:T(8,128)(2,1)S(1)} custom-call(bf16[768,1536]{1,0:T(8,128)(2,1)} %w_out.1), custom_call_target="tpu_custom_call" | custom-call | bytes 2359296 | tf_op jit(solution)/shard_map/fetch_out/pallas_call | solution.py:44
  16.5 0.1 collective-permute-done.6.refs_2_
  16.6 0.1 collective-permute-start.7
  16.7 0.4 %collective-permute-start.10 = (bf16[128,128]{1,0:T(8,128)(2,1)S(1)}, bf16[128,128]{1,0:T(8,128)(2,1)S(1)}, u32[]{:S(2)}, u32[]{:S(2)}) collective-permute-start(bf16[128,128]{1,0:T(8,128)(2,1)S(1)} %collective-permute-done.3.refs_1_), channel_id=1, source_target_pairs={{0,2},{2,0},{1,3},{3,1},{4,6},{6,4},{5,7},{7,5},{8,10},{10,8},{9,1... | collective-permute-start | bytes 98312 | tf_op jit(solution)/shard_map/ppermute | solution.py:23
  17.1 1.1 %own_features.1 = (bf16[384,512]{1,0:T(8,128)(2,1)S(1)}, bf16[320,1536]{1,0:T(8,128)(2,1)S(1)}, bf16[128,768]{1,0:T(8,128)(2,1)S(1)}, f32[384,1]{1,0:T(8,128)S(1...) custom-call(bf16[128,128]{1,0:T(8,128)(2,1)S(1)} %get-tuple-element.54.refs_0_, ...), custom_call_target="tpu_custom_call" | custom-call | flops 490733568 | bytes 6068224 | tf_op jit(solution)/shard_map/own_features/pallas_call | solution.py:44
  18.2 1.1 %other_features.1 = (bf16[512,512]{1,0:T(8,128)(2,1)S(1)}, bf16[128,256]{1,0:T(8,128)(2,1)S(1)}, f32[512,1]{1,0:T(8,128)S(1)}, f32[512,320]{1,0:T(8,128)S(1)}, f32[128,512]{1,0:T(8,128)S(1)}) custom-call(bf16[256,384]{1,0:T(8,128)(2,1)S(1)} %collective-permute-done.refs_0_, bf16[256,384]{1,0:T(8,128)(2,1)S(1)} %collective-permute-done.1.refs_1_, ...), custom_call_target="tpu_custom_call" | custom-call | flops 327155712 | bytes 7182336 | tf_op jit(solution)/shard_map/other_features/pallas_call | solution.py:44
  19.3 0.0 slice-start
  19.3 2.0 %attend.1 = (bf16[128,768]{1,0:T(8,128)(2,1)S(1)}, bf16[128,768]{1,0:T(8,128)(2,1)S(1)}, bf16[128,1536]{1,0:T(8,128)(2,1)S(1)}) custom-call(bf16[256,384]{1,0:T(8,128)(2,1)S(1)} %collective-permute-done.refs_0_, bf16[256,384]{1,0:T(8,128)(2,1)S(1)} %collective-permute-done.1.refs_1_, bf16[256,384]{1,0:T(8,128)(2,1)S(1)} %collective-permute-done.2.refs_2_, ...), custom_call_target="tpu_custom_call" | custom-call | flops 528482304 | bytes 11016192 | tf_op jit(solution)/shard_map/attend/pallas_call | solution.py:44
  21.3 1.6 %collective-permute-start.12 = (bf16[128,768]{1,0:T(8,128)(2,1)S(1)}, bf16[128,768]{1,0:T(8,128)(2,1)S(1)}, u32[]{:S(2)}, u32[]{:S(2)}) collective-permute-start(bf16[128,768]{1,0:T(8,128)(2,1)S(1)} %get-tuple-element.82.refs_0_), channel_id=1, source_target_pairs={{0,1},{1,0},{2,3},{3,2},{4,5},{5,4},{6,7},{7,6},{8,9},{9,8},{10,11... | collective-permute-start | bytes 589832 | tf_op jit(solution)/shard_map/ppermute | solution.py:23
  22.9 0.3 second_share.1.refs_0_
  23.3 0.6 %collective-permute-start.11 = (bf16[128,768]{1,0:T(8,128)(2,1)S(1)}, bf16[128,768]{1,0:T(8,128)(2,1)S(1)}, u32[]{:S(2)}, u32[]{:S(2)}) collective-permute-start(bf16[128,768]{1,0:T(8,128)(2,1)S(1)} %second_share.1.refs_0_), channel_id=1, source_target_pairs={{0,1},{1,0},{2,3},{3,2},{4,5},{5,4},{6,7},{7,6},{8,9},{9,8},{10,11... | collective-permute-start | bytes 589832 | tf_op jit(solution)/shard_map/ppermute | solution.py:23
  23.8 0.6 %copy.13 = bf16[1536,2,768]{2,0,1:T(8,128)(2,1)S(1)} copy(bf16[1536,2,768]{2,1,0:T(2,128)(2,1)S(1)} %bitcast.10) | data formatting | bytes 9437184 | tf_op jit(solution)/shard_map/optimization_barrier | solution.py:606
  24.4 4.7 %collective-permute-done.12.refs_1_ = bf16[128,768]{1,0:T(8,128)(2,1)S(1)} collective-permute-done((bf16[128,768]{1,0:T(8,128)(2,1)S(1)}, bf16[128,768]{1,0:T(8,128)(2,1)S(1)}, u32[]{:S(2)}, u32[]{:S(2)}) %collective-permute-start.12) | collective-permute-done | bytes 196640 | tf_op jit(solution)/shard_map/ppermute | solution.py:23
  29.2 0.5 %first_tracks.1 = (f32[128,1]{1,0:T(8,128)S(1)}, f32[128,768]{1,0:T(8,128)S(1)}, f32[128,768]{1,0:T(8,128)S(1)}) custom-call(bf16[128,768]{1,0:T(8,128)(2,1)S(1)} %get-tuple-element.82.refs_0_, bf16[128,768]{1,0:T(8,128)(2,1)S(1)} %collective-permute-done.12.refs_1_, bf16[128,1536]{1,0:T(8,128)(2,1)S(1)} %get-tuple-element.79.refs_2_, ...), custom_call_target="tpu_custom_call" | custom-call | flops 301989888 | bytes 6363136 | tf_op jit(solution)/shard_map/first_tracks/pallas_call | solution.py:44
  29.7 2.9 %collective-permute-done.11.refs_1_ = bf16[128,768]{1,0:T(8,128)(2,1)S(1)} collective-permute-done((bf16[128,768]{1,0:T(8,128)(2,1)S(1)}, bf16[128,768]{1,0:T(8,128)(2,1)S(1)}, u32[]{:S(2)}, u32[]{:S(2)}) %collective-permute-start.11) | collective-permute-done | bytes 196640 | tf_op jit(solution)/shard_map/ppermute | solution.py:23
  32.5 0.5 %sent_tracks.1 = (bf16[128,768]{1,0:T(8,128)(2,1)S(1)}, bf16[128,768]{1,0:T(8,128)(2,1)S(1)}, f32[128,1]{1,0:T(8,128)S(1)}) custom-call(bf16[128,768]{1,0:T(8,128)(2,1)S(1)} %second_share.1.refs_0_, bf16[128,768]{1,0:T(8,128)(2,1)S(1)} %collective-permute-done.11.refs_1_, bf16[128,1536]{1,0:T(8,128)(2,1)S(1)} %get-tuple-element.79.refs_2_, ...), custom_call_target="tpu_custom_call" | custom-call | flops 150994944 | bytes 6428672 | tf_op jit(solution)/shard_map/sent_tracks/pallas_call | solution.py:44
  33.0 0.1 collective-permute-start.13
  33.1 0.1 copy-done
  33.2 0.6 %kept_tracks.1.kept = bf16[128,768]{1,0:T(8,128)(2,1)S(1)} custom-call(bf16[128,768]{1,0:T(8,128)(2,1)S(1)} %get-tuple-element.85.gained, bf16[2,1536,768]{2,1,0:T(8,128)(2,1)S(1)} %bitcast.8, f32[128,768]{1,0:T(8,128)S(1)} %get-tuple-element.86.to_keep, f32[128,1]{1,0:T(8,128)S(1)} %get-tuple-element.87.scale, s32[1,768]{1,0:T(1,128)S(1)} %reshape.7.pairs), custom_call_target="tpu_custom_call" | custom-call | flops 150994944 | bytes 5573632 | tf_op jit(solution)/shard_map/kept_tracks/pallas_call | solution.py:44
  33.8 0.7 %collective-permute-done.13.received = bf16[128,768]{1,0:T(8,128)(2,1)S(1)} collective-permute-done((bf16[128,768]{1,0:T(8,128)(2,1)S(1)}, bf16[128,768]{1,0:T(8,128)(2,1)S(1)}, u32[]{:S(2)}, u32[]{:S(2)}) %collective-permute-start.13) | collective-permute-done | bytes 196640 | tf_op jit(solution)/shard_map/ppermute | solution.py:23
  34.6 0.9 %average.1 = f32[128,768]{1,0:T(8,128)} custom-call(bf16[128,768]{1,0:T(8,128)(2,1)S(1)} %kept_tracks.1.kept, bf16[128,768]{1,0:T(8,128)(2,1)S(1)} %collective-permute-done.13.received, s32[1,768]{1,0:T(1,128)S(1)} %reshape.7.pairs), custom_call_target="tpu_custom_call" | custom-call | bytes 1182720 | tf_op jit(solution)/shard_map/average/pallas_call | solution.py:44
  (16 shorter events, 0.0 us)
Async XLA Ops:
  1.2 7.2 %collective-permute-start.4 = (bf16[160,384]{1,0:T(8,128)(2,1)S(1)}, bf16[160,384]{1,0:T(8,128)(2,1)S(1)}, u32[]{:S(2)}, u32[]{:S(2)}) collective-permute-start(bf16[160,384]{1,0:T(8,128)(2,1)S(1)} %get-tuple-element.51), channel_id=1, source_target_pairs={{0,1},{1,0},{2,3},{3,2},{4,5},{5,4},{6,7},{7,6},{8,9},{9,8},{10,11... | collective-permute-start | bytes 368648 | tf_op jit(solution)/shard_map/ppermute | solution.py:23
  4.2 10.1 %collective-permute-start = (bf16[256,384]{1,0:T(8,128)(2,1)S(1)}, bf16[256,384]{1,0:T(8,128)(2,1)S(1)}, u32[]{:S(2)}, u32[]{:S(2)}) collective-permute-start(bf16[256,384]{1,0:T(8,128)(2,1)S(1)} %get-tuple-element.47), channel_id=1, source_target_pairs={{0,1},{1,0},{2,3},{3,2},{4,5},{5,4},{6,7},{7,6},{8,9},{9,8},{10,11... | collective-permute-start | bytes 589832 | tf_op jit(solution)/shard_map/ppermute | solution.py:23
  4.2 12.2 %collective-permute-start.2 = (bf16[256,384]{1,0:T(8,128)(2,1)S(1)}, bf16[256,384]{1,0:T(8,128)(2,1)S(1)}, u32[]{:S(2)}, u32[]{:S(2)}) collective-permute-start(bf16[256,384]{1,0:T(8,128)(2,1)S(1)} %get-tuple-element.48), channel_id=1, source_target_pairs={{0,1},{1,0},{2,3},{3,2},{4,5},{5,4},{6,7},{7,6},{8,9},{9,8},{10,11... | collective-permute-start | bytes 589832 | tf_op jit(solution)/shard_map/ppermute | solution.py:23
  8.3 3.7 %collective-permute-start.5 = (bf16[160,384]{1,0:T(8,128)(2,1)S(1)}, bf16[160,384]{1,0:T(8,128)(2,1)S(1)}, u32[]{:S(2)}, u32[]{:S(2)}) collective-permute-start(bf16[160,384]{1,0:T(8,128)(2,1)S(1)} %collective-permute-done.4.refs_6_), channel_id=1, source_target_pairs={{0,2},{2,0},{1,3},{3,1},{4,6},{6,4},{5,7},{7,5},{8,10},{10,8},{9,1... | collective-permute-start | bytes 368648 | tf_op jit(solution)/shard_map/ppermute | solution.py:23
  8.3 6.1 %collective-permute-start.8 = (bf16[160,384]{1,0:T(8,128)(2,1)S(1)}, bf16[160,384]{1,0:T(8,128)(2,1)S(1)}, u32[]{:S(2)}, u32[]{:S(2)}) collective-permute-start(bf16[160,384]{1,0:T(8,128)(2,1)S(1)} %collective-permute-done.4.refs_6_), channel_id=1, source_target_pairs={{0,16},{16,0},{1,17},{17,1},{2,18},{18,2},{3,19},{19,3},{4,20},{20... | collective-permute-start | bytes 368648 | tf_op jit(solution)/shard_map/ppermute | solution.py:23
  10.4 6.0 %collective-permute-start.3 = (bf16[128,128]{1,0:T(8,128)(2,1)S(1)}, bf16[128,128]{1,0:T(8,128)(2,1)S(1)}, u32[]{:S(2)}, u32[]{:S(2)}) collective-permute-start(bf16[128,128]{1,0:T(8,128)(2,1)S(1)} %get-tuple-element.54.refs_0_), channel_id=1, source_target_pairs={{0,4},{2,10},{4,8},{6,14},{8,12},{10,2},{12,0},{14,6},{1,5},{3,11}... | collective-permute-start | bytes 98312 | tf_op jit(solution)/shard_map/ppermute | solution.py:506
  12.0 4.6 %collective-permute-start.6 = (bf16[128,128]{1,0:T(8,128)(2,1)S(1)}, bf16[128,128]{1,0:T(8,128)(2,1)S(1)}, u32[]{:S(2)}, u32[]{:S(2)}) collective-permute-start(bf16[128,128]{1,0:T(8,128)(2,1)S(1)} %get-tuple-element.54.refs_0_), channel_id=1, source_target_pairs={{0,12},{4,0},{8,4},{12,8},{1,13},{5,1},{9,5},{13,9},{2,14},{6,2},{... | collective-permute-start | bytes 98312 | tf_op jit(solution)/shard_map/ppermute | solution.py:23
  14.2 3.9 %collective-permute-start.1 = (bf16[256,384]{1,0:T(8,128)(2,1)S(1)}, bf16[256,384]{1,0:T(8,128)(2,1)S(1)}, u32[]{:S(2)}, u32[]{:S(2)}) collective-permute-start(bf16[256,384]{1,0:T(8,128)(2,1)S(1)} %collective-permute-done.refs_0_), channel_id=1, source_target_pairs={{0,2},{2,0},{1,3},{3,1},{4,6},{6,4},{5,7},{7,5},{8,10},{10,8},{9,1... | collective-permute-start | bytes 589832 | tf_op jit(solution)/shard_map/ppermute | solution.py:23
  14.4 2.7 %collective-permute-start.9 = (bf16[160,384]{1,0:T(8,128)(2,1)S(1)}, bf16[160,384]{1,0:T(8,128)(2,1)S(1)}, u32[]{:S(2)}, u32[]{:S(2)}) collective-permute-start(bf16[160,384]{1,0:T(8,128)(2,1)S(1)} %collective-permute-done.8.refs_8_), channel_id=1, source_target_pairs={{0,2},{2,0},{1,3},{3,1},{4,6},{6,4},{5,7},{7,5},{8,10},{10,8},{9,1... | collective-permute-start | bytes 368648 | tf_op jit(solution)/shard_map/ppermute | solution.py:23
  16.6 2.7 %collective-permute-start.7 = (bf16[256,384]{1,0:T(8,128)(2,1)S(1)}, bf16[256,384]{1,0:T(8,128)(2,1)S(1)}, u32[]{:S(2)}, u32[]{:S(2)}) collective-permute-start(bf16[256,384]{1,0:T(8,128)(2,1)S(1)} %collective-permute-done.2.refs_2_), channel_id=1, source_target_pairs={{0,2},{2,0},{1,3},{3,1},{4,6},{6,4},{5,7},{7,5},{8,10},{10,8},{9,1... | collective-permute-start | bytes 589832 | tf_op jit(solution)/shard_map/ppermute | solution.py:23
  16.7 1.5 %collective-permute-start.10 = (bf16[128,128]{1,0:T(8,128)(2,1)S(1)}, bf16[128,128]{1,0:T(8,128)(2,1)S(1)}, u32[]{:S(2)}, u32[]{:S(2)}) collective-permute-start(bf16[128,128]{1,0:T(8,128)(2,1)S(1)} %collective-permute-done.3.refs_1_), channel_id=1, source_target_pairs={{0,2},{2,0},{1,3},{3,1},{4,6},{6,4},{5,7},{7,5},{8,10},{10,8},{9,1... | collective-permute-start | bytes 98312 | tf_op jit(solution)/shard_map/ppermute | solution.py:23
  19.3 4.5 %slice-start = ((s8[4718592]{0:T(1024)(128)(4,1)}), s8[4194304]{0:T(1024)(128)(4,1)S(1)}, s32[]{:S(2)}) async-start(s8[4718592]{0:T(1024)(128)(4,1)} %bitcast.9), calls=%async_computation | async-start | bytes 8388608
  19.3 4.5 %slice-start.1 = ((s8[4718592]{0:T(1024)(128)(4,1)}), s8[524288]{0:T(1024)(128)(4,1)S(1)}, s32[]{:S(2)}) async-start(s8[4718592]{0:T(1024)(128)(4,1)} %bitcast.9), calls=%async_computation.1 | async-start | bytes 1048576
  21.3 7.8 %collective-permute-start.12 = (bf16[128,768]{1,0:T(8,128)(2,1)S(1)}, bf16[128,768]{1,0:T(8,128)(2,1)S(1)}, u32[]{:S(2)}, u32[]{:S(2)}) collective-permute-start(bf16[128,768]{1,0:T(8,128)(2,1)S(1)} %get-tuple-element.82.refs_0_), channel_id=1, source_target_pairs={{0,1},{1,0},{2,3},{3,2},{4,5},{5,4},{6,7},{7,6},{8,9},{9,8},{10,11... | collective-permute-start | bytes 589832 | tf_op jit(solution)/shard_map/ppermute | solution.py:23
  23.3 9.3 %collective-permute-start.11 = (bf16[128,768]{1,0:T(8,128)(2,1)S(1)}, bf16[128,768]{1,0:T(8,128)(2,1)S(1)}, u32[]{:S(2)}, u32[]{:S(2)}) collective-permute-start(bf16[128,768]{1,0:T(8,128)(2,1)S(1)} %second_share.1.refs_0_), channel_id=1, source_target_pairs={{0,1},{1,0},{2,3},{3,2},{4,5},{5,4},{6,7},{7,6},{8,9},{9,8},{10,11... | collective-permute-start | bytes 589832 | tf_op jit(solution)/shard_map/ppermute | solution.py:23
  32.5 0.7 %copy-start = (s32[768]{0:T(1024)S(1)}, s32[768]{0:T(1024)}, u32[]{:S(2)}) copy-start(s32[768]{0:T(1024)} %param.19) | copy-start | bytes 9220
  33.0 1.5 %collective-permute-start.13 = (bf16[128,768]{1,0:T(8,128)(2,1)S(1)}, bf16[128,768]{1,0:T(8,128)(2,1)S(1)}, u32[]{:S(2)}, u32[]{:S(2)}) collective-permute-start(bf16[128,768]{1,0:T(8,128)(2,1)S(1)} %get-tuple-element.88), channel_id=1, source_target_pairs={{0,2},{2,0},{1,3},{3,1},{4,6},{6,4},{5,7},{7,5},{8,10},{10,8},{9,1... | collective-permute-start | bytes 589832 | tf_op jit(solution)/shard_map/ppermute | solution.py:23

commit v9 on v8

--- a/solution.py
+++ b/solution.py
@@ -299,13 +299,11 @@
     if carry:
         earlier, refs = refs[:2], refs[2:]
     mine, theirs, onehot, kv_t, w_query, gain, square, kv_sum, q_sum = refs[:9]
-    own, cosine, sine, out = refs[9:13]
-    founds = refs[13 : 13 + len(steps) - 1]
-    share, merged, inputs = refs[12 + len(steps) : 15 + len(steps)]
-    table, squares, sums, queries, keys, values = refs[15 + len(steps) :]
+    cosine, sine, out = refs[9:12]
+    share, merged, last = refs[12:15]
+    table, squares, sums, queries, keys, values = refs[15:]
     half, width = mine.shape
-    rows, own_width = own.shape
-    features = inputs.shape[1]
+    rows, features = merged.shape[0], w_query.shape[0]
     total = onehot.shape[0]
     block = block_of(total, rows)
     if carry:
@@ -316,12 +314,7 @@
     start = chunk_start(*steps[-1], chunks, width) - carry
     span, weights = (0, total), (kv_t, w_query, gain)
     before, after = (square, kv_sum, q_sum), (squares, sums, queries)
-    last = absorb(onehot, span, table, rows, start, width + carry, weights, before, after)
-    inputs[:, pl.ds(pl.multiple_of(start, LANES), width + carry)] = last
-    for found, spot in zip(founds, steps):
-        inputs[:, pl.ds(pl.multiple_of(chunk_start(*spot, chunks, width), LANES), found.shape[1])] = found[...]
-    begin = pl.multiple_of(lax.axis_index("heads") * own_width, LANES)
-    inputs[:, pl.ds(begin, own_width)] = own[...]
+    last[...] = absorb(onehot, span, table, rows, start, width + carry, weights, before, after)
 
     def finish(begin):
         here = pl.ds(begin, block)
@@ -344,8 +337,14 @@
     share[...] = matmul(merged[...], out[:, : share.shape[1]]).astype(BF16)
 
 
-def second_kernel(merged, out, share):
+def second_kernel(spots, full, *refs):
+    merged, out, own = refs[:3]
+    founds, (share, inputs) = refs[3:-2], refs[-2:]
     share[...] = matmul(merged[...], out[:, share.shape[1] :]).astype(BF16)
+    inputs[:, pl.ds(pl.multiple_of(lax.axis_index("heads") * full, LANES), full)] = own[...]
+    for found, spot in zip(founds, spots):
+        begin = pl.multiple_of(chunk_start(spot[0], 0, 1, full) + spot[1], LANES)
+        inputs[:, pl.ds(begin, found.shape[1])] = found[...]
 
 
 def gather_hidden(shares, inputs, gain, chunk):
@@ -570,18 +569,18 @@
         found, *state = results
         founds.append(found)
     o_cols = q_cols // KDIM * VDIM
-    share_one, merged, inputs = call(
+    share_one, merged, last = call(
         functools.partial(attend_kernel, steps, chunks, carry),
         [
             shape((rows, features // 2), BF16),
             shape((rows, o_cols), BF16),
-            shape((rows, features), BF16),
+            shape((rows, wide + carry), BF16),
         ],
         (list(pieces[-2]) if carry else [])
         + list(pieces[-1])
         + [onehot, kv_t, query_own, gain]
         + state
-        + [own, cosine, sine, out_here] + founds,
+        + [cosine, sine, out_here],
         "attend",
         scratch=[
             pltpu.VMEM((entries, wide + carry), BF16),
@@ -594,10 +593,12 @@
         flops=2 * total * wide * (entries + kv_all) + 2 * total * q_cols * rows * 3,
         spare=8 * total * entries,
     )
-    (share_two,) = call(
-        second_kernel,
-        [shape((rows, features // 2), BF16)],
-        [merged, out_here],
+    spots = [(step, i * wide) for step, i in steps]
+    spots[-1] = (spots[-1][0], spots[-1][1] - carry)
+    share_two, inputs = call(
+        functools.partial(second_kernel, spots, width),
+        [shape((rows, features // 2), BF16), shape((rows, features), BF16)],
+        [merged, out_here, own] + founds + [last],
         "second_share",
         flops=rows * o_cols * features,
     )

time: 35.7 us -> 35.7 us (level)
  no operation moved by 1% of the time
where the time goes in v9:
time: 35.7 us; the launch traced here: 35.4 us
  starting transfers between devices  14 us (39%)
  Pallas kernels  11.7 us (33%)
  waiting for transfers between devices  8.85 us (25%)
  local copies, waits for them, and re-layouts  0.73 us (2%)
    ppermute x13, starting transfers between devices, shifted(): lax.ppermute(value, axis, [(i, (i + distance) % size) for i in range(size)])  12.5 us
    pallas_call x11, Pallas kernels, call(): pl.pallas_call(kernel, out_shape=list(outs), in_specs=specs, out_specs=[p...  11.7 us
    ppermute x13, waiting for transfers between devices, shifted(): lax.ppermute(value, axis, [(i, (i + distance) % size) for i in range(size)])  8.85 us
    ppermute x1, starting transfers between devices, body(): raw.append(lax.ppermute(own_codes, ('pos', 'strand'), pairs))  1.58 us
  transfers between devices with their start and end apart: 14, of which 6 were waited for; matrix products, arithmetic and copies ran while one was open for 2% of the time, Pallas kernels for 20%

profile of v9, /device:TPU:0, one launch (start us, length us, event | category | flops | bytes accessed | tf_op | source)
XLA Modules:
  0.0 35.4 jit_solution(3429361071499676087)
XLA Ops:
  0.0 1.1 %stage.1 = (bf16[160,384]{1,0:T(8,128)(2,1)S(1)}, bf16[256,384]{1,0:T(8,128)(2,1)S(1)}, bf16[256,384]{1,0:T(8,128)(2,1)S(1)}, bf16[128,128]{1,0:T(8,128)(2,1)S(1)}) custom-call(bf16[512,768]{1,0:T(8,128)(2,1)} %embed.3, bf16[64,1536]{1,0:T(8,128)(2,1)} %bitcast.13, bf16[96,1536]{1,0:T(8,128)(2,1)} %bitcast.11, s32[128,128]{1,0:T(8,128)} %bitcast.15), custom_call_target="tpu_custom_call" | custom-call | bytes 614400 | tf_op jit(solution)/shard_map/stage/pallas_call | solution.py:44
  1.2 3.0 %collective-permute-start.4 = (bf16[160,384]{1,0:T(8,128)(2,1)S(1)}, bf16[160,384]{1,0:T(8,128)(2,1)S(1)}, u32[]{:S(2)}, u32[]{:S(2)}) collective-permute-start(bf16[160,384]{1,0:T(8,128)(2,1)S(1)} %get-tuple-element.53), channel_id=1, source_target_pairs={{0,1},{1,0},{2,3},{3,2},{4,5},{5,4},{6,7},{7,6},{8,9},{9,8},{10,11... | collective-permute-start | bytes 368648 | tf_op jit(solution)/shard_map/ppermute | solution.py:23
  4.2 0.1 collective-permute-start
  4.2 1.9 %collective-permute-start.2 = (bf16[256,384]{1,0:T(8,128)(2,1)S(1)}, bf16[256,384]{1,0:T(8,128)(2,1)S(1)}, u32[]{:S(2)}, u32[]{:S(2)}) collective-permute-start(bf16[256,384]{1,0:T(8,128)(2,1)S(1)} %get-tuple-element.50), channel_id=1, source_target_pairs={{0,1},{1,0},{2,3},{3,2},{4,5},{5,4},{6,7},{7,6},{8,9},{9,8},{10,11... | collective-permute-start | bytes 589832 | tf_op jit(solution)/shard_map/ppermute | solution.py:23
  6.2 1.9 %prepare.1 = (bf16[512,768]{1,0:T(8,128)(2,1)S(1)}, bf16[64,1536]{1,0:T(8,128)(2,1)S(1)}, bf16[96,1536]{1,0:T(8,128)(2,1)S(1)}, bf16[1536,512]{1,0:T(8,128)(2,1)...) custom-call(bf16[512,768]{1,0:T(8,128)(2,1)} %embed.3, ...), custom_call_target="tpu_custom_call" | custom-call | bytes 3399680 | tf_op jit(solution)/shard_map/prepare/pallas_call | solution.py:44
  8.1 0.2 collective-permute-done.4.refs_6_
  8.3 2.1 %collective-permute-start.8 = (bf16[160,384]{1,0:T(8,128)(2,1)S(1)}, bf16[160,384]{1,0:T(8,128)(2,1)S(1)}, u32[]{:S(2)}, u32[]{:S(2)}) collective-permute-start(bf16[160,384]{1,0:T(8,128)(2,1)S(1)} %collective-permute-done.4.refs_6_), channel_id=1, source_target_pairs={{0,16},{16,0},{1,17},{17,1},{2,18},{18,2},{3,19},{19,3},{4,20},{20... | collective-permute-start | bytes 368648 | tf_op jit(solution)/shard_map/ppermute | solution.py:23
  10.4 1.6 %collective-permute-start.3 = (bf16[128,128]{1,0:T(8,128)(2,1)S(1)}, bf16[128,128]{1,0:T(8,128)(2,1)S(1)}, u32[]{:S(2)}, u32[]{:S(2)}) collective-permute-start(bf16[128,128]{1,0:T(8,128)(2,1)S(1)} %get-tuple-element.56.refs_0_), channel_id=1, source_target_pairs={{0,4},{2,10},{4,8},{6,14},{8,12},{10,2},{12,0},{14,6},{1,5},{3,11}... | collective-permute-start | bytes 98312 | tf_op jit(solution)/shard_map/ppermute | solution.py:505
  12.0 2.2 %collective-permute-start.6 = (bf16[128,128]{1,0:T(8,128)(2,1)S(1)}, bf16[128,128]{1,0:T(8,128)(2,1)S(1)}, u32[]{:S(2)}, u32[]{:S(2)}) collective-permute-start(bf16[128,128]{1,0:T(8,128)(2,1)S(1)} %get-tuple-element.56.refs_0_), channel_id=1, source_target_pairs={{0,12},{4,0},{8,4},{12,8},{1,13},{5,1},{9,5},{13,9},{2,14},{6,2},{... | collective-permute-start | bytes 98312 | tf_op jit(solution)/shard_map/ppermute | solution.py:23
  14.2 0.2 collective-permute-done.8.refs_8_
  14.4 0.4 %collective-permute-start.9 = (bf16[160,384]{1,0:T(8,128)(2,1)S(1)}, bf16[160,384]{1,0:T(8,128)(2,1)S(1)}, u32[]{:S(2)}, u32[]{:S(2)}) collective-permute-start(bf16[160,384]{1,0:T(8,128)(2,1)S(1)} %collective-permute-done.8.refs_8_), channel_id=1, source_target_pairs={{0,2},{2,0},{1,3},{3,1},{4,6},{6,4},{5,7},{7,5},{8,10},{10,8},{9,1... | collective-permute-start | bytes 368648 | tf_op jit(solution)/shard_map/ppermute | solution.py:23
  14.7 1.7 %fetch_out.1.refs_13_.refs_1_ = bf16[768,1536]{1,0:T(8,128)(2,1)S(1)} custom-call(bf16[768,1536]{1,0:T(8,128)(2,1)} %w_out.1), custom_call_target="tpu_custom_call" | custom-call | bytes 2359296 | tf_op jit(solution)/shard_map/fetch_out/pallas_call | solution.py:44
  16.5 0.1 collective-permute-done.6.refs_2_
  16.6 0.1 collective-permute-start.7
  16.7 0.4 %collective-permute-start.10 = (bf16[128,128]{1,0:T(8,128)(2,1)S(1)}, bf16[128,128]{1,0:T(8,128)(2,1)S(1)}, u32[]{:S(2)}, u32[]{:S(2)}) collective-permute-start(bf16[128,128]{1,0:T(8,128)(2,1)S(1)} %collective-permute-done.3.refs_1_), channel_id=1, source_target_pairs={{0,2},{2,0},{1,3},{3,1},{4,6},{6,4},{5,7},{7,5},{8,10},{10,8},{9,1... | collective-permute-start | bytes 98312 | tf_op jit(solution)/shard_map/ppermute | solution.py:23
  17.1 1.1 %own_features.1 = (bf16[384,512]{1,0:T(8,128)(2,1)S(1)}, bf16[320,1536]{1,0:T(8,128)(2,1)S(1)}, bf16[128,768]{1,0:T(8,128)(2,1)S(1)}, f32[384,1]{1,0:T(8,128)S(1...) custom-call(bf16[128,128]{1,0:T(8,128)(2,1)S(1)} %get-tuple-element.56.refs_0_, ...), custom_call_target="tpu_custom_call" | custom-call | flops 490733568 | bytes 6068224 | tf_op jit(solution)/shard_map/own_features/pallas_call | solution.py:44
  18.2 1.1 %other_features.1 = (bf16[512,512]{1,0:T(8,128)(2,1)S(1)}, bf16[128,256]{1,0:T(8,128)(2,1)S(1)}, f32[512,1]{1,0:T(8,128)S(1)}, f32[512,320]{1,0:T(8,128)S(1)}, f32[128,512]{1,0:T(8,128)S(1)}) custom-call(bf16[256,384]{1,0:T(8,128)(2,1)S(1)} %collective-permute-done.refs_0_, bf16[256,384]{1,0:T(8,128)(2,1)S(1)} %collective-permute-done.1.refs_1_, ...), custom_call_target="tpu_custom_call" | custom-call | flops 327155712 | bytes 7182336 | tf_op jit(solution)/shard_map/other_features/pallas_call | solution.py:44
  19.3 0.0 slice-start
  19.3 2.0 %attend.1 = (bf16[128,768]{1,0:T(8,128)(2,1)S(1)}, bf16[128,768]{1,0:T(8,128)(2,1)S(1)}, bf16[128,512]{1,0:T(8,128)(2,1)S(1)}) custom-call(bf16[256,384]{1,0:T(8,128)(2,1)S(1)} %collective-permute-done.refs_0_, bf16[256,384]{1,0:T(8,128)(2,1)S(1)} %collective-permute-done.1.refs_1_, bf16[256,384]{1,0:T(8,128)(2,1)S(1)} %collective-permute-done.2.refs_2_, ...), custom_call_target="tpu_custom_call" | custom-call | flops 528482304 | bytes 10491904 | tf_op jit(solution)/shard_map/attend/pallas_call | solution.py:44
  21.3 1.6 %collective-permute-start.12 = (bf16[128,768]{1,0:T(8,128)(2,1)S(1)}, bf16[128,768]{1,0:T(8,128)(2,1)S(1)}, u32[]{:S(2)}, u32[]{:S(2)}) collective-permute-start(bf16[128,768]{1,0:T(8,128)(2,1)S(1)} %get-tuple-element.86.refs_0_), channel_id=1, source_target_pairs={{0,1},{1,0},{2,3},{3,2},{4,5},{5,4},{6,7},{7,6},{8,9},{9,8},{10,11... | collective-permute-start | bytes 589832 | tf_op jit(solution)/shard_map/ppermute | solution.py:23
  22.9 0.3 second_share.1
  23.2 0.6 %collective-permute-start.11 = (bf16[128,768]{1,0:T(8,128)(2,1)S(1)}, bf16[128,768]{1,0:T(8,128)(2,1)S(1)}, u32[]{:S(2)}, u32[]{:S(2)}) collective-permute-start(bf16[128,768]{1,0:T(8,128)(2,1)S(1)} %get-tuple-element.82.refs_0_), channel_id=1, source_target_pairs={{0,1},{1,0},{2,3},{3,2},{4,5},{5,4},{6,7},{7,6},{8,9},{9,8},{10,11... | collective-permute-start | bytes 589832 | tf_op jit(solution)/shard_map/ppermute | solution.py:23
  23.8 0.6 %copy.13 = bf16[1536,2,768]{2,0,1:T(8,128)(2,1)S(1)} copy(bf16[1536,2,768]{2,1,0:T(2,128)(2,1)S(1)} %bitcast.10) | data formatting | bytes 9437184 | tf_op jit(solution)/shard_map/optimization_barrier | solution.py:607
  24.4 4.7 %collective-permute-done.12.refs_1_ = bf16[128,768]{1,0:T(8,128)(2,1)S(1)} collective-permute-done((bf16[128,768]{1,0:T(8,128)(2,1)S(1)}, bf16[128,768]{1,0:T(8,128)(2,1)S(1)}, u32[]{:S(2)}, u32[]{:S(2)}) %collective-permute-start.12) | collective-permute-done | bytes 196640 | tf_op jit(solution)/shard_map/ppermute | solution.py:23
  29.2 0.5 %first_tracks.1 = (f32[128,1]{1,0:T(8,128)S(1)}, f32[128,768]{1,0:T(8,128)S(1)}, f32[128,768]{1,0:T(8,128)S(1)}) custom-call(bf16[128,768]{1,0:T(8,128)(2,1)S(1)} %get-tuple-element.86.refs_0_, bf16[128,768]{1,0:T(8,128)(2,1)S(1)} %collective-permute-done.12.refs_1_, bf16[128,1536]{1,0:T(8,128)(2,1)S(1)} %get-tuple-element.83.refs_2_, ...), custom_call_target="tpu_custom_call" | custom-call | flops 301989888 | bytes 6363136 | tf_op jit(solution)/shard_map/first_tracks/pallas_call | solution.py:44
  29.6 2.9 %collective-permute-done.11.refs_1_ = bf16[128,768]{1,0:T(8,128)(2,1)S(1)} collective-permute-done((bf16[128,768]{1,0:T(8,128)(2,1)S(1)}, bf16[128,768]{1,0:T(8,128)(2,1)S(1)}, u32[]{:S(2)}, u32[]{:S(2)}) %collective-permute-start.11) | collective-permute-done | bytes 196640 | tf_op jit(solution)/shard_map/ppermute | solution.py:23
  32.5 0.5 %sent_tracks.1 = (bf16[128,768]{1,0:T(8,128)(2,1)S(1)}, bf16[128,768]{1,0:T(8,128)(2,1)S(1)}, f32[128,1]{1,0:T(8,128)S(1)}) custom-call(bf16[128,768]{1,0:T(8,128)(2,1)S(1)} %get-tuple-element.82.refs_0_, bf16[128,768]{1,0:T(8,128)(2,1)S(1)} %collective-permute-done.11.refs_1_, bf16[128,1536]{1,0:T(8,128)(2,1)S(1)} %get-tuple-element.83.refs_2_, ...), custom_call_target="tpu_custom_call" | custom-call | flops 150994944 | bytes 6428672 | tf_op jit(solution)/shard_map/sent_tracks/pallas_call | solution.py:44
  33.0 0.1 collective-permute-start.13
  33.1 0.1 copy-done
  33.2 0.6 %kept_tracks.1.kept = bf16[128,768]{1,0:T(8,128)(2,1)S(1)} custom-call(bf16[128,768]{1,0:T(8,128)(2,1)S(1)} %get-tuple-element.89.gained, bf16[2,1536,768]{2,1,0:T(8,128)(2,1)S(1)} %bitcast.8, f32[128,768]{1,0:T(8,128)S(1)} %get-tuple-element.90.to_keep, f32[128,1]{1,0:T(8,128)S(1)} %get-tuple-element.91.scale, s32[1,768]{1,0:T(1,128)S(1)} %reshape.7.pairs), custom_call_target="tpu_custom_call" | custom-call | flops 150994944 | bytes 5573632 | tf_op jit(solution)/shard_map/kept_tracks/pallas_call | solution.py:44
  33.8 0.7 %collective-permute-done.13.received = bf16[128,768]{1,0:T(8,128)(2,1)S(1)} collective-permute-done((bf16[128,768]{1,0:T(8,128)(2,1)S(1)}, bf16[128,768]{1,0:T(8,128)(2,1)S(1)}, u32[]{:S(2)}, u32[]{:S(2)}) %collective-permute-start.13) | collective-permute-done | bytes 196640 | tf_op jit(solution)/shard_map/ppermute | solution.py:23
  34.5 0.9 %average.1 = f32[128,768]{1,0:T(8,128)} custom-call(bf16[128,768]{1,0:T(8,128)(2,1)S(1)} %kept_tracks.1.kept, bf16[128,768]{1,0:T(8,128)(2,1)S(1)} %collective-permute-done.13.received, s32[1,768]{1,0:T(1,128)S(1)} %reshape.7.pairs), custom_call_target="tpu_custom_call" | custom-call | bytes 1182720 | tf_op jit(solution)/shard_map/average/pallas_call | solution.py:44
  (16 shorter events, 0.0 us)
Async XLA Ops:
  1.2 7.2 %collective-permute-start.4 = (bf16[160,384]{1,0:T(8,128)(2,1)S(1)}, bf16[160,384]{1,0:T(8,128)(2,1)S(1)}, u32[]{:S(2)}, u32[]{:S(2)}) collective-permute-start(bf16[160,384]{1,0:T(8,128)(2,1)S(1)} %get-tuple-element.53), channel_id=1, source_target_pairs={{0,1},{1,0},{2,3},{3,2},{4,5},{5,4},{6,7},{7,6},{8,9},{9,8},{10,11... | collective-permute-start | bytes 368648 | tf_op jit(solution)/shard_map/ppermute | solution.py:23
  4.2 10.1 %collective-permute-start = (bf16[256,384]{1,0:T(8,128)(2,1)S(1)}, bf16[256,384]{1,0:T(8,128)(2,1)S(1)}, u32[]{:S(2)}, u32[]{:S(2)}) collective-permute-start(bf16[256,384]{1,0:T(8,128)(2,1)S(1)} %get-tuple-element.49), channel_id=1, source_target_pairs={{0,1},{1,0},{2,3},{3,2},{4,5},{5,4},{6,7},{7,6},{8,9},{9,8},{10,11... | collective-permute-start | bytes 589832 | tf_op jit(solution)/shard_map/ppermute | solution.py:23
  4.2 12.2 %collective-permute-start.2 = (bf16[256,384]{1,0:T(8,128)(2,1)S(1)}, bf16[256,384]{1,0:T(8,128)(2,1)S(1)}, u32[]{:S(2)}, u32[]{:S(2)}) collective-permute-start(bf16[256,384]{1,0:T(8,128)(2,1)S(1)} %get-tuple-element.50), channel_id=1, source_target_pairs={{0,1},{1,0},{2,3},{3,2},{4,5},{5,4},{6,7},{7,6},{8,9},{9,8},{10,11... | collective-permute-start | bytes 589832 | tf_op jit(solution)/shard_map/ppermute | solution.py:23
  8.3 3.7 %collective-permute-start.5 = (bf16[160,384]{1,0:T(8,128)(2,1)S(1)}, bf16[160,384]{1,0:T(8,128)(2,1)S(1)}, u32[]{:S(2)}, u32[]{:S(2)}) collective-permute-start(bf16[160,384]{1,0:T(8,128)(2,1)S(1)} %collective-permute-done.4.refs_6_), channel_id=1, source_target_pairs={{0,2},{2,0},{1,3},{3,1},{4,6},{6,4},{5,7},{7,5},{8,10},{10,8},{9,1... | collective-permute-start | bytes 368648 | tf_op jit(solution)/shard_map/ppermute | solution.py:23
  8.3 6.1 %collective-permute-start.8 = (bf16[160,384]{1,0:T(8,128)(2,1)S(1)}, bf16[160,384]{1,0:T(8,128)(2,1)S(1)}, u32[]{:S(2)}, u32[]{:S(2)}) collective-permute-start(bf16[160,384]{1,0:T(8,128)(2,1)S(1)} %collective-permute-done.4.refs_6_), channel_id=1, source_target_pairs={{0,16},{16,0},{1,17},{17,1},{2,18},{18,2},{3,19},{19,3},{4,20},{20... | collective-permute-start | bytes 368648 | tf_op jit(solution)/shard_map/ppermute | solution.py:23
  10.4 6.0 %collective-permute-start.3 = (bf16[128,128]{1,0:T(8,128)(2,1)S(1)}, bf16[128,128]{1,0:T(8,128)(2,1)S(1)}, u32[]{:S(2)}, u32[]{:S(2)}) collective-permute-start(bf16[128,128]{1,0:T(8,128)(2,1)S(1)} %get-tuple-element.56.refs_0_), channel_id=1, source_target_pairs={{0,4},{2,10},{4,8},{6,14},{8,12},{10,2},{12,0},{14,6},{1,5},{3,11}... | collective-permute-start | bytes 98312 | tf_op jit(solution)/shard_map/ppermute | solution.py:505
  12.0 4.6 %collective-permute-start.6 = (bf16[128,128]{1,0:T(8,128)(2,1)S(1)}, bf16[128,128]{1,0:T(8,128)(2,1)S(1)}, u32[]{:S(2)}, u32[]{:S(2)}) collective-permute-start(bf16[128,128]{1,0:T(8,128)(2,1)S(1)} %get-tuple-element.56.refs_0_), channel_id=1, source_target_pairs={{0,12},{4,0},{8,4},{12,8},{1,13},{5,1},{9,5},{13,9},{2,14},{6,2},{... | collective-permute-start | bytes 98312 | tf_op jit(solution)/shard_map/ppermute | solution.py:23
  14.2 3.9 %collective-permute-start.1 = (bf16[256,384]{1,0:T(8,128)(2,1)S(1)}, bf16[256,384]{1,0:T(8,128)(2,1)S(1)}, u32[]{:S(2)}, u32[]{:S(2)}) collective-permute-start(bf16[256,384]{1,0:T(8,128)(2,1)S(1)} %collective-permute-done.refs_0_), channel_id=1, source_target_pairs={{0,2},{2,0},{1,3},{3,1},{4,6},{6,4},{5,7},{7,5},{8,10},{10,8},{9,1... | collective-permute-start | bytes 589832 | tf_op jit(solution)/shard_map/ppermute | solution.py:23
  14.4 2.7 %collective-permute-start.9 = (bf16[160,384]{1,0:T(8,128)(2,1)S(1)}, bf16[160,384]{1,0:T(8,128)(2,1)S(1)}, u32[]{:S(2)}, u32[]{:S(2)}) collective-permute-start(bf16[160,384]{1,0:T(8,128)(2,1)S(1)} %collective-permute-done.8.refs_8_), channel_id=1, source_target_pairs={{0,2},{2,0},{1,3},{3,1},{4,6},{6,4},{5,7},{7,5},{8,10},{10,8},{9,1... | collective-permute-start | bytes 368648 | tf_op jit(solution)/shard_map/ppermute | solution.py:23
  16.6 2.7 %collective-permute-start.7 = (bf16[256,384]{1,0:T(8,128)(2,1)S(1)}, bf16[256,384]{1,0:T(8,128)(2,1)S(1)}, u32[]{:S(2)}, u32[]{:S(2)}) collective-permute-start(bf16[256,384]{1,0:T(8,128)(2,1)S(1)} %collective-permute-done.2.refs_2_), channel_id=1, source_target_pairs={{0,2},{2,0},{1,3},{3,1},{4,6},{6,4},{5,7},{7,5},{8,10},{10,8},{9,1... | collective-permute-start | bytes 589832 | tf_op jit(solution)/shard_map/ppermute | solution.py:23
  16.7 1.5 %collective-permute-start.10 = (bf16[128,128]{1,0:T(8,128)(2,1)S(1)}, bf16[128,128]{1,0:T(8,128)(2,1)S(1)}, u32[]{:S(2)}, u32[]{:S(2)}) collective-permute-start(bf16[128,128]{1,0:T(8,128)(2,1)S(1)} %collective-permute-done.3.refs_1_), channel_id=1, source_target_pairs={{0,2},{2,0},{1,3},{3,1},{4,6},{6,4},{5,7},{7,5},{8,10},{10,8},{9,1... | collective-permute-start | bytes 98312 | tf_op jit(solution)/shard_map/ppermute | solution.py:23
  19.3 4.5 %slice-start = ((s8[4718592]{0:T(1024)(128)(4,1)}), s8[4194304]{0:T(1024)(128)(4,1)S(1)}, s32[]{:S(2)}) async-start(s8[4718592]{0:T(1024)(128)(4,1)} %bitcast.9), calls=%async_computation | async-start | bytes 8388608
  19.3 4.5 %slice-start.1 = ((s8[4718592]{0:T(1024)(128)(4,1)}), s8[524288]{0:T(1024)(128)(4,1)S(1)}, s32[]{:S(2)}) async-start(s8[4718592]{0:T(1024)(128)(4,1)} %bitcast.9), calls=%async_computation.1 | async-start | bytes 1048576
  21.3 7.8 %collective-permute-start.12 = (bf16[128,768]{1,0:T(8,128)(2,1)S(1)}, bf16[128,768]{1,0:T(8,128)(2,1)S(1)}, u32[]{:S(2)}, u32[]{:S(2)}) collective-permute-start(bf16[128,768]{1,0:T(8,128)(2,1)S(1)} %get-tuple-element.86.refs_0_), channel_id=1, source_target_pairs={{0,1},{1,0},{2,3},{3,2},{4,5},{5,4},{6,7},{7,6},{8,9},{9,8},{10,11... | collective-permute-start | bytes 589832 | tf_op jit(solution)/shard_map/ppermute | solution.py:23
  23.2 9.3 %collective-permute-start.11 = (bf16[128,768]{1,0:T(8,128)(2,1)S(1)}, bf16[128,768]{1,0:T(8,128)(2,1)S(1)}, u32[]{:S(2)}, u32[]{:S(2)}) collective-permute-start(bf16[128,768]{1,0:T(8,128)(2,1)S(1)} %get-tuple-element.82.refs_0_), channel_id=1, source_target_pairs={{0,1},{1,0},{2,3},{3,2},{4,5},{5,4},{6,7},{7,6},{8,9},{9,8},{10,11... | collective-permute-start | bytes 589832 | tf_op jit(solution)/shard_map/ppermute | solution.py:23
  32.5 0.7 %copy-start = (s32[768]{0:T(1024)S(1)}, s32[768]{0:T(1024)}, u32[]{:S(2)}) copy-start(s32[768]{0:T(1024)} %param.19) | copy-start | bytes 9220
  33.0 1.5 %collective-permute-start.13 = (bf16[128,768]{1,0:T(8,128)(2,1)S(1)}, bf16[128,768]{1,0:T(8,128)(2,1)S(1)}, u32[]{:S(2)}, u32[]{:S(2)}) collective-permute-start(bf16[128,768]{1,0:T(8,128)(2,1)S(1)} %get-tuple-element.92), channel_id=1, source_target_pairs={{0,2},{2,0},{1,3},{3,1},{4,6},{6,4},{5,7},{7,5},{8,10},{10,8},{9,1... | collective-permute-start | bytes 589832 | tf_op jit(solution)/shard_map/ppermute | solution.py:23

commit v10 on v9

--- a/solution.py
+++ b/solution.py
@@ -363,20 +363,26 @@
 
 def first_tracks_kernel(size, *refs):
     shares = refs[:size]
-    inputs, gain, tracks, square, to_send, to_keep = refs[size:]
+    inputs, gain, tracks, second, square, to_send, to_keep, base = refs[size:]
     strand = lax.axis_index("strand")
     width = shares[0].shape[1]
+    base[...] = inputs[:, width:].astype(F32) + second[...].astype(F32)
     square[...], gained = gather_hidden(shares, inputs, gain, 0)
     to_send[...] = matmul(gained, tracks[1 - strand, :width, :])
     to_keep[...] = matmul(gained, tracks[strand, :width, :])
 
 
 def send_kernel(size, *refs):
-    shares = refs[:size]
-    inputs, gain, tracks, square, to_send, sent, gained_out, scale_out = refs[size:]
+    shares = refs[: size - 1]
+    base, gain, tracks, square, to_send, sent, gained_out, scale_out = refs[size - 1 :]
     strand = lax.axis_index("strand")
-    width = shares[0].shape[1]
-    total, gained = gather_hidden(shares, inputs, gain, 1)
+    width = base.shape[1]
+    hidden = base[...]
+    for other in shares:
+        hidden = hidden + other[...].astype(F32)
+    hidden = hidden.astype(BF16).astype(F32)
+    total = jnp.sum(hidden * hidden, axis=1, keepdims=True)
+    gained = (hidden * gain[:, width:]).astype(BF16)
     scale = lax.rsqrt((square[...] + total) / (2 * width) + 1e-06)
     logits = to_send[...] + matmul(gained, tracks[1 - strand, width:, :])
     sent[...] = soft(logits * scale).astype(BF16)
@@ -606,14 +612,15 @@
     twos = [share_two] + [shifted(share_two, "heads", k) for k in range(1, size)]
     weights, _ = lax.optimization_barrier((w_tracks, share_two))
     tracks = lax.optimization_barrier(weights.transpose(1, 0, 2))
-    square, to_send, to_keep = call(
+    square, to_send, to_keep, base = call(
         functools.partial(first_tracks_kernel, size),
         [
             shape((rows, 1), F32),
             shape((rows, tracks_half), F32),
             shape((rows, tracks_half), F32),
+            shape((rows, features // 2), F32),
         ],
-        ones + [inputs, last_gain, tracks],
+        ones + [inputs, last_gain, tracks, share_two],
         "first_tracks",
         flops=2 * rows * features * tracks_half,
     )
@@ -624,7 +631,7 @@
             shape((rows, features // 2), BF16),
             shape((rows, 1), F32),
         ],
-        twos + [inputs, last_gain, tracks, square, to_send],
+        twos[1:] + [base, last_gain, tracks, square, to_send],
         "sent_tracks",
         flops=rows * features * tracks_half,
     )

time: 35.7 us -> 35.6 us (level)
  no operation moved by 1% of the time
where the time goes in v10:
time: 35.6 us; the launch traced here: 35.4 us
  starting transfers between devices  14 us (39%)
  Pallas kernels  11.7 us (33%)
  waiting for transfers between devices  8.81 us (25%)
  local copies, waits for them, and re-layouts  0.75 us (2%)
    ppermute x13, starting transfers between devices, shifted(): lax.ppermute(value, axis, [(i, (i + distance) % size) for i in range(size)])  12.5 us
    pallas_call x11, Pallas kernels, call(): pl.pallas_call(kernel, out_shape=list(outs), in_specs=specs, out_specs=[p...  11.7 us
    ppermute x13, waiting for transfers between devices, shifted(): lax.ppermute(value, axis, [(i, (i + distance) % size) for i in range(size)])  8.81 us
    ppermute x1, starting transfers between devices, body(): raw.append(lax.ppermute(own_codes, ('pos', 'strand'), pairs))  1.58 us
  transfers between devices with their start and end apart: 14, of which 6 were waited for; matrix products, arithmetic and copies ran while one was open for 2% of the time, Pallas kernels for 20%

profile of v10, /device:TPU:0, one launch (start us, length us, event | category | flops | bytes accessed | tf_op | source)
XLA Modules:
  0.0 35.4 jit_solution(8710507490262627954)
XLA Ops:
  0.0 1.1 %stage.1 = (bf16[160,384]{1,0:T(8,128)(2,1)S(1)}, bf16[256,384]{1,0:T(8,128)(2,1)S(1)}, bf16[256,384]{1,0:T(8,128)(2,1)S(1)}, bf16[128,128]{1,0:T(8,128)(2,1)S(1)}) custom-call(bf16[512,768]{1,0:T(8,128)(2,1)} %embed.3, bf16[64,1536]{1,0:T(8,128)(2,1)} %bitcast.13, bf16[96,1536]{1,0:T(8,128)(2,1)} %bitcast.11, s32[128,128]{1,0:T(8,128)} %bitcast.15), custom_call_target="tpu_custom_call" | custom-call | bytes 614400 | tf_op jit(solution)/shard_map/stage/pallas_call | solution.py:44
  1.2 3.0 %collective-permute-start.4 = (bf16[160,384]{1,0:T(8,128)(2,1)S(1)}, bf16[160,384]{1,0:T(8,128)(2,1)S(1)}, u32[]{:S(2)}, u32[]{:S(2)}) collective-permute-start(bf16[160,384]{1,0:T(8,128)(2,1)S(1)} %get-tuple-element.54), channel_id=1, source_target_pairs={{0,1},{1,0},{2,3},{3,2},{4,5},{5,4},{6,7},{7,6},{8,9},{9,8},{10,11... | collective-permute-start | bytes 368648 | tf_op jit(solution)/shard_map/ppermute | solution.py:23
  4.2 0.1 collective-permute-start
  4.2 1.9 %collective-permute-start.2 = (bf16[256,384]{1,0:T(8,128)(2,1)S(1)}, bf16[256,384]{1,0:T(8,128)(2,1)S(1)}, u32[]{:S(2)}, u32[]{:S(2)}) collective-permute-start(bf16[256,384]{1,0:T(8,128)(2,1)S(1)} %get-tuple-element.51), channel_id=1, source_target_pairs={{0,1},{1,0},{2,3},{3,2},{4,5},{5,4},{6,7},{7,6},{8,9},{9,8},{10,11... | collective-permute-start | bytes 589832 | tf_op jit(solution)/shard_map/ppermute | solution.py:23
  6.2 1.9 %prepare.1 = (bf16[512,768]{1,0:T(8,128)(2,1)S(1)}, bf16[64,1536]{1,0:T(8,128)(2,1)S(1)}, bf16[96,1536]{1,0:T(8,128)(2,1)S(1)}, bf16[1536,512]{1,0:T(8,128)(2,1)...) custom-call(bf16[512,768]{1,0:T(8,128)(2,1)} %embed.3, ...), custom_call_target="tpu_custom_call" | custom-call | bytes 3399680 | tf_op jit(solution)/shard_map/prepare/pallas_call | solution.py:44
  8.1 0.2 collective-permute-done.4.refs_6_
  8.3 2.1 %collective-permute-start.8 = (bf16[160,384]{1,0:T(8,128)(2,1)S(1)}, bf16[160,384]{1,0:T(8,128)(2,1)S(1)}, u32[]{:S(2)}, u32[]{:S(2)}) collective-permute-start(bf16[160,384]{1,0:T(8,128)(2,1)S(1)} %collective-permute-done.4.refs_6_), channel_id=1, source_target_pairs={{0,16},{16,0},{1,17},{17,1},{2,18},{18,2},{3,19},{19,3},{4,20},{20... | collective-permute-start | bytes 368648 | tf_op jit(solution)/shard_map/ppermute | solution.py:23
  10.4 1.6 %collective-permute-start.3 = (bf16[128,128]{1,0:T(8,128)(2,1)S(1)}, bf16[128,128]{1,0:T(8,128)(2,1)S(1)}, u32[]{:S(2)}, u32[]{:S(2)}) collective-permute-start(bf16[128,128]{1,0:T(8,128)(2,1)S(1)} %get-tuple-element.57.refs_0_), channel_id=1, source_target_pairs={{0,4},{2,10},{4,8},{6,14},{8,12},{10,2},{12,0},{14,6},{1,5},{3,11}... | collective-permute-start | bytes 98312 | tf_op jit(solution)/shard_map/ppermute | solution.py:511
  12.0 2.2 %collective-permute-start.6 = (bf16[128,128]{1,0:T(8,128)(2,1)S(1)}, bf16[128,128]{1,0:T(8,128)(2,1)S(1)}, u32[]{:S(2)}, u32[]{:S(2)}) collective-permute-start(bf16[128,128]{1,0:T(8,128)(2,1)S(1)} %get-tuple-element.57.refs_0_), channel_id=1, source_target_pairs={{0,12},{4,0},{8,4},{12,8},{1,13},{5,1},{9,5},{13,9},{2,14},{6,2},{... | collective-permute-start | bytes 98312 | tf_op jit(solution)/shard_map/ppermute | solution.py:23
  14.2 0.2 collective-permute-done.8.refs_8_
  14.4 0.4 %collective-permute-start.9 = (bf16[160,384]{1,0:T(8,128)(2,1)S(1)}, bf16[160,384]{1,0:T(8,128)(2,1)S(1)}, u32[]{:S(2)}, u32[]{:S(2)}) collective-permute-start(bf16[160,384]{1,0:T(8,128)(2,1)S(1)} %collective-permute-done.8.refs_8_), channel_id=1, source_target_pairs={{0,2},{2,0},{1,3},{3,1},{4,6},{6,4},{5,7},{7,5},{8,10},{10,8},{9,1... | collective-permute-start | bytes 368648 | tf_op jit(solution)/shard_map/ppermute | solution.py:23
  14.7 1.7 %fetch_out.1.refs_13_.refs_1_ = bf16[768,1536]{1,0:T(8,128)(2,1)S(1)} custom-call(bf16[768,1536]{1,0:T(8,128)(2,1)} %w_out.1), custom_call_target="tpu_custom_call" | custom-call | bytes 2359296 | tf_op jit(solution)/shard_map/fetch_out/pallas_call | solution.py:44
  16.5 0.1 collective-permute-done.6.refs_2_
  16.6 0.1 collective-permute-start.7
  16.7 0.4 %collective-permute-start.10 = (bf16[128,128]{1,0:T(8,128)(2,1)S(1)}, bf16[128,128]{1,0:T(8,128)(2,1)S(1)}, u32[]{:S(2)}, u32[]{:S(2)}) collective-permute-start(bf16[128,128]{1,0:T(8,128)(2,1)S(1)} %collective-permute-done.3.refs_1_), channel_id=1, source_target_pairs={{0,2},{2,0},{1,3},{3,1},{4,6},{6,4},{5,7},{7,5},{8,10},{10,8},{9,1... | collective-permute-start | bytes 98312 | tf_op jit(solution)/shard_map/ppermute | solution.py:23
  17.1 1.1 %own_features.1 = (bf16[384,512]{1,0:T(8,128)(2,1)S(1)}, bf16[320,1536]{1,0:T(8,128)(2,1)S(1)}, bf16[128,768]{1,0:T(8,128)(2,1)S(1)}, f32[384,1]{1,0:T(8,128)S(1...) custom-call(bf16[128,128]{1,0:T(8,128)(2,1)S(1)} %get-tuple-element.57.refs_0_, ...), custom_call_target="tpu_custom_call" | custom-call | flops 490733568 | bytes 6068224 | tf_op jit(solution)/shard_map/own_features/pallas_call | solution.py:44
  18.2 1.1 %other_features.1 = (bf16[512,512]{1,0:T(8,128)(2,1)S(1)}, bf16[128,256]{1,0:T(8,128)(2,1)S(1)}, f32[512,1]{1,0:T(8,128)S(1)}, f32[512,320]{1,0:T(8,128)S(1)}, f32[128,512]{1,0:T(8,128)S(1)}) custom-call(bf16[256,384]{1,0:T(8,128)(2,1)S(1)} %collective-permute-done.refs_0_, bf16[256,384]{1,0:T(8,128)(2,1)S(1)} %collective-permute-done.1.refs_1_, ...), custom_call_target="tpu_custom_call" | custom-call | flops 327155712 | bytes 7182336 | tf_op jit(solution)/shard_map/other_features/pallas_call | solution.py:44
  19.3 0.0 slice-start
  19.3 2.0 %attend.1 = (bf16[128,768]{1,0:T(8,128)(2,1)S(1)}, bf16[128,768]{1,0:T(8,128)(2,1)S(1)}, bf16[128,512]{1,0:T(8,128)(2,1)S(1)}) custom-call(bf16[256,384]{1,0:T(8,128)(2,1)S(1)} %collective-permute-done.refs_0_, bf16[256,384]{1,0:T(8,128)(2,1)S(1)} %collective-permute-done.1.refs_1_, bf16[256,384]{1,0:T(8,128)(2,1)S(1)} %collective-permute-done.2.refs_2_, ...), custom_call_target="tpu_custom_call" | custom-call | flops 528482304 | bytes 10491904 | tf_op jit(solution)/shard_map/attend/pallas_call | solution.py:44
  21.3 1.6 %collective-permute-start.12 = (bf16[128,768]{1,0:T(8,128)(2,1)S(1)}, bf16[128,768]{1,0:T(8,128)(2,1)S(1)}, u32[]{:S(2)}, u32[]{:S(2)}) collective-permute-start(bf16[128,768]{1,0:T(8,128)(2,1)S(1)} %get-tuple-element.84.refs_0_), channel_id=1, source_target_pairs={{0,1},{1,0},{2,3},{3,2},{4,5},{5,4},{6,7},{7,6},{8,9},{9,8},{10,11... | collective-permute-start | bytes 589832 | tf_op jit(solution)/shard_map/ppermute | solution.py:23
  22.9 0.3 second_share.1
  23.2 0.6 %collective-permute-start.11 = (bf16[128,768]{1,0:T(8,128)(2,1)S(1)}, bf16[128,768]{1,0:T(8,128)(2,1)S(1)}, u32[]{:S(2)}, u32[]{:S(2)}) collective-permute-start(bf16[128,768]{1,0:T(8,128)(2,1)S(1)} %get-tuple-element.83.refs_5_), channel_id=1, source_target_pairs={{0,1},{1,0},{2,3},{3,2},{4,5},{5,4},{6,7},{7,6},{8,9},{9,8},{10,11... | collective-permute-start | bytes 589832 | tf_op jit(solution)/shard_map/ppermute | solution.py:23
  23.8 0.6 %copy.13 = bf16[1536,2,768]{2,0,1:T(8,128)(2,1)S(1)} copy(bf16[1536,2,768]{2,1,0:T(2,128)(2,1)S(1)} %bitcast.10) | data formatting | bytes 9437184 | tf_op jit(solution)/shard_map/optimization_barrier | solution.py:613
  24.4 4.7 %collective-permute-done.12.refs_1_ = bf16[128,768]{1,0:T(8,128)(2,1)S(1)} collective-permute-done((bf16[128,768]{1,0:T(8,128)(2,1)S(1)}, bf16[128,768]{1,0:T(8,128)(2,1)S(1)}, u32[]{:S(2)}, u32[]{:S(2)}) %collective-permute-start.12) | collective-permute-done | bytes 196640 | tf_op jit(solution)/shard_map/ppermute | solution.py:23
  29.2 0.5 %first_tracks.1 = (f32[128,1]{1,0:T(8,128)S(1)}, f32[128,768]{1,0:T(8,128)S(1)}, f32[128,768]{1,0:T(8,128)S(1)}, f32[128,768]{1,0:T(8,128)S(1)}) custom-call(bf16[128,768]{1,0:T(8,128)(2,1)S(1)} %get-tuple-element.84.refs_0_, bf16[128,768]{1,0:T(8,128)(2,1)S(1)} %collective-permute-done.12.refs_1_, bf16[128,1536]{1,0:T(8,128)(2,1)S(1)} %get-tuple-element.85.refs_2_, ...), custom_call_target="tpu_custom_call" | custom-call | flops 301989888 | bytes 6952960 | tf_op jit(solution)/shard_map/first_tracks/pallas_call | solution.py:44
  29.7 2.9 %collective-permute-done.11.refs_0_ = bf16[128,768]{1,0:T(8,128)(2,1)S(1)} collective-permute-done((bf16[128,768]{1,0:T(8,128)(2,1)S(1)}, bf16[128,768]{1,0:T(8,128)(2,1)S(1)}, u32[]{:S(2)}, u32[]{:S(2)}) %collective-permute-start.11) | collective-permute-done | bytes 196640 | tf_op jit(solution)/shard_map/ppermute | solution.py:23
  32.5 0.5 %sent_tracks.1 = (bf16[128,768]{1,0:T(8,128)(2,1)S(1)}, bf16[128,768]{1,0:T(8,128)(2,1)S(1)}, f32[128,1]{1,0:T(8,128)S(1)}) custom-call(bf16[128,768]{1,0:T(8,128)(2,1)S(1)} %collective-permute-done.11.refs_0_, f32[128,768]{1,0:T(8,128)S(1)} %get-tuple-element.88.refs_1_, f32[1,1536]{1,0:T(1,128)S(1)} %get-tuple-element.86.refs_3_.refs_2_, ...), custom_call_target="tpu_custom_call" | custom-call | flops 150994944 | bytes 6232064 | tf_op jit(solution)/shard_map/sent_tracks/pallas_call | solution.py:44
  33.0 0.1 collective-permute-start.13
  33.1 0.1 copy-done
  33.2 0.6 %kept_tracks.1.kept = bf16[128,768]{1,0:T(8,128)(2,1)S(1)} custom-call(bf16[128,768]{1,0:T(8,128)(2,1)S(1)} %get-tuple-element.91.gained, bf16[2,1536,768]{2,1,0:T(8,128)(2,1)S(1)} %bitcast.8, f32[128,768]{1,0:T(8,128)S(1)} %get-tuple-element.92.to_keep, f32[128,1]{1,0:T(8,128)S(1)} %get-tuple-element.93.scale, s32[1,768]{1,0:T(1,128)S(1)} %reshape.7.pairs), custom_call_target="tpu_custom_call" | custom-call | flops 150994944 | bytes 5573632 | tf_op jit(solution)/shard_map/kept_tracks/pallas_call | solution.py:44
  33.8 0.7 %collective-permute-done.13.received = bf16[128,768]{1,0:T(8,128)(2,1)S(1)} collective-permute-done((bf16[128,768]{1,0:T(8,128)(2,1)S(1)}, bf16[128,768]{1,0:T(8,128)(2,1)S(1)}, u32[]{:S(2)}, u32[]{:S(2)}) %collective-permute-start.13) | collective-permute-done | bytes 196640 | tf_op jit(solution)/shard_map/ppermute | solution.py:23
  34.5 0.9 %average.1 = f32[128,768]{1,0:T(8,128)} custom-call(bf16[128,768]{1,0:T(8,128)(2,1)S(1)} %kept_tracks.1.kept, bf16[128,768]{1,0:T(8,128)(2,1)S(1)} %collective-permute-done.13.received, s32[1,768]{1,0:T(1,128)S(1)} %reshape.7.pairs), custom_call_target="tpu_custom_call" | custom-call | bytes 1182720 | tf_op jit(solution)/shard_map/average/pallas_call | solution.py:44
  (16 shorter events, 0.0 us)
Async XLA Ops:
  1.2 7.2 %collective-permute-start.4 = (bf16[160,384]{1,0:T(8,128)(2,1)S(1)}, bf16[160,384]{1,0:T(8,128)(2,1)S(1)}, u32[]{:S(2)}, u32[]{:S(2)}) collective-permute-start(bf16[160,384]{1,0:T(8,128)(2,1)S(1)} %get-tuple-element.54), channel_id=1, source_target_pairs={{0,1},{1,0},{2,3},{3,2},{4,5},{5,4},{6,7},{7,6},{8,9},{9,8},{10,11... | collective-permute-start | bytes 368648 | tf_op jit(solution)/shard_map/ppermute | solution.py:23
  4.2 10.1 %collective-permute-start = (bf16[256,384]{1,0:T(8,128)(2,1)S(1)}, bf16[256,384]{1,0:T(8,128)(2,1)S(1)}, u32[]{:S(2)}, u32[]{:S(2)}) collective-permute-start(bf16[256,384]{1,0:T(8,128)(2,1)S(1)} %get-tuple-element.50), channel_id=1, source_target_pairs={{0,1},{1,0},{2,3},{3,2},{4,5},{5,4},{6,7},{7,6},{8,9},{9,8},{10,11... | collective-permute-start | bytes 589832 | tf_op jit(solution)/shard_map/ppermute | solution.py:23
  4.2 12.2 %collective-permute-start.2 = (bf16[256,384]{1,0:T(8,128)(2,1)S(1)}, bf16[256,384]{1,0:T(8,128)(2,1)S(1)}, u32[]{:S(2)}, u32[]{:S(2)}) collective-permute-start(bf16[256,384]{1,0:T(8,128)(2,1)S(1)} %get-tuple-element.51), channel_id=1, source_target_pairs={{0,1},{1,0},{2,3},{3,2},{4,5},{5,4},{6,7},{7,6},{8,9},{9,8},{10,11... | collective-permute-start | bytes 589832 | tf_op jit(solution)/shard_map/ppermute | solution.py:23
  8.3 3.7 %collective-permute-start.5 = (bf16[160,384]{1,0:T(8,128)(2,1)S(1)}, bf16[160,384]{1,0:T(8,128)(2,1)S(1)}, u32[]{:S(2)}, u32[]{:S(2)}) collective-permute-start(bf16[160,384]{1,0:T(8,128)(2,1)S(1)} %collective-permute-done.4.refs_6_), channel_id=1, source_target_pairs={{0,2},{2,0},{1,3},{3,1},{4,6},{6,4},{5,7},{7,5},{8,10},{10,8},{9,1... | collective-permute-start | bytes 368648 | tf_op jit(solution)/shard_map/ppermute | solution.py:23
  8.3 6.1 %collective-permute-start.8 = (bf16[160,384]{1,0:T(8,128)(2,1)S(1)}, bf16[160,384]{1,0:T(8,128)(2,1)S(1)}, u32[]{:S(2)}, u32[]{:S(2)}) collective-permute-start(bf16[160,384]{1,0:T(8,128)(2,1)S(1)} %collective-permute-done.4.refs_6_), channel_id=1, source_target_pairs={{0,16},{16,0},{1,17},{17,1},{2,18},{18,2},{3,19},{19,3},{4,20},{20... | collective-permute-start | bytes 368648 | tf_op jit(solution)/shard_map/ppermute | solution.py:23
  10.4 6.0 %collective-permute-start.3 = (bf16[128,128]{1,0:T(8,128)(2,1)S(1)}, bf16[128,128]{1,0:T(8,128)(2,1)S(1)}, u32[]{:S(2)}, u32[]{:S(2)}) collective-permute-start(bf16[128,128]{1,0:T(8,128)(2,1)S(1)} %get-tuple-element.57.refs_0_), channel_id=1, source_target_pairs={{0,4},{2,10},{4,8},{6,14},{8,12},{10,2},{12,0},{14,6},{1,5},{3,11}... | collective-permute-start | bytes 98312 | tf_op jit(solution)/shard_map/ppermute | solution.py:511
  12.0 4.6 %collective-permute-start.6 = (bf16[128,128]{1,0:T(8,128)(2,1)S(1)}, bf16[128,128]{1,0:T(8,128)(2,1)S(1)}, u32[]{:S(2)}, u32[]{:S(2)}) collective-permute-start(bf16[128,128]{1,0:T(8,128)(2,1)S(1)} %get-tuple-element.57.refs_0_), channel_id=1, source_target_pairs={{0,12},{4,0},{8,4},{12,8},{1,13},{5,1},{9,5},{13,9},{2,14},{6,2},{... | collective-permute-start | bytes 98312 | tf_op jit(solution)/shard_map/ppermute | solution.py:23
  14.2 3.9 %collective-permute-start.1 = (bf16[256,384]{1,0:T(8,128)(2,1)S(1)}, bf16[256,384]{1,0:T(8,128)(2,1)S(1)}, u32[]{:S(2)}, u32[]{:S(2)}) collective-permute-start(bf16[256,384]{1,0:T(8,128)(2,1)S(1)} %collective-permute-done.refs_0_), channel_id=1, source_target_pairs={{0,2},{2,0},{1,3},{3,1},{4,6},{6,4},{5,7},{7,5},{8,10},{10,8},{9,1... | collective-permute-start | bytes 589832 | tf_op jit(solution)/shard_map/ppermute | solution.py:23
  14.4 2.7 %collective-permute-start.9 = (bf16[160,384]{1,0:T(8,128)(2,1)S(1)}, bf16[160,384]{1,0:T(8,128)(2,1)S(1)}, u32[]{:S(2)}, u32[]{:S(2)}) collective-permute-start(bf16[160,384]{1,0:T(8,128)(2,1)S(1)} %collective-permute-done.8.refs_8_), channel_id=1, source_target_pairs={{0,2},{2,0},{1,3},{3,1},{4,6},{6,4},{5,7},{7,5},{8,10},{10,8},{9,1... | collective-permute-start | bytes 368648 | tf_op jit(solution)/shard_map/ppermute | solution.py:23
  16.6 2.7 %collective-permute-start.7 = (bf16[256,384]{1,0:T(8,128)(2,1)S(1)}, bf16[256,384]{1,0:T(8,128)(2,1)S(1)}, u32[]{:S(2)}, u32[]{:S(2)}) collective-permute-start(bf16[256,384]{1,0:T(8,128)(2,1)S(1)} %collective-permute-done.2.refs_2_), channel_id=1, source_target_pairs={{0,2},{2,0},{1,3},{3,1},{4,6},{6,4},{5,7},{7,5},{8,10},{10,8},{9,1... | collective-permute-start | bytes 589832 | tf_op jit(solution)/shard_map/ppermute | solution.py:23
  16.7 1.5 %collective-permute-start.10 = (bf16[128,128]{1,0:T(8,128)(2,1)S(1)}, bf16[128,128]{1,0:T(8,128)(2,1)S(1)}, u32[]{:S(2)}, u32[]{:S(2)}) collective-permute-start(bf16[128,128]{1,0:T(8,128)(2,1)S(1)} %collective-permute-done.3.refs_1_), channel_id=1, source_target_pairs={{0,2},{2,0},{1,3},{3,1},{4,6},{6,4},{5,7},{7,5},{8,10},{10,8},{9,1... | collective-permute-start | bytes 98312 | tf_op jit(solution)/shard_map/ppermute | solution.py:23
  19.3 4.5 %slice-start = ((s8[4718592]{0:T(1024)(128)(4,1)}), s8[4194304]{0:T(1024)(128)(4,1)S(1)}, s32[]{:S(2)}) async-start(s8[4718592]{0:T(1024)(128)(4,1)} %bitcast.9), calls=%async_computation | async-start | bytes 8388608
  19.3 4.5 %slice-start.1 = ((s8[4718592]{0:T(1024)(128)(4,1)}), s8[524288]{0:T(1024)(128)(4,1)S(1)}, s32[]{:S(2)}) async-start(s8[4718592]{0:T(1024)(128)(4,1)} %bitcast.9), calls=%async_computation.1 | async-start | bytes 1048576
  21.3 7.8 %collective-permute-start.12 = (bf16[128,768]{1,0:T(8,128)(2,1)S(1)}, bf16[128,768]{1,0:T(8,128)(2,1)S(1)}, u32[]{:S(2)}, u32[]{:S(2)}) collective-permute-start(bf16[128,768]{1,0:T(8,128)(2,1)S(1)} %get-tuple-element.84.refs_0_), channel_id=1, source_target_pairs={{0,1},{1,0},{2,3},{3,2},{4,5},{5,4},{6,7},{7,6},{8,9},{9,8},{10,11... | collective-permute-start | bytes 589832 | tf_op jit(solution)/shard_map/ppermute | solution.py:23
  23.2 9.3 %collective-permute-start.11 = (bf16[128,768]{1,0:T(8,128)(2,1)S(1)}, bf16[128,768]{1,0:T(8,128)(2,1)S(1)}, u32[]{:S(2)}, u32[]{:S(2)}) collective-permute-start(bf16[128,768]{1,0:T(8,128)(2,1)S(1)} %get-tuple-element.83.refs_5_), channel_id=1, source_target_pairs={{0,1},{1,0},{2,3},{3,2},{4,5},{5,4},{6,7},{7,6},{8,9},{9,8},{10,11... | collective-permute-start | bytes 589832 | tf_op jit(solution)/shard_map/ppermute | solution.py:23
  32.5 0.7 %copy-start = (s32[768]{0:T(1024)S(1)}, s32[768]{0:T(1024)}, u32[]{:S(2)}) copy-start(s32[768]{0:T(1024)} %param.19) | copy-start | bytes 9220
  33.0 1.5 %collective-permute-start.13 = (bf16[128,768]{1,0:T(8,128)(2,1)S(1)}, bf16[128,768]{1,0:T(8,128)(2,1)S(1)}, u32[]{:S(2)}, u32[]{:S(2)}) collective-permute-start(bf16[128,768]{1,0:T(8,128)(2,1)S(1)} %get-tuple-element.94), channel_id=1, source_target_pairs={{0,2},{2,0},{1,3},{3,1},{4,6},{6,4},{5,7},{7,5},{8,10},{10,8},{9,1... | collective-permute-start | bytes 589832 | tf_op jit(solution)/shard_map/ppermute | solution.py:23
